TPU v7x, 32 devices: a whole 2x2x4 slice. The times are simulated.
32 devices in a mesh: gx: 8 (over y, x, core), gy: 4 (over z).
Axes of the slice: x: 2, y: 2, z: 4, core: 2. Of those that a mesh axis runs over, the one named last changes fastest.
Arguments:
- saved_mid: bfloat16 [384, 128, 256], P('gx', 'gy'), may hold values from -6 to 6
- out_grad: bfloat16 [384, 128, 256], P('gx', 'gy'), may hold values from -6 to 6
- expert_weight: bfloat16 [10, 9, 256, 256], replicated, may hold values from -0.125 to 0.125
- routes: int32 [24, 8, 4], P('gx', 'gy'), may hold values from 0 to 7, all different within a row
- gates: float32 [24, 8, 6], P('gx', 'gy'), may hold values from 0.5 to 1.5
- band_matrix: bfloat16 [16, 256, 256], replicated, may hold values from -0.375 to 0.375
- band_ids: int32 [64, 32], replicated, may hold values from 0 to 15
Outputs:
- field_grad: bfloat16 [384, 128, 256], P('gx', 'gy')
Inputs may be any that keep to these rules, and one draw needn't show every extreme that they name: `routes`: each tile names 4 different routed experts.
All inputs are finite; a program needn't handle non-finite values.
Results may differ from a plain program's by a relative error of at most 0.0095.
Values may be sent and summed in bfloat16 or wider, within the bound.
No kernel may reach another device: no remote copies, remote signals or barrier semaphores. Data moves between devices by JAX's collectives and lax.ppermute only.
A program may use at most 128 MiB of HBM per device.

v0:
```python
import math

import jax
import jax.numpy as jnp
from jax import lax
from jax.sharding import PartitionSpec as P

SHARED = 2
TILE = 16
KH = 64
KW = 32


tap_offsets = ((-1, -1), (-1, 0), (-1, 1), (0, -1), (0, 0), (0, 1), (1, -1), (1, 0), (1, 1))


def with_halo(block, sides, width):
    for axis, dim in sides:
        count = lax.axis_size(axis)
        forward = [(i, i + 1) for i in range(count - 1)]
        backward = [(target, source) for source, target in forward]
        low = lax.ppermute(
            lax.slice_in_dim(block, block.shape[dim] - width, None, axis=dim), axis, forward
        )
        high = lax.ppermute(lax.slice_in_dim(block, 0, width, axis=dim), axis, backward)
        block = jnp.concatenate([low, block, high], axis=dim)
    return block


def gelu_slope(values):
    normal_cdf = 0.5 * (1.0 + lax.erf(values * 0.7071067811865476))
    density = jnp.exp(-0.5 * values * values) * 0.3989422804014327
    return normal_cdf + values * density


def angle_table(index, freq, period):
    product = index[:, None] * freq[None, :] % period
    theta = product.astype(jnp.float32) * (2.0 * math.pi / period)
    return (jnp.cos(theta), jnp.sin(theta))


def body(saved_mid, out_grad, expert_weight, routes, gates, band_matrix, band_ids):
    highest = lax.Precision.HIGHEST
    rows_dev, cols_dev, channels = saved_mid.shape
    tiles_down = rows_dev // TILE
    tiles_across = cols_dev // TILE

    def to_tiles(field):
        depth = field.shape[-1]
        field = field.reshape(tiles_down, TILE, tiles_across, TILE, depth).transpose(0, 2, 1, 3, 4)
        return field.reshape(tiles_down * tiles_across, TILE * TILE, depth)

    extended = with_halo(saved_mid, (("gx", 0), ("gy", 1)), 1)
    patches = jnp.concatenate(
        [
            extended[1 + row_off : 1 + row_off + rows_dev, 1 + col_off : 1 + col_off + cols_dev]
            for row_off, col_off in tap_offsets
        ],
        axis=2,
    )
    patch_tiles = to_tiles(patches)
    grad_tiles = to_tiles(out_grad)
    route_rows = routes.reshape(-1, routes.shape[-1])
    gate_rows = gates.reshape(-1, gates.shape[-1])
    flat_weight = expert_weight.reshape(expert_weight.shape[0], 9 * channels, channels)

    def one_tile(pieces):
        tile_patch, tile_grad, route_row, gate_row = pieces
        chosen_ids = jnp.concatenate([jnp.arange(SHARED, dtype=jnp.int32), route_row + SHARED])
        chosen = jnp.take(flat_weight, chosen_ids, axis=0)
        preact = jnp.einsum("pk,sko->spo", tile_patch, chosen, preferred_element_type=jnp.float32)
        deltas = (
            gate_row[:, None, None] * gelu_slope(preact) * tile_grad.astype(jnp.float32)[None]
        ).astype(jnp.bfloat16)
        return jnp.einsum("spo,sko->pk", deltas, chosen, preferred_element_type=jnp.float32).astype(
            jnp.bfloat16
        )

    field = lax.map(one_tile, (patch_tiles, grad_tiles, route_rows, gate_rows))
    depth = field.shape[-1]
    field = field.reshape(tiles_down, tiles_across, TILE, TILE, depth).transpose(0, 2, 1, 3, 4)
    tap_field = field.reshape(rows_dev, cols_dev, depth)
    grad_mid = out_grad.astype(jnp.float32)
    padded = with_halo(tap_field, (("gx", 0), ("gy", 1)), 1)
    for tap_index, (row_off, col_off) in enumerate(tap_offsets):
        shifted = padded[
            1 - row_off : 1 - row_off + rows_dev,
            1 - col_off : 1 - col_off + cols_dev,
            tap_index * channels : (tap_index + 1) * channels,
        ]
        grad_mid = grad_mid + shifted.astype(jnp.float32)
    row_index = lax.axis_index("gx")
    col_index = lax.axis_index("gy")
    full_rows = rows_dev * lax.axis_size("gx")
    full_cols = cols_dev * lax.axis_size("gy")
    row_ids = row_index * rows_dev + jnp.arange(rows_dev, dtype=jnp.int32)
    col_ids = col_index * cols_dev + jnp.arange(cols_dev, dtype=jnp.int32)
    row_modes = jnp.arange(KH, dtype=jnp.int32)
    row_freq = jnp.where(row_modes < KH // 2, row_modes, full_rows - KH + row_modes)
    row_cos, row_sin = angle_table(row_ids, row_freq, full_rows)
    col_cos, col_sin = angle_table(col_ids, jnp.arange(KW, dtype=jnp.int32), full_cols)
    analysis_scale = 1.0 / math.sqrt(full_rows * full_cols)
    half_cos = jnp.einsum("hwc,wn->hnc", grad_mid, col_cos, precision=highest)
    half_sin = jnp.einsum("hwc,wn->hnc", grad_mid, col_sin, precision=highest)
    column_sums = lax.psum_scatter(
        jnp.stack([half_cos, half_sin]).astype(jnp.bfloat16), "gy", scatter_dimension=2, tiled=True
    ).astype(jnp.float32)
    coef_cos = jnp.einsum("hm,hnc->mnc", row_cos, column_sums[0], precision=highest) - jnp.einsum(
        "hm,hnc->mnc", row_sin, column_sums[1], precision=highest
    )
    coef_sin = jnp.einsum("hm,hnc->mnc", row_sin, column_sums[0], precision=highest) + jnp.einsum(
        "hm,hnc->mnc", row_cos, column_sums[1], precision=highest
    )
    owned = lax.psum_scatter(
        (jnp.stack([coef_cos, coef_sin]) * analysis_scale).astype(jnp.bfloat16),
        "gx",
        scatter_dimension=1,
        tiled=True,
    ).astype(jnp.float32)
    rows_owned = owned.shape[1]
    cols_owned = owned.shape[2]
    owned_bands = lax.dynamic_slice(
        band_ids, (row_index * rows_owned, col_index * cols_owned), (rows_owned, cols_owned)
    ).reshape(-1)
    chosen = jnp.take(band_matrix, owned_bands, axis=0)
    mixed_modes = (
        jnp.einsum(
            "rjo,jio->rji",
            owned.reshape(2, rows_owned * cols_owned, channels).astype(jnp.bfloat16),
            chosen,
            preferred_element_type=jnp.float32,
        )
        .astype(jnp.bfloat16)
        .reshape(2, rows_owned, cols_owned, channels)
    )
    spectrum = lax.all_gather(
        lax.all_gather(mixed_modes, "gx", axis=1, tiled=True), "gy", axis=2, tiled=True
    )
    spec_cos = spectrum[0].astype(jnp.float32)
    spec_sin = spectrum[1].astype(jnp.float32)
    z_cos = jnp.einsum("mnc,hm->hnc", spec_cos, row_cos, precision=highest) + jnp.einsum(
        "mnc,hm->hnc", spec_sin, row_sin, precision=highest
    )
    z_sin = jnp.einsum("mnc,hm->hnc", spec_sin, row_cos, precision=highest) - jnp.einsum(
        "mnc,hm->hnc", spec_cos, row_sin, precision=highest
    )
    spectral = jnp.einsum("hnc,wn->hwc", z_cos, col_cos, precision=highest) + jnp.einsum(
        "hnc,wn->hwc", z_sin, col_sin, precision=highest
    )
    spectral = spectral / math.sqrt(2 * KH * KW)
    return (grad_mid + spectral).astype(jnp.bfloat16)


def solution(mesh):
    placed = (
        P("gx", "gy", None),
        P("gx", "gy", None),
        P(),
        P("gx", "gy", None),
        P("gx", "gy", None),
        P(),
        P(),
    )
    return jax.shard_map(
        body, mesh=mesh, in_specs=placed, out_specs=P("gx", "gy", None), check_vma=False
    )
```

profile of v0, /device:TPU:0, one launch (start us, length us, event | category | flops | bytes accessed | tf_op | source)
XLA Modules:
  0.0 382.7 jit_solution(1970371522593051472)
XLA Ops:
  22.5 4.3 %collective-permute-done.3 = bf16[50,1,256]{2,1,0:T(2,128)(2,1)S(1)} collective-permute-done((bf16[50,1,256]{2,1,0:T(2,128)(2,1)S(1)}, bf16[50,1,256]{2,1,0:T(2,128)(2,1)S(1)}, u32[]{:S(2)}, u32[]{:S(2)}) %collective-permute-start.3) | collective-permute-done | bytes 25632 | tf_op jit(solution)/shard_map/ppermute | solution.py:25
  32.5 147.3 %while.10 = (s32[]{:T(128)}, bf16[6,256,2304]{2,1,0:T(8,128)(2,1)}, f32[6,6]{1,0:T(8,128)S(1)}, s32[6,4]{1,0:T(8,128)S(1)}, bf16[10,2304,256]{2,1,0:T(8,128)(2,1...) while((s32[]{:T(128)}, bf16[6,256,2304]{2,1,0:T(8,128)(2,1)}, ...), condition=%wide.region_1.2_spmd, body=%wide.region_0.1_spmd.sunk | while | flops 3635938304 | bytes 31857488 | solution.py:79
  32.6 8.8 %gather_fusion = bf16[6,2304,256]{2,1,0:T(8,128)(2,1)} fusion(bf16[10,2304,256]{2,1,0:T(8,128)(2,1)} %get-tuple-element.157, s32[1024]{0:T(1024)S(1)} %pad_clamp_fusion.3), kind=kCustom, calls=%fused_computation.clone.1 | custom fusion | bytes 14155800 | tf_op jit(solution)/shard_map/while/body/eval_jaxpr/jit(_take)/gather | solution.py:70
  42.5 14.6 %fusion.208 = bf16[6,256,2304]{2,1,0:T(8,128)(2,1)} fusion(bf16[6,256,2304]{2,1,0:T(8,128)(2,1)} %get-tuple-element.146, s32[]{:T(128)} %get-tuple-element.145, bf16[6,2304,256]{2,1,0:T(8,128)(2,1)} %gather_fusion, pred[6]{0:T(512)(128)(4,1)S(1)} %compare_and_fusion.3, bf16[6,256,2304]{2,1,0:T(8,128)(2,1)} %get-tuple-element.158, ...), kind=kOutput, calls=%fused_computation.6.clone.1 | convolution fusion | flops 3635871744 | bytes 16779776 | tf_op jit(solution)/shard_map/while/body/eval_jaxpr/spo,sko->pk/dot_general | solution.py:75
  57.2 8.7 %gather_fusion = bf16[6,2304,256]{2,1,0:T(8,128)(2,1)} fusion(bf16[10,2304,256]{2,1,0:T(8,128)(2,1)} %get-tuple-element.157, s32[1024]{0:T(1024)S(1)} %pad_clamp_fusion.3), kind=kCustom, calls=%fused_computation.clone.1 | custom fusion | bytes 14155800 | tf_op jit(solution)/shard_map/while/body/eval_jaxpr/jit(_take)/gather | solution.py:70
  67.1 14.6 %fusion.208 = bf16[6,256,2304]{2,1,0:T(8,128)(2,1)} fusion(bf16[6,256,2304]{2,1,0:T(8,128)(2,1)} %get-tuple-element.146, s32[]{:T(128)} %get-tuple-element.145, bf16[6,2304,256]{2,1,0:T(8,128)(2,1)} %gather_fusion, pred[6]{0:T(512)(128)(4,1)S(1)} %compare_and_fusion.3, bf16[6,256,2304]{2,1,0:T(8,128)(2,1)} %get-tuple-element.158, ...), kind=kOutput, calls=%fused_computation.6.clone.1 | convolution fusion | flops 3635871744 | bytes 16779776 | tf_op jit(solution)/shard_map/while/body/eval_jaxpr/spo,sko->pk/dot_general | solution.py:75
  81.8 8.7 %gather_fusion = bf16[6,2304,256]{2,1,0:T(8,128)(2,1)} fusion(bf16[10,2304,256]{2,1,0:T(8,128)(2,1)} %get-tuple-element.157, s32[1024]{0:T(1024)S(1)} %pad_clamp_fusion.3), kind=kCustom, calls=%fused_computation.clone.1 | custom fusion | bytes 14155800 | tf_op jit(solution)/shard_map/while/body/eval_jaxpr/jit(_take)/gather | solution.py:70
  91.6 14.5 %fusion.208 = bf16[6,256,2304]{2,1,0:T(8,128)(2,1)} fusion(bf16[6,256,2304]{2,1,0:T(8,128)(2,1)} %get-tuple-element.146, s32[]{:T(128)} %get-tuple-element.145, bf16[6,2304,256]{2,1,0:T(8,128)(2,1)} %gather_fusion, pred[6]{0:T(512)(128)(4,1)S(1)} %compare_and_fusion.3, bf16[6,256,2304]{2,1,0:T(8,128)(2,1)} %get-tuple-element.158, ...), kind=kOutput, calls=%fused_computation.6.clone.1 | convolution fusion | flops 3635871744 | bytes 16779776 | tf_op jit(solution)/shard_map/while/body/eval_jaxpr/spo,sko->pk/dot_general | solution.py:75
  106.3 8.8 %gather_fusion = bf16[6,2304,256]{2,1,0:T(8,128)(2,1)} fusion(bf16[10,2304,256]{2,1,0:T(8,128)(2,1)} %get-tuple-element.157, s32[1024]{0:T(1024)S(1)} %pad_clamp_fusion.3), kind=kCustom, calls=%fused_computation.clone.1 | custom fusion | bytes 14155800 | tf_op jit(solution)/shard_map/while/body/eval_jaxpr/jit(_take)/gather | solution.py:70
  116.2 14.5 %fusion.208 = bf16[6,256,2304]{2,1,0:T(8,128)(2,1)} fusion(bf16[6,256,2304]{2,1,0:T(8,128)(2,1)} %get-tuple-element.146, s32[]{:T(128)} %get-tuple-element.145, bf16[6,2304,256]{2,1,0:T(8,128)(2,1)} %gather_fusion, pred[6]{0:T(512)(128)(4,1)S(1)} %compare_and_fusion.3, bf16[6,256,2304]{2,1,0:T(8,128)(2,1)} %get-tuple-element.158, ...), kind=kOutput, calls=%fused_computation.6.clone.1 | convolution fusion | flops 3635871744 | bytes 16779776 | tf_op jit(solution)/shard_map/while/body/eval_jaxpr/spo,sko->pk/dot_general | solution.py:75
  130.8 8.8 %gather_fusion = bf16[6,2304,256]{2,1,0:T(8,128)(2,1)} fusion(bf16[10,2304,256]{2,1,0:T(8,128)(2,1)} %get-tuple-element.157, s32[1024]{0:T(1024)S(1)} %pad_clamp_fusion.3), kind=kCustom, calls=%fused_computation.clone.1 | custom fusion | bytes 14155800 | tf_op jit(solution)/shard_map/while/body/eval_jaxpr/jit(_take)/gather | solution.py:70
  140.7 14.6 %fusion.208 = bf16[6,256,2304]{2,1,0:T(8,128)(2,1)} fusion(bf16[6,256,2304]{2,1,0:T(8,128)(2,1)} %get-tuple-element.146, s32[]{:T(128)} %get-tuple-element.145, bf16[6,2304,256]{2,1,0:T(8,128)(2,1)} %gather_fusion, pred[6]{0:T(512)(128)(4,1)S(1)} %compare_and_fusion.3, bf16[6,256,2304]{2,1,0:T(8,128)(2,1)} %get-tuple-element.158, ...), kind=kOutput, calls=%fused_computation.6.clone.1 | convolution fusion | flops 3635871744 | bytes 16779776 | tf_op jit(solution)/shard_map/while/body/eval_jaxpr/spo,sko->pk/dot_general | solution.py:75
  155.4 8.8 %gather_fusion = bf16[6,2304,256]{2,1,0:T(8,128)(2,1)} fusion(bf16[10,2304,256]{2,1,0:T(8,128)(2,1)} %get-tuple-element.157, s32[1024]{0:T(1024)S(1)} %pad_clamp_fusion.3), kind=kCustom, calls=%fused_computation.clone.1 | custom fusion | bytes 14155800 | tf_op jit(solution)/shard_map/while/body/eval_jaxpr/jit(_take)/gather | solution.py:70
  165.3 14.5 %fusion.208 = bf16[6,256,2304]{2,1,0:T(8,128)(2,1)} fusion(bf16[6,256,2304]{2,1,0:T(8,128)(2,1)} %get-tuple-element.146, s32[]{:T(128)} %get-tuple-element.145, bf16[6,2304,256]{2,1,0:T(8,128)(2,1)} %gather_fusion, pred[6]{0:T(512)(128)(4,1)S(1)} %compare_and_fusion.3, bf16[6,256,2304]{2,1,0:T(8,128)(2,1)} %get-tuple-element.158, ...), kind=kOutput, calls=%fused_computation.6.clone.1 | convolution fusion | flops 3635871744 | bytes 16779776 | tf_op jit(solution)/shard_map/while/body/eval_jaxpr/spo,sko->pk/dot_general | solution.py:75
  179.8 4.0 %copy.65 = bf16[3,2,16,16,2304]{4,3,1,2,0:T(8,128)(2,1)S(1)} copy(bf16[3,2,16,16,2304]{4,3,2,1,0:T(8,128)(2,1)} %bitcast.174) | data formatting | bytes 14155776 | tf_op jit(solution)/shard_map/reshape | solution.py:81
  194.1 5.3 %collective-permute-start.7 = (bf16[50,1,2304]{2,1,0:T(2,128)(2,1)}, bf16[50,1,2304]{2,1,0:T(2,128)(2,1)}, u32[]{:S(2)}, u32[]{:S(2)}) collective-permute-start(bf16[50,1,2304]{2,1,0:T(2,128)(2,1)} %get-tuple-element.81), channel_id=1, source_target_pairs={{0,1},{1,2},{2,3},{4,5},{5,6},{6,7},{8,9},{9,10},{10,11},{12,13},{... | collective-permute-start | bytes 691208 | tf_op jit(solution)/shard_map/ppermute | solution.py:22
  199.4 6.2 %collective-permute-done.6 = bf16[50,1,2304]{2,1,0:T(2,128)(2,1)} collective-permute-done((bf16[50,1,2304]{2,1,0:T(2,128)(2,1)}, bf16[50,1,2304]{2,1,0:T(2,128)(2,1)}, u32[]{:S(2)}, u32[]{:S(2)}) %collective-permute-start.6) | collective-permute-done | bytes 230432 | tf_op jit(solution)/shard_map/ppermute | solution.py:25
  207.4 6.4 %convert_add_fusion = f32[48,32,256]{2,1,0:T(8,128)S(1)} fusion(bf16[48,32,256]{2,1,0:T(8,128)(2,1)S(1)} %copy-done.5, bf16[50,1,2304]{2,1,0:T(2,128)(2,1)} %collective-permute-done.7, bf16[1,32,2304]{2,1,0:T(8,128)(2,1)S(1)} %collective-permute-done.5, bf16[48,32,2304]{2,1,0:T(8,128)(2,1)} %bitcast.171, bf16[1,32,2304]{2,1,0:T(8,128)(2,1)S(1)} %collective-permute-done.4, ...), kind=kLoop, calls=%fused_computation.60 | loop fusion | flops 26345472 | bytes 11440128 | tf_op jit(solution)/shard_map/add | solution.py:91
  218.6 42.4 %reduce-scatter.7.cloned.1.call-done = bf16[8,24576]{1,0:T(8,128)(2,1)} async-done(((bf16[32,24576]{1,0:T(8,128)(2,1)}), bf16[8,24576]{1,0:T(8,128)(2,1)}) %reduce-scatter.7.cloned.1.call-update) | async-done | bytes 393232
  266.6 5.6 %gather_fusion.1 = bf16[64,256,256]{2,1,0:T(8,128)(2,1)} fusion(bf16[16,256,256]{2,1,0:T(8,128)(2,1)S(1)} %copy-done, s32[1024]{0:T(1024)S(1)} %pad_clamp_fusion.1), kind=kCustom, calls=%fused_computation.1 | custom fusion | bytes 16777472 | tf_op jit(solution)/shard_map/jit(_take)/gather | solution.py:125
  272.2 26.5 %reduce-scatter.9.cloned.1.call-done = bf16[8,4096]{1,0:T(8,128)(2,1)} async-done(((bf16[64,4096]{1,0:T(8,128)(2,1)}), bf16[8,4096]{1,0:T(8,128)(2,1)}) %reduce-scatter.9.cloned.1.call-update) | async-done | bytes 65552
  299.6 5.7 %fusion.56 = bf16[64,256,2]{1,2,0:T(2,128)(2,1)S(1)} fusion(bf16[64,256,256]{2,1,0:T(8,128)(2,1)} %gather_fusion.1, pred[64]{0:T(512)(128)(4,1)S(1)} %compare_and_fusion.1, bf16[2,64,256]{2,1,0:T(8,128)(2,1)S(1)} %copy_bitcast_fusion), kind=kOutput, calls=%fused_computation.75 | convolution fusion | flops 21004288 | bytes 8519744 | tf_op jit(solution)/shard_map/rjo,jio->rji/dot_general | solution.py:127
  305.3 11.0 %all_gather.6 = bf16[2,64,8,256]{3,2,1,0:T(8,128)(2,1)} all-gather(bf16[2,8,8,256]{3,2,1,0:T(8,128)(2,1)S(1)} %copy.74), channel_id=1, replica_groups=mesh['gx'=8,'gy'=4] {'gx'}, dimensions={1}, use_global_device_ids=true | all-gather | bytes 589824 | tf_op jit(solution)/shard_map/all_gather | solution.py:137
  316.3 46.4 %all-gather.2.cloned.1.call-done = bf16[2,64,32,256]{3,2,1,0:T(8,128)(2,1)} async-done(((bf16[2,64,8,256]{3,2,1,0:T(8,128)(2,1)}), bf16[2,64,32,256]{3,2,1,0:T(8,128)(2,1)}) %all-gather.2.cloned.1.call-update) | async-done | bytes 2097168 | tf_op jit(solution)/shard_map/all_gather | solution.py:136
  (146 shorter events, 65.2 us)
Async XLA Ops:
  6.5 260.0 %copy-start = (bf16[16,256,256]{2,1,0:T(8,128)(2,1)S(1)}, bf16[16,256,256]{2,1,0:T(8,128)(2,1)}, u32[]{:S(2)}) copy-start(bf16[16,256,256]{2,1,0:T(8,128)(2,1)} %param.14) | copy-start | bytes 6291460
  6.5 254.5 %reduce-scatter.7.cloned.1.call-start = ((), (), s32[]{:S(2)}) async-start(), calls=%async_computation.3 | async-start | bytes 1966080
  7.4 3.7 collective-permute-start
  9.8 5.2 %collective-permute-start.1 = (bf16[1,32,256]{2,1,0:T(8,128)(2,1)S(1)}, bf16[1,32,256]{2,1,0:T(8,128)(2,1)S(1)}, u32[]{:S(2)}, u32[]{:S(2)}) collective-permute-start(bf16[1,32,256]{2,1,0:T(8,128)(2,1)S(1)} %get-tuple-element.88), channel_id=1, source_target_pairs={{4,0},{8,4},{12,8},{16,12},{20,16},{24,20},{28,24},{5,1},{9,5},{13... | collective-permute-start | bytes 49160 | tf_op jit(solution)/shard_map/ppermute | solution.py:25
  11.1 9.5 %copy-start.6 = (f32[3,2,6]{2,1,0:T(2,128)S(1)}, f32[3,2,6]{2,1,0:T(2,128)}, u32[]{:S(2)}) copy-start(f32[3,2,6]{2,1,0:T(2,128)} %param.13) | copy-start | bytes 436
  11.1 9.5 %copy-start.7 = (s32[3,2,4]{2,1,0:T(2,128)S(1)}, s32[3,2,4]{2,1,0:T(2,128)}, u32[]{:S(2)}) copy-start(s32[3,2,4]{2,1,0:T(2,128)} %param.12) | copy-start | bytes 292
  15.1 7.1 %collective-permute-start.2 = (bf16[50,1,256]{2,1,0:T(2,128)(2,1)S(1)}, bf16[50,1,256]{2,1,0:T(2,128)(2,1)S(1)}, u32[]{:S(2)}, u32[]{:S(2)}) collective-permute-start(bf16[50,1,256]{2,1,0:T(2,128)(2,1)S(1)} %get-tuple-element.87), channel_id=1, source_target_pairs={{0,1},{1,2},{2,3},{4,5},{5,6},{6,7},{8,9},{9,10},{10,11},{12,13},{... | collective-permute-start | bytes 76808 | tf_op jit(solution)/shard_map/ppermute | solution.py:22
  20.7 1.7 copy-start.4
  20.7 6.1 %collective-permute-start.3 = (bf16[50,1,256]{2,1,0:T(2,128)(2,1)S(1)}, bf16[50,1,256]{2,1,0:T(2,128)(2,1)S(1)}, u32[]{:S(2)}, u32[]{:S(2)}) collective-permute-start(bf16[50,1,256]{2,1,0:T(2,128)(2,1)S(1)} %get-tuple-element.86), channel_id=1, source_target_pairs={{1,0},{2,1},{3,2},{5,4},{6,5},{7,6},{9,8},{10,9},{11,10},{13,12},{... | collective-permute-start | bytes 76808 | tf_op jit(solution)/shard_map/ppermute | solution.py:25
  183.8 9.0 %copy-start.1 = (bf16[3,2,16,16,2304]{4,3,1,2,0:T(8,128)(2,1)}, bf16[3,2,16,16,2304]{4,3,1,2,0:T(8,128)(2,1)S(1)}, u32[]{:S(2)}) copy-start(bf16[3,2,16,16,2304]{4,3,1,2,0:T(8,128)(2,1)S(1)} %copy.65) | copy-start | bytes 21233668
  183.8 4.6 %collective-permute-start.4 = (bf16[1,32,2304]{2,1,0:T(8,128)(2,1)S(1)}, bf16[1,32,2304]{2,1,0:T(8,128)(2,1)S(1)}, u32[]{:S(2)}, u32[]{:S(2)}) collective-permute-start(bf16[1,32,2304]{2,1,0:T(8,128)(2,1)S(1)} %get-tuple-element.82), channel_id=1, source_target_pairs={{0,4},{4,8},{8,12},{12,16},{16,20},{20,24},{24,28},{1,5},{5,9},{9,... | collective-permute-start | bytes 442376 | tf_op jit(solution)/shard_map/ppermute | solution.py:22
  187.0 20.5 %copy-start.5 = (bf16[48,32,256]{2,1,0:T(8,128)(2,1)S(1)}, bf16[48,32,256]{2,1,0:T(8,128)(2,1)}, u32[]{:S(2)}) copy-start(bf16[48,32,256]{2,1,0:T(8,128)(2,1)} %param.10) | copy-start | bytes 2359300
  187.0 4.2 %collective-permute-start.5 = (bf16[1,32,2304]{2,1,0:T(8,128)(2,1)S(1)}, bf16[1,32,2304]{2,1,0:T(8,128)(2,1)S(1)}, u32[]{:S(2)}, u32[]{:S(2)}) collective-permute-start(bf16[1,32,2304]{2,1,0:T(8,128)(2,1)S(1)} %get-tuple-element.83), channel_id=1, source_target_pairs={{4,0},{8,4},{12,8},{16,12},{20,16},{24,20},{28,24},{5,1},{9,5},{13... | collective-permute-start | bytes 442376 | tf_op jit(solution)/shard_map/ppermute | solution.py:25
  192.8 12.8 %collective-permute-start.6 = (bf16[50,1,2304]{2,1,0:T(2,128)(2,1)}, bf16[50,1,2304]{2,1,0:T(2,128)(2,1)}, u32[]{:S(2)}, u32[]{:S(2)}) collective-permute-start(bf16[50,1,2304]{2,1,0:T(2,128)(2,1)} %get-tuple-element.80), channel_id=1, source_target_pairs={{1,0},{2,1},{3,2},{5,4},{6,5},{7,6},{9,8},{10,9},{11,10},{13,12},{... | collective-permute-start | bytes 691208 | tf_op jit(solution)/shard_map/ppermute | solution.py:25
  194.1 13.3 %collective-permute-start.7 = (bf16[50,1,2304]{2,1,0:T(2,128)(2,1)}, bf16[50,1,2304]{2,1,0:T(2,128)(2,1)}, u32[]{:S(2)}, u32[]{:S(2)}) collective-permute-start(bf16[50,1,2304]{2,1,0:T(2,128)(2,1)} %get-tuple-element.81), channel_id=1, source_target_pairs={{0,1},{1,2},{2,3},{4,5},{5,6},{6,7},{8,9},{9,10},{10,11},{12,13},{... | collective-permute-start | bytes 691208 | tf_op jit(solution)/shard_map/ppermute | solution.py:22
  213.8 3.3 copy-start.2
  218.5 80.2 %reduce-scatter.9.cloned.1.call-start = ((), (), s32[]{:S(2)}) async-start(), calls=%async_computation.4 | async-start | bytes 589824
  265.5 97.3 %all-gather.2.cloned.1.call-start = ((), (), s32[]{:S(2)}) async-start(), calls=%async_computation.2 | async-start | bytes 2621440 | tf_op jit(solution)/shard_map/all_gather | solution.py:136
  370.3 2.4 copy-start.3
Sparse Core Ops, SparseCore 0:
  218.7 42.3 reduce-scatter.6
  265.6 33.0 reduce-scatter.8
  316.5 46.2 all-gather.1
where the time goes:
time: 384 us; the launch traced here: 383 us
  waiting for transfers between devices  133 us (35%)
  matrix products  110 us (29%)
  local copies, waits for them, and re-layouts  82.9 us (22%)
  starting transfers between devices  19.8 us (5%)
  between operations  13.5 us (4%)
  other arithmetic  11.9 us (3%)
  blocking collectives  11 us (3%)
    dot_general x6, matrix products, one_tile(): jnp.einsum('spo,sko->pk', deltas, chosen, preferred_element_type=jnp.floa...  87.4 us
    unnamed x5, waiting for transfers between devices  69 us
    gather x6, local copies, waits for them, and re-layouts, one_tile(): chosen = jnp.take(flat_weight, chosen_ids, axis=0)  52.4 us
    all_gather x1, waiting for transfers between devices, body(): lax.all_gather(lax.all_gather(mixed_modes, 'gx', axis=1, tiled=True), 'gy...  46.4 us
    ppermute x4, waiting for transfers between devices, with_halo(): lax.ppermute(lax.slice_in_dim(block, 0, width, axis=dim), axis, backward)  16 us
    ppermute x4, starting transfers between devices, with_halo(): lax.ppermute(lax.slice_in_dim(block, block.shape[dim] - width, None, axis...  14.3 us
    all_gather x1, blocking collectives, body(): lax.all_gather(mixed_modes, 'gx', axis=1, tiled=True)  11 us
  transfers between devices with their start and end apart: 11, of which 8 were waited for; matrix products, arithmetic and copies ran while one was open for 3% of the time, Pallas kernels for 0%

commit v1 on v0

v1 whole, which is shorter than its diff:
```python
import functools
import math

import jax
import jax.numpy as jnp
from jax import lax
from jax.experimental import pallas as pl
from jax.experimental.pallas import tpu as pltpu
from jax.sharding import PartitionSpec as P

SHARED = 2
TILE = 16
KH = 64
KW = 32
LANES = 128
F32 = jnp.float32
BF16 = jnp.bfloat16
NT = (((1,), (1,)), ((), ()))
VMEM_LIMIT = 44 << 20


def round_up(value, unit):
    return -(-value // unit) * unit


def layout(mesh_rows, cols_dev):
    slots = KH // 2 // mesh_rows
    reals = 2 * slots
    groups = max(1, 16 // reals)
    width = cols_dev + 2
    fold = -(-width // reals)
    unit = 8 * groups // math.gcd(8, groups)
    virtual = round_up(max(width + fold, reals * fold), unit)
    return slots, reals, groups, width, fold, virtual, virtual // groups


def gelu_slope(values):
    size = jnp.abs(values)
    t = 1.0 / (1.0 + 0.23164189 * size)
    bell = jnp.exp(-0.5 * values * values)
    poly = 0.5307027145 * t - 0.7265760135
    poly = poly * t + 0.7107068705
    poly = poly * t - 0.1422483680
    poly = poly * t + 0.1274147960
    tail = bell * (poly * t - 0.3989422804 * size)
    return jnp.where(values >= 0.0, 1.0 - tail, tail)


def get_rows(ref, start, count, stride=None):
    return jnp.concatenate([ref[h, pl.ds(start, count, stride), :] for h in range(ref.shape[0])], axis=1)


def set_rows(ref, start, values, stride=None):
    for h in range(ref.shape[0]):
        ref[h, pl.ds(start, values.shape[0], stride), :] = values[:, h * LANES : (h + 1) * LANES]


def planes(rows, ch):
    return pltpu.VMEM((ch // LANES, rows, LANES), F32)


def conv_kernel(sizes, routes, gates, valid, x, left, right, top, bottom, grad_out, weight, row_table,
                keep, give, grad, e_left, e_right, e_top, e_bottom,
                shifted, patch, delta, acc, ext, sums, lcol, rcol):
    rows_dev, cols_dev, ch = x.shape
    slots, reals, groups, width, fold, virtual, per = sizes
    chips = keep.shape[0]
    across = cols_dev // TILE
    tiles = (rows_dev // TILE) * across
    area = TILE * TILE
    column = lax.broadcasted_iota(jnp.int32, (cols_dev, ch), 0)

    lcol[...] = left[...].astype(F32) * valid[0]
    rcol[...] = right[...].astype(F32) * valid[1]

    def put_row(at, row, low, high):
        shifted[1, at] = row.astype(BF16)
        shifted[0, at] = jnp.where(column == 0, low, pltpu.roll(row, 1, 0)).astype(BF16)
        shifted[2, at] = jnp.where(column == cols_dev - 1, high, pltpu.roll(row, cols_dev - 1, 0)).astype(BF16)

    def fill(step, carry):
        for sub in range(8):
            at = step * 8 + sub
            put_row(at + 1, x[at].astype(F32), lcol[pl.ds(at, 1), :], rcol[pl.ds(at, 1), :])
        return carry

    lax.fori_loop(0, rows_dev // 8, fill, 0)
    for ref, at, flag in ((top, 0, valid[2]), (bottom, rows_dev + 1, valid[3])):
        edge = ref[...].astype(F32) * flag
        put_row(at, edge[:cols_dev], edge[cols_dev : cols_dev + 1], edge[cols_dev + 1 : cols_dev + 2])

    def clear(at, carry):
        for b in range(3):
            acc[b, at] = jnp.zeros((cols_dev, ch), F32)
        return carry

    lax.fori_loop(0, rows_dev + 2, clear, 0)

    def one_tile(tile, carry):
        row = tile // across * TILE
        col = pl.multiple_of(tile % across * TILE, TILE)
        for a in range(3):
            for b in range(3):
                tap = 3 * a + b
                patch[:, tap * ch : (tap + 1) * ch] = shifted[
                    b, pl.ds(row + a, TILE), pl.ds(col, TILE), :
                ].reshape(area, ch)
        upstream = grad_out[pl.ds(row, TILE), pl.ds(col, TILE), :].reshape(area, ch).astype(F32)
        top_count = routes.shape[1]
        experts = list(range(SHARED)) + [routes[tile, k] + SHARED for k in range(top_count)]
        count = len(experts)
        for first in range(0, count, 2):
            pair = range(first, min(first + 2, count))
            kernel = jnp.concatenate([weight[experts[s]] for s in pair], axis=1)
            preact = jnp.dot(patch[...], kernel, preferred_element_type=F32)
            for place, s in enumerate(pair):
                slope = gelu_slope(preact[:, place * ch : (place + 1) * ch])
                delta[:, s * ch : (s + 1) * ch] = (gates[tile, s] * slope * upstream).astype(BF16)
        for a in range(3):
            total = None
            for s in range(count):
                part = lax.dot_general(
                    delta[:, s * ch : (s + 1) * ch],
                    weight[experts[s], a * 3 * ch : (a + 1) * 3 * ch, :],
                    NT,
                    preferred_element_type=F32,
                )
                total = part if total is None else total + part
            for b in range(3):
                acc[b, pl.ds(row + a, TILE), pl.ds(col, TILE), :] += total[:, b * ch : (b + 1) * ch].reshape(
                    TILE, TILE, ch
                )
        return carry

    lax.fori_loop(0, tiles, one_tile, 0)

    filler = jnp.zeros((virtual - cols_dev, ch), F32)

    def put_ext(at, inner):
        middle = acc[1, at] + inner if inner is not None else acc[1, at]
        total = jnp.concatenate([acc[0, at], filler], axis=0)
        total = total + pltpu.roll(jnp.concatenate([middle, filler], axis=0), 1, 0)
        total = total + pltpu.roll(jnp.concatenate([acc[2, at], filler], axis=0), 2, 0)
        set_rows(ext, pl.multiple_of(at * virtual, 8), total)
        return pltpu.roll(total, virtual - 1, 0)[:cols_dev]

    def join(step, carry):
        for sub in range(4):
            at = step * 4 + sub
            grad[at] = put_ext(at + 1, grad_out[at].astype(F32))
        return carry

    lax.fori_loop(0, rows_dev // 4, join, 0)
    e_top[...] = put_ext(0, None).astype(BF16)
    e_bottom[...] = put_ext(rows_dev + 1, None).astype(BF16)
    for ref, at in ((e_left, 0), (e_right, width - 1)):
        ref[:rows_dev] = get_rows(ext, virtual + at, rows_dev, virtual).astype(BF16)
        ref[rows_dev:] = jnp.concatenate(
            [
                get_rows(ext, at, 1),
                get_rows(ext, (rows_dev + 1) * virtual + at, 1),
                jnp.zeros((ref.shape[0] - rows_dev - 2, ch), F32),
            ],
            axis=0,
        ).astype(BF16)

    depth = row_table.shape[1]
    set_rows(ext, (rows_dev + 2) * virtual, jnp.zeros(((depth - rows_dev - 2) * virtual, ch), F32))
    sums[...] = jnp.zeros(sums.shape, F32)
    later = {}

    def emit(v, found):
        for half, ref in enumerate((keep, give)):
            for c in range(chips):
                begin = (half * chips + c) * reals
                parts = []
                for u in range(v, virtual, per):
                    if u < width:
                        parts.append(found[u][begin : begin + reals])
                    elif u < width + fold:
                        parts.append(get_rows(sums, u - width, reals, fold))
                    else:
                        parts.append(jnp.zeros((reals, ch), F32))
                ref[c, :, v * ch : (v + 1) * ch] = jnp.concatenate(parts, axis=0).astype(BF16)

    for v in range(per):
        wanted = [u for u in range(v, virtual, per) if u < width]
        cells = jnp.concatenate(
            [get_rows(ext, u, depth, virtual).astype(BF16) for u in wanted], axis=1
        )
        freqs = jnp.dot(row_table[...], cells, preferred_element_type=F32)
        found = {u: freqs[:, i * ch : (i + 1) * ch] for i, u in enumerate(wanted)}
        at = 2 * chips * reals
        for u in wanted:
            set_rows(sums, u, found[u][at : at + 1])
        if len(wanted) == groups:
            emit(v, found)
        else:
            later[v] = found
    for v, found in later.items():
        emit(v, found)


def regroup_kernel(sizes, parts, out, rows):
    slots, reals, groups, width, fold, virtual, per = sizes
    ch = out.shape[2]
    set_rows(rows, reals * virtual, jnp.zeros((virtual, ch), F32))
    for v in range(per):
        total = parts[0, :, v * ch : (v + 1) * ch].astype(F32)
        for c in range(1, parts.shape[0]):
            total = total + parts[c, :, v * ch : (v + 1) * ch].astype(F32)
        for i, u in enumerate(range(v, virtual, per)):
            piece = total[i * reals : (i + 1) * reals]
            set_rows(rows, u, piece, virtual)
            if width <= u < width + fold:
                set_rows(rows, reals * virtual + u - width, piece, fold)
    for j in range(slots):
        block = [get_rows(rows, 2 * j * virtual, 2 * virtual), get_rows(rows, reals * virtual, virtual)]
        spare = out.shape[1] - 3 * virtual
        if spare:
            block.append(jnp.zeros((spare, ch), F32))
        out[j] = jnp.concatenate(block, axis=0).astype(BF16)


def modes_kernel(virtual, scale, back_scale, first, parts, col_table, back_table, ids, bands, out):
    sources, slots, _, ch = parts.shape
    cols_dev = out.shape[2] // 3
    for s in range(slots):
        special = first[s] > 0
        cosines, sines, plain = [], [], []
        for z in range(sources):
            block = parts[z, s].astype(F32)
            cosines.append(block[:virtual])
            sines.append(block[virtual : 2 * virtual])
            plain.append(block[2 * virtual : 3 * virtual])
        cosine = jnp.concatenate(cosines, axis=0)
        sine = jnp.concatenate(sines, axis=0)
        low_cos = jnp.where(special, jnp.concatenate(plain, axis=0), cosine)
        low_sin = jnp.where(special, 0.0, sine)
        cells = jnp.concatenate([low_cos, low_sin, cosine, sine], axis=1).astype(BF16)
        freqs = jnp.dot(col_table[...], cells, preferred_element_type=F32)
        over_cos, over_sin = freqs[:KW], freqs[KW:]
        coefs = jnp.concatenate(
            [
                over_cos[:, :ch] - over_sin[:, ch : 2 * ch],
                over_cos[:, 2 * ch : 3 * ch] + over_sin[:, 3 * ch :],
                over_cos[:, ch : 2 * ch] + over_sin[:, :ch],
                over_sin[:, 2 * ch : 3 * ch] - over_cos[:, 3 * ch :],
            ],
            axis=0,
        )
        coefs = (coefs * scale).astype(BF16)
        band = ids[s]
        mixed = None
        for b in range(bands.shape[0]):
            chosen = jnp.where(band == b, coefs, jnp.zeros_like(coefs))
            part = lax.dot_general(chosen, bands[b], NT, preferred_element_type=F32)
            mixed = part if mixed is None else mixed + part
        mixed = (mixed * back_scale).astype(BF16)
        plus_cos, minus_cos = mixed[:KW], mixed[KW : 2 * KW]
        plus_sin, minus_sin = mixed[2 * KW : 3 * KW], mixed[3 * KW :]
        sides = jnp.concatenate(
            [
                jnp.concatenate([plus_cos, plus_sin], axis=0),
                jnp.concatenate([plus_sin, -plus_cos], axis=0),
                jnp.concatenate([minus_cos, minus_sin], axis=0),
                jnp.concatenate([-minus_sin, minus_cos], axis=0),
            ],
            axis=1,
        )
        field = jnp.dot(back_table[...], sides, preferred_element_type=F32)
        plus_p, plus_q = field[:, :ch], field[:, ch : 2 * ch]
        both_p = jnp.where(special, 0.0, plus_p) + field[:, 2 * ch : 3 * ch]
        both_q = jnp.where(special, 0.0, plus_q) + field[:, 3 * ch :]
        alone = jnp.where(special, plus_p, 0.0)
        for z in range(sources):
            span = slice(z * cols_dev, (z + 1) * cols_dev)
            out[z, s] = jnp.concatenate([both_p[span], both_q[span], alone[span]], axis=0).astype(BF16)


def final_kernel(valid, mine, theirs, table, grad, left, right, top, bottom, out, rows, cells, lcol, rcol):
    rows_dev, cols_dev, ch = out.shape
    chips, block = mine.shape[:2]
    main = block - cols_dev
    depth = table.shape[1]
    for half, ref in enumerate((mine, theirs)):
        for c in range(chips):
            begin = (half * chips + c) * main
            set_rows(rows, begin, ref[c, :main].astype(F32))
    used = 2 * chips * main
    set_rows(rows, used, mine[0, main:].astype(F32) + theirs[0, main:].astype(F32))
    set_rows(rows, used + cols_dev, jnp.zeros((rows.shape[1] - used - cols_dev, ch), F32))
    lcol[...] = left[:rows_dev].astype(F32) * valid[0]
    rcol[...] = right[:rows_dev].astype(F32) * valid[1]
    for w in range(0, cols_dev, 2):
        modes = jnp.concatenate(
            [get_rows(rows, w + i, depth, cols_dev).astype(BF16) for i in range(2)], axis=1
        )
        lines = jnp.dot(table[...], modes, preferred_element_type=F32)
        for i in range(2):
            set_rows(cells, w + i, lines[:, i * ch : (i + 1) * ch], cols_dev)
    column = lax.broadcasted_iota(jnp.int32, (cols_dev, ch), 0)

    def total(at):
        line = get_rows(cells, pl.multiple_of(at * cols_dev, 8), cols_dev) + grad[at]
        line = line + jnp.where(column == 0, lcol[pl.ds(at, 1), :], 0.0)
        return line + jnp.where(column == cols_dev - 1, rcol[pl.ds(at, 1), :], 0.0)

    def store(step, carry):
        for sub in range(4):
            at = step * 4 + sub
            out[at] = total(at).astype(BF16)
        return carry

    lax.fori_loop(0, rows_dev // 4, store, 0)
    out[0] = (total(0) + top[...].astype(F32) * valid[2]).astype(BF16)
    last = rows_dev - 1
    out[last] = (total(last) + bottom[...].astype(F32) * valid[3]).astype(BF16)


def in_vmem():
    return pl.BlockSpec(memory_space=pltpu.VMEM)


def in_smem():
    return pl.BlockSpec(memory_space=pltpu.SMEM)


def call(kernel, out_shapes, in_specs, scratch, name):
    many = isinstance(out_shapes, (list, tuple))
    return pl.pallas_call(
        kernel,
        out_shape=out_shapes,
        in_specs=in_specs,
        out_specs=[in_vmem() for _ in out_shapes] if many else in_vmem(),
        scratch_shapes=scratch,
        compiler_params=pltpu.CompilerParams(vmem_limit_bytes=VMEM_LIMIT),
        name=name,
    )


def cos_sin(product, period):
    theta = (product % period).astype(F32) * (2.0 * math.pi / period)
    return jnp.cos(theta), jnp.sin(theta)


def body(saved_mid, out_grad, expert_weight, routes, gates, band_matrix, band_ids):
    rows_dev, cols_dev, ch = saved_mid.shape
    n_gx, n_gy = lax.axis_size("gx"), lax.axis_size("gy")
    gx, gy = lax.axis_index("gx"), lax.axis_index("gy")
    full_rows, full_cols = rows_dev * n_gx, cols_dev * n_gy
    sizes = layout(n_gx, cols_dev)
    slots, reals, groups, width, fold, virtual, per = sizes
    chips = n_gx // 2
    core = gx % 2
    same_core = [list(range(start, n_gx, 2)) for start in range(2)]
    swap = [(i, i ^ 1) for i in range(n_gx)]
    experts = expert_weight.shape[0]

    def ring(array, axis, step):
        count = lax.axis_size(axis)
        return lax.ppermute(array, axis, [(i, (i + step) % count) for i in range(count)])

    def shape(*dims, dtype=BF16):
        return jax.ShapeDtypeStruct(dims, dtype)

    valid = jnp.stack([gy > 0, gy < n_gy - 1, gx > 0, gx < n_gx - 1]).astype(F32)

    chip_ids = jnp.arange(chips, dtype=jnp.int32)
    owners = jnp.concatenate([2 * chip_ids + core, 2 * chip_ids + 1 - core])
    slot_ids = (owners[:, None] * slots + jnp.arange(slots, dtype=jnp.int32)[None, :]).reshape(-1)
    freqs = jnp.where(slot_ids == 0, KH // 2, slot_ids)
    used = 2 * chips * reals
    depth_out = round_up(used + 1, 16)

    def row_angles(rows):
        cosine, sine = cos_sin(rows[:, None] * freqs[None, :], full_rows)
        table = jnp.stack([cosine, sine], axis=2).reshape(rows.shape[0], used)
        ones = jnp.ones((rows.shape[0], 1), F32)
        spare = jnp.zeros((rows.shape[0], depth_out - used - 1), F32)
        return jnp.concatenate([table, ones, spare], axis=1)

    depth_in = round_up(rows_dev + 2, 16)
    ext_rows = gx * rows_dev - 1 + jnp.arange(depth_in, dtype=jnp.int32)
    inside = (ext_rows >= 0) & (ext_rows < full_rows) & (jnp.arange(depth_in) < rows_dev + 2)
    row_table = jnp.where(inside[:, None], row_angles(ext_rows), 0.0).T.astype(BF16)
    back_rows = row_angles(gx * rows_dev + jnp.arange(rows_dev, dtype=jnp.int32)).astype(BF16)

    wide = jnp.arange(virtual, dtype=jnp.int32)[None, :]
    ext_cols = jnp.arange(n_gy, dtype=jnp.int32)[:, None] * cols_dev - 1 + wide
    inside = ((ext_cols >= 0) & (ext_cols < full_cols) & (wide < width)).reshape(-1)
    col_modes = jnp.arange(KW, dtype=jnp.int32)
    cosine, sine = cos_sin(col_modes[:, None] * ext_cols.reshape(-1)[None, :], full_cols)
    col_table = jnp.where(inside[None, :], jnp.concatenate([cosine, sine], axis=0), 0.0).astype(BF16)
    cosine, sine = cos_sin(jnp.arange(full_cols, dtype=jnp.int32)[:, None] * col_modes[None, :], full_cols)
    back_cols = jnp.concatenate([cosine, sine], axis=1).astype(BF16)

    left = ring(saved_mid[:, cols_dev - 1, :], "gy", 1)
    right = ring(saved_mid[:, 0, :], "gy", -1)

    def edge_row(at):
        corners = [
            left[at : at + 1] * valid[0].astype(BF16),
            right[at : at + 1] * valid[1].astype(BF16),
        ]
        return jnp.concatenate([saved_mid[at], *corners], axis=0)

    bottom = ring(edge_row(0), "gx", -1)
    top = ring(edge_row(rows_dev - 1), "gx", 1)

    tiles = (rows_dev // TILE) * (cols_dev // TILE)
    packed = per * ch
    edge_rows = rows_dev + 16
    keep, give, grad, e_left, e_right, e_top, e_bottom = call(
        functools.partial(conv_kernel, sizes),
        [
            shape(chips, groups * reals, packed),
            shape(chips, groups * reals, packed),
            shape(rows_dev, cols_dev, ch, dtype=F32),
            shape(edge_rows, ch),
            shape(edge_rows, ch),
            shape(cols_dev, ch),
            shape(cols_dev, ch),
        ],
        [in_smem()] * 3 + [in_vmem()] * 8,
        [
            pltpu.VMEM((3, rows_dev + 2, cols_dev, ch), BF16),
            pltpu.VMEM((TILE * TILE, 9 * ch), BF16),
            pltpu.VMEM((TILE * TILE, (SHARED + routes.shape[2]) * ch), BF16),
            pltpu.VMEM((3, rows_dev + 2, cols_dev, ch), F32),
            planes(depth_in * virtual, ch),
            planes(round_up(max(width, reals * fold), 8), ch),
            pltpu.VMEM((rows_dev, ch), F32),
            pltpu.VMEM((rows_dev, ch), F32),
        ],
        "conv",
    )(
        routes.reshape(tiles, -1),
        gates.reshape(tiles, -1),
        valid,
        saved_mid,
        left,
        right,
        top,
        bottom,
        out_grad,
        expert_weight.reshape(experts, 9 * ch, ch),
        row_table,
    )

    gift = lax.ppermute(give, "gx", swap)
    summed = (keep.astype(F32) + gift.astype(F32)).astype(BF16)
    parts = lax.all_to_all(summed, "gx", 0, 0, tiled=True, axis_index_groups=same_core)
    slot_rows = round_up(3 * virtual, 16)
    regrouped = call(
        functools.partial(regroup_kernel, sizes),
        shape(slots, slot_rows, ch),
        [in_vmem()],
        [planes((reals + 1) * virtual, ch)],
        "regroup",
    )(parts)

    from_left = ring(e_right, "gy", 1)
    from_right = ring(e_left, "gy", -1)

    def with_corners(edge, at):
        low = from_left[at : at + 1].astype(F32) * valid[0]
        high = from_right[at : at + 1].astype(F32) * valid[1]
        column = jnp.arange(cols_dev)[:, None]
        edge = edge.astype(F32) + jnp.where(column == 0, low, 0.0)
        return (edge + jnp.where(column == cols_dev - 1, high, 0.0)).astype(BF16)

    from_below = ring(with_corners(e_top, rows_dev), "gx", -1)
    from_above = ring(with_corners(e_bottom, rows_dev + 1), "gx", 1)

    split = slots % n_gy == 0
    if split:
        here = slots // n_gy
        cells = lax.all_to_all(regrouped.reshape(n_gy, here, slot_rows, ch), "gy", 0, 0, tiled=True)
        first_slot = gx * slots + gy * here
    else:
        here = slots
        cells = lax.all_gather(regrouped, "gy", axis=0)
        first_slot = gx * slots
    my_slots = first_slot + jnp.arange(here, dtype=jnp.int32)
    special = (my_slots == 0).astype(jnp.int32)
    plus_ids = jnp.take(band_ids, my_slots, axis=0)
    minus_ids = jnp.take(band_ids, jnp.where(my_slots == 0, KH // 2, KH - my_slots), axis=0)
    mode_ids = jnp.concatenate([plus_ids, minus_ids, plus_ids, minus_ids], axis=1)[:, :, None]
    mixed = call(
        functools.partial(
            modes_kernel,
            virtual,
            1.0 / math.sqrt(full_rows * full_cols),
            1.0 / math.sqrt(2 * KH * KW),
        ),
        shape(n_gy, here, 3 * cols_dev, ch),
        [in_smem()] + [in_vmem()] * 5,
        [],
        "modes",
    )(special, cells, col_table, back_cols, mode_ids, band_matrix)
    if split:
        mixed = lax.all_to_all(mixed, "gy", 0, 0, tiled=True).reshape(slots, 3 * cols_dev, ch)
    else:
        mixed = lax.dynamic_index_in_dim(mixed, gy, 0, keepdims=False)
    block = jnp.concatenate(
        [mixed[:, : 2 * cols_dev].reshape(slots * 2 * cols_dev, ch), mixed[0, 2 * cols_dev :]], axis=0
    )
    mine = lax.all_gather(block, "gx", axis=0, axis_index_groups=same_core)
    theirs = lax.ppermute(mine, "gx", swap)
    return call(
        final_kernel,
        shape(rows_dev, cols_dev, ch),
        [in_smem()] + [in_vmem()] * 8,
        [
            planes(depth_out * cols_dev, ch),
            planes(rows_dev * cols_dev, ch),
            pltpu.VMEM((rows_dev, ch), F32),
            pltpu.VMEM((rows_dev, ch), F32),
        ],
        "final",
    )(valid, mine, theirs, back_rows, grad, from_left, from_right, from_above, from_below)


def solution(mesh):
    placed = (
        P("gx", "gy", None),
        P("gx", "gy", None),
        P(),
        P("gx", "gy", None),
        P("gx", "gy", None),
        P(),
        P(),
    )
    return jax.shard_map(
        body, mesh=mesh, in_specs=placed, out_specs=P("gx", "gy", None), check_vma=False
    )
```

time: 384 us -> 120 us (0.31)
  matrix products: 110 us -> 0 us
  waiting for transfers between devices: 133 us -> 23.7 us
  local copies, waits for them, and re-layouts: 82.9 us -> 9.26 us
  Pallas kernels: 0 us -> 44.4 us
  between operations: 13.5 us -> 1.57 us
  other arithmetic: 11.9 us -> 3.75 us
  starting transfers between devices: 19.8 us -> 25.9 us
    dot_general x19 -> x0, matrix products: 110 us -> none  [the longest x6 87.4 us: one_tile(): jnp.einsum('spo,sko->pk', deltas, chosen, preferred_element_type=jnp.floa...]
    unnamed x5 -> x0, waiting for transfers between devices: 69 us -> none
    gather x7 -> x1, local copies, waits for them, and re-layouts: 58 us -> 0.86 us  [body(): plus_ids = jnp.take(band_ids, my_slots, axis=0)]
    all_gather x1 -> x0, waiting for transfers between devices: 46.4 us -> none  [body(): lax.all_gather(lax.all_gather(mixed_modes, 'gx', axis=1, tiled=True), 'gy...]
    pallas_call x0 -> x4, Pallas kernels: none -> 44.4 us  [the longest x1 37.1 us: body(): call(functools.partial(conv_kernel, sizes), [shape(chips, groups * reals,...]
    all_to_all x0 -> x3, waiting for transfers between devices: none -> 18 us  [the longest x1 9.45 us: body(): lax.all_to_all(summed, 'gx', 0, 0, tiled=True, axis_index_groups=same_core)]
    ppermute x8 -> x10, waiting for transfers between devices: 17.7 us -> 5.71 us  [the longest x8 3.79 us: ring(): lax.ppermute(array, axis, [(i, (i + step) % count) for i in range(count)])]
    all_to_all x0 -> x3, starting transfers between devices: none -> 10.5 us  [the longest x1 3.61 us: body(): lax.all_to_all(summed, 'gx', 0, 0, tiled=True, axis_index_groups=same_core)]
  transfers between devices with their start and end apart: 11 -> 13, of which waited for: 8 -> 6; matrix products, arithmetic and copies ran while one was open for 3% -> 6% of each run, Pallas kernels for 0% -> 2%
where the time goes in v1:
time: 120 us; the launch traced here: 119 us
  Pallas kernels  44.4 us (37%)
  starting transfers between devices  25.9 us (22%)
  waiting for transfers between devices  23.7 us (20%)
  blocking collectives  10.3 us (9%)
  local copies, waits for them, and re-layouts  9.26 us (8%)
  other arithmetic  3.75 us (3%)
  between operations  1.57 us (1%)
    pallas_call x1, Pallas kernels, body(): call(functools.partial(conv_kernel, sizes), [shape(chips, groups * reals,...  37.1 us
    ppermute x8, starting transfers between devices, ring(): lax.ppermute(array, axis, [(i, (i + step) % count) for i in range(count)])  15.4 us
    all_gather x1, blocking collectives, body(): mine = lax.all_gather(block, 'gx', axis=0, axis_index_groups=same_core)  10.3 us
    all_to_all x1, waiting for transfers between devices, body(): lax.all_to_all(summed, 'gx', 0, 0, tiled=True, axis_index_groups=same_core)  9.45 us
    all_to_all x1, waiting for transfers between devices, body(): lax.all_to_all(regrouped.reshape(n_gy, here, slot_rows, ch), 'gy', 0, 0,...  6.95 us
    pallas_call x1, Pallas kernels, body(): call(final_kernel, shape(rows_dev, cols_dev, ch), [in_smem()] + [in_vmem(...  4.48 us
    ppermute x8, waiting for transfers between devices, ring(): lax.ppermute(array, axis, [(i, (i + step) % count) for i in range(count)])  3.79 us
    all_to_all x1, starting transfers between devices, body(): lax.all_to_all(summed, 'gx', 0, 0, tiled=True, axis_index_groups=same_core)  3.61 us
  transfers between devices with their start and end apart: 13, of which 6 were waited for; matrix products, arithmetic and copies ran while one was open for 6% of the time, Pallas kernels for 2%

profile of v1, /device:TPU:0, one launch (start us, length us, event | category | flops | bytes accessed | tf_op | source)
XLA Modules:
  0.0 118.8 jit_solution(8239750622723723893)
XLA Ops:
  0.0 1.1 fusion.33
  1.1 3.1 %collective-permute-start = (bf16[48,256]{1,0:T(8,128)(2,1)S(1)}, bf16[48,256]{1,0:T(8,128)(2,1)S(1)}, u32[]{:S(2)}, u32[]{:S(2)}) collective-permute-start(bf16[48,256]{1,0:T(8,128)(2,1)S(1)} %bitcast.49), channel_id=1, source_target_pairs={{0,1},{1,2},{2,3},{3,0},{4,5},{5,6},{6,7},{7,4},{8,9},{9,10},{10,1... | collective-permute-start | bytes 73736 | tf_op jit(solution)/shard_map/ppermute | solution.py:362
  4.2 2.1 %collective-permute-start.1 = (bf16[48,256]{1,0:T(8,128)(2,1)S(1)}, bf16[48,256]{1,0:T(8,128)(2,1)S(1)}, u32[]{:S(2)}, u32[]{:S(2)}) collective-permute-start(bf16[48,256]{1,0:T(8,128)(2,1)S(1)} %bitcast.48), channel_id=1, source_target_pairs={{0,3},{1,0},{2,1},{3,2},{4,7},{5,4},{6,5},{7,6},{8,11},{9,8},{10,9... | collective-permute-start | bytes 73736 | tf_op jit(solution)/shard_map/ppermute | solution.py:362
  10.8 1.7 %collective-permute-start.3 = (bf16[34,256]{1,0:T(8,128)(2,1)S(1)}, bf16[34,256]{1,0:T(8,128)(2,1)S(1)}, u32[]{:S(2)}, u32[]{:S(2)}) collective-permute-start(bf16[34,256]{1,0:T(8,128)(2,1)S(1)} %pad_maximum_fusion.4), channel_id=1, source_target_pairs={{0,28},{4,0},{8,4},{12,8},{16,12},{20,16},{24,20},{28,24},{1,29},{... | collective-permute-start | bytes 52232 | tf_op jit(solution)/shard_map/ppermute | solution.py:362
  14.3 2.3 %collective-permute-done.2.top = bf16[34,256]{1,0:T(8,128)(2,1)S(1)} collective-permute-done((bf16[34,256]{1,0:T(8,128)(2,1)S(1)}, bf16[34,256]{1,0:T(8,128)(2,1)S(1)}, u32[]{:S(2)}, u32[]{:S(2)}) %collective-permute-start.2) | collective-permute-done | bytes 17440 | tf_op jit(solution)/shard_map/ppermute | solution.py:362
  16.6 1.1 copy-done.3
  17.8 1.1 copy-done.4
  18.9 37.1 %conv.1 = (bf16[4,16,5120]{2,1,0:T(8,128)(2,1)S(1)}, bf16[4,16,5120]{2,1,0:T(8,128)(2,1)S(1)}, f32[48,32,256]{2,1,0:T(8,128)S(1)}, bf16[64,256]{1,0:T(8,128)(2,1...) custom-call(s32[6,4]{1,0:T(8,128)S(1)} %reshape.365.routes, ...), custom_call_target="tpu_custom_call" | custom-call | tf_op jit(solution)/shard_map/conv/pallas_call | solution.py:414
  56.1 1.2 copy-done.1
  57.4 1.9 %collective-permute-done.4 = bf16[4,16,5120]{2,1,0:T(8,128)(2,1)S(1)} collective-permute-done((bf16[4,16,5120]{2,1,0:T(8,128)(2,1)S(1)}, bf16[4,16,5120]{2,1,0:T(8,128)(2,1)S(1)}, u32[]{:S(2)}, u32[]{:S(2)}) %collective-permute-start.4) | collective-permute-done | bytes 655392 | tf_op jit(solution)/shard_map/ppermute | solution.py:451
  59.3 1.0 add_convert_fusion
  60.3 3.6 %all-to-all-start = ((bf16[4,16,5120]{2,1,0:T(8,128)(2,1)}), bf16[4,16,5120]{2,1,0:T(8,128)(2,1)S(1)}, u32[]{:S(2)}, u32[]{:S(2)}) async-start(bf16[4,16,5120]{2,1,0:T(8,128)(2,1)} %add_convert_fusion), calls=%async_computation | async-start | bytes 1310720 | tf_op jit(solution)/shard_map/all_to_all | solution.py:453
  64.5 9.4 %all-to-all-done.parts = bf16[4,16,5120]{2,1,0:T(8,128)(2,1)S(1)} async-done(((bf16[4,16,5120]{2,1,0:T(8,128)(2,1)}), bf16[4,16,5120]{2,1,0:T(8,128)(2,1)S(1)}, u32[]{:S(2)}, u32[]{:S(2)}) %all-to-all-start) | async-done | bytes 655392 | tf_op jit(solution)/shard_map/all_to_all | solution.py:453
  74.7 3.4 %all-to-all-start.1 = ((bf16[4,1,128,256]{3,2,1,0:T(8,128)(2,1)}), bf16[4,1,128,256]{3,2,1,0:T(8,128)(2,1)S(1)}, u32[]{:S(2)}, u32[]{:S(2)}) async-start(bf16[4,1,128,256]{3,2,1,0:T(8,128)(2,1)} %bitcast.14), calls=%async_computation.1 | async-start | bytes 524288 | tf_op jit(solution)/shard_map/all_to_all | solution.py:479
  78.4 2.0 %collective-permute-start.6 = (bf16[64,256]{1,0:T(8,128)(2,1)S(1)}, bf16[64,256]{1,0:T(8,128)(2,1)S(1)}, u32[]{:S(2)}, u32[]{:S(2)}) collective-permute-start(bf16[64,256]{1,0:T(8,128)(2,1)S(1)} %get-tuple-element.16), channel_id=1, source_target_pairs={{0,1},{1,2},{2,3},{3,0},{4,5},{5,6},{6,7},{7,4},{8,9},{9,10},{10,1... | collective-permute-start | bytes 98312 | tf_op jit(solution)/shard_map/ppermute | solution.py:362
  80.5 7.0 %all-to-all-done.1.parts = bf16[4,1,128,256]{3,2,1,0:T(8,128)(2,1)S(1)} async-done(((bf16[4,1,128,256]{3,2,1,0:T(8,128)(2,1)}), bf16[4,1,128,256]{3,2,1,0:T(8,128)(2,1)S(1)}, u32[]{:S(2)}, u32[]{:S(2)}) %all-to-all-start.1) | async-done | bytes 262176 | tf_op jit(solution)/shard_map/all_to_all | solution.py:479
  87.4 1.9 %modes.1 = bf16[4,1,96,256]{3,2,1,0:T(8,128)(2,1)} custom-call(s32[1]{0:T(128)S(6)} %convert_element_type.96.first, bf16[4,1,128,256]{3,2,1,0:T(8,128)(2,1)S(1)} %all-to-all-done.1.parts, bf16[64,160]{1,0:T(8,128)(2,1)S(1)} %fusion.col_table, bf16[128,64]{1,0:T(8,128)(2,1)S(1)} %pad_maximum_fusion.2.back_table, s32[1,128,1]{2,1,0:T(8,128)S(1)} %copy.27.ids, ...), custom_call_target="tpu_custom_call" | custom-call | tf_op jit(solution)/shard_map/modes/pallas_call | solution.py:490
  89.4 3.5 %all-to-all-start.2 = ((bf16[4,1,96,256]{3,2,1,0:T(8,128)(2,1)}), bf16[4,1,96,256]{3,2,1,0:T(8,128)(2,1)S(1)}, u32[]{:S(2)}, u32[]{:S(2)}) async-start(bf16[4,1,96,256]{3,2,1,0:T(8,128)(2,1)} %modes.1), calls=%async_computation.2 | async-start | bytes 393216 | tf_op jit(solution)/shard_map/all_to_all | solution.py:503
  93.2 3.8 %collective-permute-start.7 = (bf16[64,256]{1,0:T(8,128)(2,1)S(1)}, bf16[64,256]{1,0:T(8,128)(2,1)S(1)}, u32[]{:S(2)}, u32[]{:S(2)}) collective-permute-start(bf16[64,256]{1,0:T(8,128)(2,1)S(1)} %get-tuple-element.17), channel_id=1, source_target_pairs={{0,3},{1,0},{2,1},{3,2},{4,7},{5,4},{6,5},{7,6},{8,11},{9,8},{10,9... | collective-permute-start | bytes 98312 | tf_op jit(solution)/shard_map/ppermute | solution.py:362
  97.5 1.6 %all-to-all-done.2 = bf16[4,1,96,256]{3,2,1,0:T(8,128)(2,1)S(1)} async-done(((bf16[4,1,96,256]{3,2,1,0:T(8,128)(2,1)}), bf16[4,1,96,256]{3,2,1,0:T(8,128)(2,1)S(1)}, u32[]{:S(2)}, u32[]{:S(2)}) %all-to-all-start.2) | async-done | bytes 196640 | tf_op jit(solution)/shard_map/all_to_all | solution.py:503
  99.1 10.3 %all-gather = bf16[1152,256]{1,0:T(8,128)(2,1)S(1)} all-gather(bf16[288,256]{1,0:T(8,128)(2,1)S(1)} %pad_maximum_fusion), channel_id=2, replica_groups={{0,8,16,24},{4,12,20,28},{1,9,17,25},{5,13,21,29},{2,10,18,26},{6,14,22..., dimensions={0}, use_global_device_ids=true | all-gather | bytes 737280 | tf_op jit(solution)/shard_map/all_gather | solution.py:509
  110.7 2.1 %collective-permute-start.9 = (bf16[32,256]{1,0:T(8,128)(2,1)S(1)}, bf16[32,256]{1,0:T(8,128)(2,1)S(1)}, u32[]{:S(2)}, u32[]{:S(2)}) collective-permute-start(bf16[32,256]{1,0:T(8,128)(2,1)S(1)} %get-tuple-element.47), channel_id=1, source_target_pairs={{0,28},{4,0},{8,4},{12,8},{16,12},{20,16},{24,20},{28,24},{1,29},{... | collective-permute-start | bytes 49160 | tf_op jit(solution)/shard_map/ppermute | solution.py:362
  112.9 1.4 %collective-permute-done.8.top = bf16[32,256]{1,0:T(8,128)(2,1)S(1)} collective-permute-done((bf16[32,256]{1,0:T(8,128)(2,1)S(1)}, bf16[32,256]{1,0:T(8,128)(2,1)S(1)}, u32[]{:S(2)}, u32[]{:S(2)}) %collective-permute-start.8) | collective-permute-done | bytes 16416 | tf_op jit(solution)/shard_map/ppermute | solution.py:362
  114.3 4.5 %final.1 = bf16[48,32,256]{2,1,0:T(8,128)(2,1)} custom-call(f32[4]{0:T(128)S(1)} %add_convert_fusion.3.valid, bf16[4,288,256]{2,1,0:T(8,128)(2,1)S(1)} %bitcast.41, bf16[4,288,256]{2,1,0:T(8,128)(2,1)S(1)} %collective-permute-done.5.theirs, bf16[48,80]{1,0:T(8,128)(2,1)S(1)} %maximum_maximum_fusion.table, f32[48,32,256]{2,1,0:T(8,128)S(1)} %copy-done.2, ...), custom_call_target="tpu_custom_call" | custom-call | tf_op jit(solution)/shard_map/final/pallas_call | solution.py:511
  (79 shorter events, 8.9 us)
Async XLA Ops:
  1.1 9.6 %collective-permute-start = (bf16[48,256]{1,0:T(8,128)(2,1)S(1)}, bf16[48,256]{1,0:T(8,128)(2,1)S(1)}, u32[]{:S(2)}, u32[]{:S(2)}) collective-permute-start(bf16[48,256]{1,0:T(8,128)(2,1)S(1)} %bitcast.49), channel_id=1, source_target_pairs={{0,1},{1,2},{2,3},{3,0},{4,5},{5,6},{6,7},{7,4},{8,9},{9,10},{10,1... | collective-permute-start | bytes 73736 | tf_op jit(solution)/shard_map/ppermute | solution.py:362
  4.2 6.6 %collective-permute-start.1 = (bf16[48,256]{1,0:T(8,128)(2,1)S(1)}, bf16[48,256]{1,0:T(8,128)(2,1)S(1)}, u32[]{:S(2)}, u32[]{:S(2)}) collective-permute-start(bf16[48,256]{1,0:T(8,128)(2,1)S(1)} %bitcast.48), channel_id=1, source_target_pairs={{0,3},{1,0},{2,1},{3,2},{4,7},{5,4},{6,5},{7,6},{8,11},{9,8},{10,9... | collective-permute-start | bytes 73736 | tf_op jit(solution)/shard_map/ppermute | solution.py:362
  10.8 3.5 %collective-permute-start.3 = (bf16[34,256]{1,0:T(8,128)(2,1)S(1)}, bf16[34,256]{1,0:T(8,128)(2,1)S(1)}, u32[]{:S(2)}, u32[]{:S(2)}) collective-permute-start(bf16[34,256]{1,0:T(8,128)(2,1)S(1)} %pad_maximum_fusion.4), channel_id=1, source_target_pairs={{0,28},{4,0},{8,4},{12,8},{16,12},{20,16},{24,20},{28,24},{1,29},{... | collective-permute-start | bytes 52232 | tf_op jit(solution)/shard_map/ppermute | solution.py:362
  12.5 4.2 %collective-permute-start.2 = (bf16[34,256]{1,0:T(8,128)(2,1)S(1)}, bf16[34,256]{1,0:T(8,128)(2,1)S(1)}, u32[]{:S(2)}, u32[]{:S(2)}) collective-permute-start(bf16[34,256]{1,0:T(8,128)(2,1)S(1)} %pad_maximum_fusion.3), channel_id=1, source_target_pairs={{0,4},{4,8},{8,12},{12,16},{16,20},{20,24},{24,28},{28,0},{1,5},{5... | collective-permute-start | bytes 52232 | tf_op jit(solution)/shard_map/ppermute | solution.py:362
  16.6 1.1 copy-start.3
  17.8 1.1 copy-start.4
  56.1 1.2 copy-start.1
  57.2 2.1 %collective-permute-start.4 = (bf16[4,16,5120]{2,1,0:T(8,128)(2,1)S(1)}, bf16[4,16,5120]{2,1,0:T(8,128)(2,1)S(1)}, u32[]{:S(2)}, u32[]{:S(2)}) collective-permute-start(bf16[4,16,5120]{2,1,0:T(8,128)(2,1)S(1)} %get-tuple-element.14), channel_id=1, source_target_pairs={{0,4},{4,0},{8,12},{12,8},{16,20},{20,16},{24,28},{28,24},{1,5},{5... | collective-permute-start | bytes 1966088 | tf_op jit(solution)/shard_map/ppermute | solution.py:451
  60.3 27.1 %copy-start = (bf16[16,256,256]{2,1,0:T(8,128)(2,1)S(1)}, bf16[16,256,256]{2,1,0:T(8,128)(2,1)}, u32[]{:S(2)}) copy-start(bf16[16,256,256]{2,1,0:T(8,128)(2,1)} %bands.1) | copy-start | bytes 6291460
  60.3 13.6 %all-to-all-start = ((bf16[4,16,5120]{2,1,0:T(8,128)(2,1)}), bf16[4,16,5120]{2,1,0:T(8,128)(2,1)S(1)}, u32[]{:S(2)}, u32[]{:S(2)}) async-start(bf16[4,16,5120]{2,1,0:T(8,128)(2,1)} %add_convert_fusion), calls=%async_computation | async-start | bytes 1310720 | tf_op jit(solution)/shard_map/all_to_all | solution.py:453
  74.7 12.7 %all-to-all-start.1 = ((bf16[4,1,128,256]{3,2,1,0:T(8,128)(2,1)}), bf16[4,1,128,256]{3,2,1,0:T(8,128)(2,1)S(1)}, u32[]{:S(2)}, u32[]{:S(2)}) async-start(bf16[4,1,128,256]{3,2,1,0:T(8,128)(2,1)} %bitcast.14), calls=%async_computation.1 | async-start | bytes 524288 | tf_op jit(solution)/shard_map/all_to_all | solution.py:479
  78.4 18.5 %collective-permute-start.6 = (bf16[64,256]{1,0:T(8,128)(2,1)S(1)}, bf16[64,256]{1,0:T(8,128)(2,1)S(1)}, u32[]{:S(2)}, u32[]{:S(2)}) collective-permute-start(bf16[64,256]{1,0:T(8,128)(2,1)S(1)} %get-tuple-element.16), channel_id=1, source_target_pairs={{0,1},{1,2},{2,3},{3,0},{4,5},{5,6},{6,7},{7,4},{8,9},{9,10},{10,1... | collective-permute-start | bytes 98312 | tf_op jit(solution)/shard_map/ppermute | solution.py:362
  89.4 25.0 %copy-start.2 = (f32[48,32,256]{2,1,0:T(8,128)S(1)}, f32[48,32,256]{2,1,0:T(8,128)}, u32[]{:S(2)}) copy-start(f32[48,32,256]{2,1,0:T(8,128)} %copy-done.1) | copy-start | bytes 4718596
  89.4 9.7 %all-to-all-start.2 = ((bf16[4,1,96,256]{3,2,1,0:T(8,128)(2,1)}), bf16[4,1,96,256]{3,2,1,0:T(8,128)(2,1)S(1)}, u32[]{:S(2)}, u32[]{:S(2)}) async-start(bf16[4,1,96,256]{3,2,1,0:T(8,128)(2,1)} %modes.1), calls=%async_computation.2 | async-start | bytes 393216 | tf_op jit(solution)/shard_map/all_to_all | solution.py:503
  93.2 16.2 %collective-permute-start.7 = (bf16[64,256]{1,0:T(8,128)(2,1)S(1)}, bf16[64,256]{1,0:T(8,128)(2,1)S(1)}, u32[]{:S(2)}, u32[]{:S(2)}) collective-permute-start(bf16[64,256]{1,0:T(8,128)(2,1)S(1)} %get-tuple-element.17), channel_id=1, source_target_pairs={{0,3},{1,0},{2,1},{3,2},{4,7},{5,4},{6,5},{7,6},{8,11},{9,8},{10,9... | collective-permute-start | bytes 98312 | tf_op jit(solution)/shard_map/ppermute | solution.py:362
  109.4 4.9 %collective-permute-start.5 = (bf16[4,288,256]{2,1,0:T(8,128)(2,1)S(1)}, bf16[4,288,256]{2,1,0:T(8,128)(2,1)S(1)}, u32[]{:S(2)}, u32[]{:S(2)}) collective-permute-start(bf16[4,288,256]{2,1,0:T(8,128)(2,1)S(1)} %bitcast.40), channel_id=1, source_target_pairs={{0,4},{4,0},{8,12},{12,8},{16,20},{20,16},{24,28},{28,24},{1,5},{5... | collective-permute-start | bytes 1769480 | tf_op jit(solution)/shard_map/ppermute | solution.py:510
  110.2 4.1 %collective-permute-start.8 = (bf16[32,256]{1,0:T(8,128)(2,1)S(1)}, bf16[32,256]{1,0:T(8,128)(2,1)S(1)}, u32[]{:S(2)}, u32[]{:S(2)}) collective-permute-start(bf16[32,256]{1,0:T(8,128)(2,1)S(1)} %get-tuple-element.48), channel_id=1, source_target_pairs={{0,4},{4,8},{8,12},{12,16},{16,20},{20,24},{24,28},{28,0},{1,5},{5... | collective-permute-start | bytes 49160 | tf_op jit(solution)/shard_map/ppermute | solution.py:362
  110.7 3.6 %collective-permute-start.9 = (bf16[32,256]{1,0:T(8,128)(2,1)S(1)}, bf16[32,256]{1,0:T(8,128)(2,1)S(1)}, u32[]{:S(2)}, u32[]{:S(2)}) collective-permute-start(bf16[32,256]{1,0:T(8,128)(2,1)S(1)} %get-tuple-element.47), channel_id=1, source_target_pairs={{0,28},{4,0},{8,4},{12,8},{16,12},{20,16},{24,20},{28,24},{1,29},{... | collective-permute-start | bytes 49160 | tf_op jit(solution)/shard_map/ppermute | solution.py:362

commit v2 on v1

v2 whole, which is shorter than its diff:
```python
import functools
import math

import jax
import jax.numpy as jnp
import numpy as np
from jax import lax
from jax.experimental import pallas as pl
from jax.experimental.pallas import tpu as pltpu
from jax.sharding import PartitionSpec as P

SHARED = 2
TILE = 16
KH = 64
KW = 32
LANES = 128
F32 = jnp.float32
BF16 = jnp.bfloat16
NT = (((1,), (1,)), ((), ()))


def round_up(value, unit):
    return -(-value // unit) * unit


def layout(mesh_rows, cols_dev):
    slots = KH // 2 // mesh_rows
    reals = 2 * slots
    groups = max(1, 16 // reals)
    width = cols_dev + 2
    fold = -(-width // reals)
    unit = 8 * groups // math.gcd(8, groups)
    virtual = round_up(max(width + fold, reals * fold), unit)
    return slots, reals, groups, width, fold, virtual, virtual // groups


def gelu_slope(values):
    size = jnp.abs(values)
    t = 1.0 / (1.0 + 0.23164189 * size)
    bell = jnp.exp(-0.5 * values * values)
    poly = 0.5307027145 * t - 0.7265760135
    poly = poly * t + 0.7107068705
    poly = poly * t - 0.1422483680
    poly = poly * t + 0.1274147960
    tail = bell * (poly * t - 0.3989422804 * size)
    return jnp.where(values >= 0.0, 1.0 - tail, tail)


def get_rows(ref, start, count, stride=None):
    return jnp.concatenate([ref[h, pl.ds(start, count, stride), :] for h in range(ref.shape[0])], axis=1)


def set_rows(ref, start, values, stride=None):
    for h in range(ref.shape[0]):
        ref[h, pl.ds(start, values.shape[0], stride), :] = values[:, h * LANES : (h + 1) * LANES]


def planes(rows, ch):
    return pltpu.VMEM((ch // LANES, rows, LANES), F32)


def conv_kernel(sizes, picked, edges, span, routes, gates, place_ref, x_far, left, right, top, bottom, grad_out_far, weight_far, tables,
                keep, give, grad_far, e_left, e_right,
                x, grad_out, weight, grad, shifted, patch, delta_a, delta_b, acc, ext, sums, lcol, rcol,
                weight_sems, field_sems):
    rows_dev, cols_dev, ch = x.shape
    experts = weight.shape[0]
    field_copies = [
        pltpu.make_async_copy(x_far, x, field_sems.at[0]),
        pltpu.make_async_copy(grad_out_far, grad_out, field_sems.at[1]),
        pltpu.make_async_copy(grad, grad_far, field_sems.at[2]),
    ]

    def fetch(e):
        return pltpu.make_async_copy(weight_far.at[e], weight.at[e], weight_sems.at[e])

    def in_first(e):
        found = routes[0] == e - SHARED
        for k in range(1, picked):
            found = found | (routes[k] == e - SHARED)
        return found

    count = SHARED + picked
    early = list(range(SHARED)) + [routes[k] + SHARED for k in range(picked)]
    field_copies[0].start()
    for e in early[:2]:
        fetch(e).start()
    field_copies[1].start()

    slots, reals, groups, width, fold, virtual, per = sizes
    chips = keep.shape[0]
    across = cols_dev // TILE
    tiles = (rows_dev // TILE) * across
    area = TILE * TILE
    column = lax.broadcasted_iota(jnp.int32, (cols_dev, ch), 0)

    valid = neighbours(place_ref, edges)
    lcol[...] = left[...].astype(F32) * valid[0]
    rcol[...] = right[...].astype(F32) * valid[1]
    field_copies[0].wait()
    for e in early[2:4]:
        fetch(e).start()

    def put_row(at, row, low, high):
        shifted[1, at] = row.astype(BF16)
        shifted[0, at] = jnp.where(column == 0, low, pltpu.roll(row, 1, 0)).astype(BF16)
        shifted[2, at] = jnp.where(column == cols_dev - 1, high, pltpu.roll(row, cols_dev - 1, 0)).astype(BF16)

    def fill(step, carry):
        for sub in range(8):
            at = step * 8 + sub
            put_row(at + 1, x[at].astype(F32), lcol[pl.ds(at, 1), :], rcol[pl.ds(at, 1), :])
        return carry

    lax.fori_loop(0, rows_dev // 8, fill, 0)
    for ref, at, flag in ((top, 0, valid[2]), (bottom, rows_dev + 1, valid[3])):
        edge = ref[...].astype(F32) * flag
        low = edge[cols_dev : cols_dev + 1] * valid[0]
        high = edge[cols_dev + 1 : cols_dev + 2] * valid[1]
        put_row(at, edge[:cols_dev], low, high)

    def clear(at, carry):
        for b in range(3):
            acc[b, at] = jnp.zeros((cols_dev, ch), F32)
        return carry

    lax.fori_loop(0, rows_dev + 2, clear, 0)

    firsts = range(0, count, 2)

    def place(tile):
        return tile // across * TILE, pl.multiple_of(tile % across * TILE, TILE)

    def expert(tile, s):
        return s if s < SHARED else routes[tile * picked + s - SHARED] + SHARED

    def gather(tile):
        row, col = place(tile)
        for a in range(3):
            for b in range(3):
                tap = 3 * a + b
                patch[:, tap * ch : (tap + 1) * ch] = shifted[
                    b, pl.ds(row + a, TILE), pl.ds(col, TILE), :
                ].reshape(area, ch)

    def forward(tile, first):
        pair = range(first, min(first + 2, count))
        kernel = jnp.concatenate([weight[expert(tile, s)] for s in pair], axis=1)
        return jnp.dot(patch[...], kernel, preferred_element_type=F32)

    def slopes(tile, first, preact, delta):
        row, col = place(tile)
        upstream = grad_out[pl.ds(row, TILE), pl.ds(col, TILE), :].reshape(area, ch).astype(F32)
        for i, s in enumerate(range(first, min(first + 2, count))):
            slope = gelu_slope(preact[:, i * ch : (i + 1) * ch])
            delta[:, s * ch : (s + 1) * ch] = (gates[tile * count + s] * slope * upstream).astype(BF16)

    def backward(tile, a, delta):
        row, col = place(tile)
        total = None
        for s in range(count):
            part = lax.dot_general(
                delta[:, s * ch : (s + 1) * ch],
                weight[expert(tile, s), a * 3 * ch : (a + 1) * 3 * ch, :],
                NT,
                preferred_element_type=F32,
            )
            total = part if total is None else total + part
        for b in range(3):
            acc[b, pl.ds(row + a, TILE), pl.ds(col, TILE), :] += total[:, b * ch : (b + 1) * ch].reshape(
                TILE, TILE, ch
            )

    def step(tile, source, target):
        gather(tile + 1)
        for i, first in enumerate(firsts):
            preact = forward(tile + 1, first)
            for a in range(i, 3 if first == firsts[-1] else i + 1):
                backward(tile, a, source)
            slopes(tile + 1, first, preact, target)

    gather(0)
    for first in firsts:
        for e in early[first : first + 2]:
            fetch(e).wait()
        for e in early[first + 4 : first + 6]:
            fetch(e).start()
        if first == firsts[-1]:
            for e in range(SHARED, experts):

                @pl.when(jnp.logical_not(in_first(e)))
                def _():
                    fetch(e).start()

        preact = forward(0, first)
        if first == 0:
            field_copies[1].wait()
        slopes(0, first, preact, delta_a)
    for e in range(SHARED, experts):

        @pl.when(jnp.logical_not(in_first(e)))
        def _():
            fetch(e).wait()

    pairs = (tiles - 1) // 2

    def two(i, carry):
        step(2 * i, delta_a, delta_b)
        step(2 * i + 1, delta_b, delta_a)
        return carry

    lax.fori_loop(0, pairs, two, 0)
    last, source = 2 * pairs, delta_a
    if last < tiles - 1:
        step(last, delta_a, delta_b)
        last, source = last + 1, delta_b
    for a in range(3):
        backward(last, a, source)

    filler = jnp.zeros((virtual - cols_dev, ch), F32)

    def put_ext(at, inner):
        middle = acc[1, at] + inner if inner is not None else acc[1, at]
        total = jnp.concatenate([acc[0, at], filler], axis=0)
        total = total + pltpu.roll(jnp.concatenate([middle, filler], axis=0), 1, 0)
        total = total + pltpu.roll(jnp.concatenate([acc[2, at], filler], axis=0), 2, 0)
        set_rows(ext, pl.multiple_of(at * virtual, 8), total)
        return pltpu.roll(total, virtual - 1, 0)[:cols_dev]

    def join(step, carry):
        for sub in range(4):
            at = step * 4 + sub
            grad[at] = put_ext(at + 1, grad_out[at].astype(F32))
        return carry

    lax.fori_loop(0, rows_dev // 4, join, 0)
    field_copies[2].start()
    blocks = []
    for at in (0, rows_dev + 1):
        line = put_ext(at, None)
        corners = [get_rows(ext, at * virtual, 1), get_rows(ext, at * virtual + width - 1, 1)]
        line = jnp.concatenate([line, *corners, jnp.zeros((TILE - 2, ch), F32)], axis=0).astype(BF16)
        blocks += [line[i : i + TILE] for i in range(0, line.shape[0], TILE)]
    for i, block in enumerate(blocks):
        begin = (per + i // chips) * ch
        give[i % chips, :, begin : begin + ch] = block
    for ref, at in ((e_left, 0), (e_right, width - 1)):
        ref[...] = get_rows(ext, virtual + at, rows_dev, virtual).astype(BF16)

    row_table = tables[span]
    depth = row_table.shape[1]
    set_rows(ext, (rows_dev + 2) * virtual, jnp.zeros(((depth - rows_dev - 2) * virtual, ch), F32))
    sums[...] = jnp.zeros(sums.shape, F32)
    later = {}

    def emit(v, found):
        for half, ref in enumerate((keep, give)):
            for c in range(chips):
                begin = (half * chips + c) * reals
                parts = []
                for u in range(v, virtual, per):
                    if u < width:
                        parts.append(found[u][begin : begin + reals])
                    elif u < width + fold:
                        parts.append(get_rows(sums, u - width, reals, fold))
                    else:
                        parts.append(jnp.zeros((reals, ch), F32))
                ref[c, :, v * ch : (v + 1) * ch] = jnp.concatenate(parts, axis=0).astype(BF16)

    for v in range(per):
        wanted = [u for u in range(v, virtual, per) if u < width]
        cells = jnp.concatenate(
            [get_rows(ext, u, depth, virtual).astype(BF16) for u in wanted], axis=1
        )
        freqs = jnp.dot(row_table, cells, preferred_element_type=F32)
        found = {u: freqs[:, i * ch : (i + 1) * ch] for i, u in enumerate(wanted)}
        at = 2 * chips * reals
        for u in wanted:
            set_rows(sums, u, found[u][at : at + 1])
        if len(wanted) == groups:
            emit(v, found)
        else:
            later[v] = found
    for v, found in later.items():
        emit(v, found)
    field_copies[2].wait()


def neighbours(place, edges):
    gx, gy = place[0], place[1]
    found = (gy > 0, gy < edges[1] - 1, gx > 0, gx < edges[0] - 1)
    return [jnp.where(flag, 1.0, 0.0) for flag in found]


def edge_blocks(cols_dev):
    return cols_dev // TILE + 1


def find_edge(gift, chips, per, ch, blocks, which):
    parts = []
    for i in range(which * blocks, (which + 1) * blocks):
        begin = (per + i // chips) * ch
        parts.append(gift[i % chips, :, begin : begin + ch])
    return jnp.concatenate(parts, axis=1)


def regroup_kernel(sizes, chips, here, edges, span, place, gift, e_left, e_right, tables, *refs):
    slots, reals, groups, width, fold, virtual, per = sizes
    parts, (above, below, *outs, rows) = refs[:chips], refs[chips:]
    cols_dev, ch = above.shape
    rows_dev = e_left.shape[0]
    blocks = edge_blocks(cols_dev)
    set_rows(rows, reals * virtual, jnp.zeros((virtual, ch), F32))
    for v in range(per):
        total = None
        for part in parts:
            piece = part[:, v * ch : (v + 1) * ch].astype(F32)
            total = piece if total is None else total + piece
        for i, u in enumerate(range(v, virtual, per)):
            piece = total[i * reals : (i + 1) * reals]
            set_rows(rows, u, piece, virtual)
            if width <= u < width + fold:
                set_rows(rows, reals * virtual + u - width, piece, fold)
    plain = get_rows(rows, reals * virtual, virtual).astype(BF16)
    low = jnp.dot(tables[span], plain, preferred_element_type=F32)
    share = low.shape[0] // 4
    for real in range(reals):
        part = real % 2 * share
        set_rows(rows, real * virtual + width, low[part : part + share])

    valid = neighbours(place, edges)
    first_core = place[0] % 2 == 0

    def line(far, near, flag):
        flat = jnp.where(first_core, far.astype(F32), near.astype(F32)) * flag
        return [flat[:, i * ch : (i + 1) * ch] for i in range(blocks)]

    far_bottom = parts[1][:, per * ch : (per + blocks) * ch]
    far_top = parts[chips - 1][:, per * ch : (per + blocks) * ch]
    from_above = line(far_bottom, find_edge(gift, chips, per, ch, blocks, 1), valid[2])
    from_below = line(find_edge(gift, chips, per, ch, blocks, 0), far_top, valid[3])
    above[...] = jnp.concatenate(from_above[:-1], axis=0).astype(BF16)
    below[...] = jnp.concatenate(from_below[:-1], axis=0).astype(BF16)
    row = lax.broadcasted_iota(jnp.int32, (rows_dev, ch), 0)
    sides = []
    for ref, at in ((e_right, 1), (e_left, 0)):
        side = ref[...].astype(F32)
        side = side + jnp.where(row == 0, from_above[-1][at : at + 1], 0.0)
        sides.append(side + jnp.where(row == rows_dev - 1, from_below[-1][at : at + 1], 0.0))

    for place in range(slots // here):
        block = [get_rows(rows, 2 * place * here * virtual, 2 * here * virtual)]
        if outs[place].shape[0] > block[0].shape[0]:
            block.append(sides[0] if place == 1 else sides[1])
        outs[place][...] = jnp.concatenate(block, axis=0).astype(BF16)
    if here == slots:
        for ref, side in zip(outs[1:], sides):
            ref[...] = side.astype(BF16)


def modes_kernel(sizes, split, scale, back_scale, sources, place, col_table, back_table, ids, bands, *refs):
    slots, reals, groups, width, fold, virtual, per = sizes
    parts, (low_out, *outs) = refs[:sources], refs[sources:]
    ch = low_out.shape[1]
    share = low_out.shape[0] // 4
    here = parts[0].shape[0] // (2 * virtual)
    cols_dev = outs[0].shape[0] // (2 * here)
    first = place[0] * slots + (place[1] * here if split else 0)

    def bands_of(row, rows, begin):
        line = jnp.broadcast_to(ids[pl.ds(row, 1), :], (rows, KW))
        wanted = lax.broadcasted_iota(jnp.int32, (rows, KW), 0) % KW + begin
        at = lax.broadcasted_iota(jnp.int32, (rows, KW), 1)
        return jnp.sum(jnp.where(wanted == at, line, 0).astype(F32), axis=1, keepdims=True)

    low_line = bands_of(0, share, place[0] * share)
    for s in range(here):
        blocks = [part[2 * s * virtual : 2 * (s + 1) * virtual].astype(F32) for part in parts]
        cosine = jnp.concatenate([block[:virtual] for block in blocks], axis=0)
        sine = jnp.concatenate([block[virtual:] for block in blocks], axis=0)
        cells = jnp.concatenate([cosine, sine], axis=1).astype(BF16)
        freqs = jnp.dot(col_table[...], cells, preferred_element_type=F32)
        over_cos, over_sin = freqs[:KW], freqs[KW:]
        slot = first + s
        plus = jnp.where(slot == 0, 0.0, scale)
        low = sum(blocks)
        coefs = jnp.concatenate(
            [
                (over_cos[:, :ch] - over_sin[:, ch:]) * plus,
                (over_cos[:, :ch] + over_sin[:, ch:]) * scale,
                (over_cos[:, ch:] + over_sin[:, :ch]) * plus,
                (over_sin[:, :ch] - over_cos[:, ch:]) * scale,
                low[width : width + share] * scale,
                low[virtual + width : virtual + width + share] * scale,
                jnp.zeros((2 * share, ch), F32),
            ],
            axis=0,
        ).astype(BF16)
        plus_line = bands_of(slot, KW, 0)
        minus_line = bands_of(jnp.where(slot == 0, KH // 2, KH - slot), KW, 0)
        band = jnp.concatenate([plus_line, minus_line, plus_line, minus_line] + [low_line] * 4, axis=0)
        mixed = None
        for b in range(bands.shape[0]):
            chosen = jnp.where(band == float(b), coefs, jnp.zeros_like(coefs))
            part = lax.dot_general(chosen, bands[b], NT, preferred_element_type=F32)
            mixed = part if mixed is None else mixed + part
        mixed = (mixed * back_scale).astype(BF16)
        if s == 0:
            low_out[...] = mixed[4 * KW :]
        plus_cos, minus_cos = mixed[:KW], mixed[KW : 2 * KW]
        plus_sin, minus_sin = mixed[2 * KW : 3 * KW], mixed[3 * KW : 4 * KW]
        sides = jnp.concatenate(
            [
                jnp.concatenate([plus_cos, plus_sin, minus_cos, minus_sin], axis=0),
                jnp.concatenate([plus_sin, -plus_cos, -minus_sin, minus_cos], axis=0),
            ],
            axis=1,
        )
        field = jnp.dot(back_table[...], sides, preferred_element_type=F32).astype(BF16)
        for z, out in enumerate(outs):
            span = slice(z * cols_dev, (z + 1) * cols_dev)
            begin = 2 * s * cols_dev
            out[begin : begin + cols_dev] = field[span, :ch]
            out[begin + cols_dev : begin + 2 * cols_dev] = field[span, ch:]


def final_kernel(count, main, edges, spans, place, tables, grad_far, left, right, above, below, *refs):
    blocks, (out, grad, rows, cells, lcol, rcol, sem) = refs[:count], refs[count:]
    rows_dev, cols_dev, ch = out.shape
    table, low_table = tables[spans[0]], tables[spans[1]]
    depth = table.shape[1]
    valid = neighbours(place, edges)
    grad_copy = pltpu.make_async_copy(grad_far, grad, sem)
    grad_copy.start()
    for place, block in enumerate(blocks):
        set_rows(rows, place * main, block[:main].astype(F32))
    used = count * main
    low = jnp.concatenate([block[main:] for block in blocks], axis=0)
    set_rows(rows, used, jnp.dot(low_table, low, preferred_element_type=F32))
    set_rows(rows, used + cols_dev, jnp.zeros((rows.shape[1] - used - cols_dev, ch), F32))
    lcol[...] = left[left.shape[0] - rows_dev :].astype(F32) * valid[0]
    rcol[...] = right[right.shape[0] - rows_dev :].astype(F32) * valid[1]
    for w in range(0, cols_dev, 2):
        modes = jnp.concatenate(
            [get_rows(rows, w + i, depth, cols_dev).astype(BF16) for i in range(2)], axis=1
        )
        lines = jnp.dot(table, modes, preferred_element_type=F32)
        for i in range(2):
            set_rows(cells, w + i, lines[:, i * ch : (i + 1) * ch], cols_dev)
    column = lax.broadcasted_iota(jnp.int32, (cols_dev, ch), 0)

    def total(at):
        line = get_rows(cells, pl.multiple_of(at * cols_dev, 8), cols_dev) + grad[at]
        line = line + jnp.where(column == 0, lcol[pl.ds(at, 1), :], 0.0)
        return line + jnp.where(column == cols_dev - 1, rcol[pl.ds(at, 1), :], 0.0)

    grad_copy.wait()

    def store(step, carry):
        for sub in range(4):
            at = step * 4 + sub
            out[at] = total(at).astype(BF16)
        return carry

    lax.fori_loop(0, rows_dev // 4, store, 0)
    out[0] = (total(0) + above[...].astype(F32)).astype(BF16)
    last = rows_dev - 1
    out[last] = (total(last) + below[...].astype(F32)).astype(BF16)


def in_vmem():
    return pl.BlockSpec(memory_space=pltpu.VMEM)


def in_hbm():
    return pl.BlockSpec(memory_space=pltpu.HBM)


def in_smem():
    return pl.BlockSpec(memory_space=pltpu.SMEM)


def call(kernel, out_shapes, in_specs, scratch, name, limit, out_specs=None):
    many = isinstance(out_shapes, (list, tuple))
    return pl.pallas_call(
        kernel,
        out_shape=out_shapes,
        in_specs=in_specs,
        out_specs=out_specs or ([in_vmem() for _ in out_shapes] if many else in_vmem()),
        scratch_shapes=scratch,
        compiler_params=pltpu.CompilerParams(vmem_limit_bytes=limit << 20),
        name=name,
    )


def cos_sin(product, period):
    theta = (product % period) * (2.0 * math.pi / period)
    return np.cos(theta), np.sin(theta)


def padded(table, rows, cols):
    return np.pad(table, ((0, rows - table.shape[0]), (0, cols - table.shape[1])))


def angle_tables(n_gx, n_gy, rows_dev, cols_dev):
    sizes = layout(n_gx, cols_dev)
    slots, reals, groups, width, fold, virtual, per = sizes
    chips, share = n_gx // 2, KW // n_gx
    split = slots % n_gy == 0
    here = slots // n_gy if split else slots
    full_rows, full_cols = rows_dev * n_gx, cols_dev * n_gy
    used = 2 * chips * reals
    depth_in, depth_out = round_up(rows_dev + 2, 16), round_up(used + 1, 16)
    modes = np.arange(KW)
    chip_ids = np.arange(chips)

    def row_angles(rows, freqs):
        cosine, sine = cos_sin(rows[:, None] * freqs[None, :], full_rows)
        table = np.stack([cosine, sine], axis=2).reshape(len(rows), used)
        ones = np.ones((len(rows), 1))
        return np.concatenate([table, ones, np.zeros((len(rows), depth_out - used - 1))], axis=1)

    def low_angles(cols, owners):
        product = (owners[:, None] * share + np.arange(share)[None, :])[None] * cols[:, None, None]
        cosine, sine = cos_sin(product, full_cols)
        spare = np.zeros_like(cosine)
        return np.concatenate([cosine, sine, spare, spare], axis=2)

    def owners_of(order, core):
        return np.concatenate([2 * order + core, 2 * order + 1 - core])

    both, forth, back = [], [], []
    wide = np.arange(virtual)
    for gy in range(n_gy):
        sources = (gy - np.arange(n_gy)) % n_gy if split else np.arange(n_gy)
        ext_cols = sources[:, None] * cols_dev - 1 + wide[None, :]
        inside = (ext_cols >= 0) & (ext_cols < full_cols) & (wide < width)[None, :]
        cosine, sine = cos_sin(modes[:, None] * ext_cols.reshape(1, -1), full_cols)
        forth.append(np.concatenate([cosine, sine]) * inside.reshape(1, -1))
        all_cols = (sources[:, None] * cols_dev + np.arange(cols_dev)[None, :]).reshape(-1, 1)
        back.append(np.concatenate(cos_sin(all_cols * modes[None, :], full_cols) * 2, axis=1))
    for gx in range(n_gx):
        chip, core = gx // 2, gx % 2
        for gy in range(n_gy):
            places = np.arange(slots)
            if split:
                places = (places + gy * here) % slots

            def frequencies(owners):
                ids = (owners[:, None] * slots + places[None, :]).reshape(-1)
                return np.where(ids == 0, KH // 2, ids)

            order = (chip_ids + chip) % chips
            ext_rows = gx * rows_dev - 1 + np.arange(depth_in)
            inside = (ext_rows >= 0) & (ext_rows < full_rows) & (np.arange(depth_in) < rows_dev + 2)
            row_table = (row_angles(ext_rows, frequencies(owners_of(order, core))) * inside[:, None]).T
            owners = owners_of((chip - chip_ids) % chips, core)
            back_rows = row_angles(gx * rows_dev + np.arange(rows_dev), frequencies(owners))
            cols = gy * cols_dev - 1 + wide
            inside = (cols >= 0) & (cols < full_cols) & (wide < width)
            low_table = (low_angles(cols, np.array([gx]))[:, 0] * inside[:, None]).T
            back_low = low_angles(gy * cols_dev + np.arange(cols_dev), owners).reshape(cols_dev, -1)
            tables = [row_table, back_rows, low_table, back_low]
            lanes = round_up(max(table.shape[1] for table in tables), LANES)
            both.append(np.concatenate([padded(t, round_up(len(t), 16), lanes) for t in tables]))
    both = np.stack(both).reshape(n_gx, n_gy, *both[0].shape)
    return [np.asarray(table, np.float32).astype(BF16) for table in (both, np.stack(forth), np.stack(back))]


def table_spans(sizes, rows_dev, cols_dev, n_gx):
    slots, reals, groups, width, fold, virtual, per = sizes
    used, share = n_gx * reals, KW // n_gx
    shapes = [
        (round_up(used + 1, 16), round_up(rows_dev + 2, 16)),
        (rows_dev, round_up(used + 1, 16)),
        (4 * share, virtual),
        (cols_dev, n_gx * 4 * share),
    ]
    spans, begin = [], 0
    for rows, cols in shapes:
        spans.append((slice(begin, begin + rows), slice(0, cols)))
        begin += round_up(rows, 16)
    return spans


def body(saved_mid, out_grad, expert_weight, routes, gates, band_matrix, band_ids):
    rows_dev, cols_dev, ch = saved_mid.shape
    n_gx, n_gy = lax.axis_size("gx"), lax.axis_size("gy")
    gx, gy = lax.axis_index("gx"), lax.axis_index("gy")
    full_rows, full_cols = rows_dev * n_gx, cols_dev * n_gy
    sizes = layout(n_gx, cols_dev)
    slots, reals, groups, width, fold, virtual, per = sizes
    chips = n_gx // 2
    swap = [(i, i ^ 1) for i in range(n_gx)]
    experts = expert_weight.shape[0]

    def ring(array, axis, step):
        count = lax.axis_size(axis)
        return lax.ppermute(array, axis, [(i, (i + step) % count) for i in range(count)])

    def shape(*dims, dtype=BF16):
        return jax.ShapeDtypeStruct(dims, dtype)

    split = slots % n_gy == 0
    here = slots // n_gy if split else slots
    depth_in, depth_out = round_up(rows_dev + 2, 16), round_up(n_gx * reals + 1, 16)
    spans = table_spans(sizes, rows_dev, cols_dev, n_gx)
    tables, col_tables, back_tables = angle_tables(n_gx, n_gy, rows_dev, cols_dev)
    tables = jnp.asarray(tables)[gx, gy]
    col_table, back_table = jnp.asarray(col_tables)[gy], jnp.asarray(back_tables)[gy]
    share = KW // n_gx
    place = jnp.stack([gx, gy]).astype(jnp.int32)
    edges = (n_gx, n_gy)

    left = ring(saved_mid[:, cols_dev - 1, :], "gy", 1)
    right = ring(saved_mid[:, 0, :], "gy", -1)

    def edge_row(at):
        return jnp.concatenate([saved_mid[at], left[at : at + 1], right[at : at + 1]], axis=0)

    bottom = ring(edge_row(0), "gx", -1)
    top = ring(edge_row(rows_dev - 1), "gx", 1)

    picked = routes.shape[2]
    packed = per * ch
    lines = edge_blocks(cols_dev)
    extra = -(-2 * lines // chips) * ch
    keep, give, grad, e_left, e_right = call(
        functools.partial(conv_kernel, sizes, picked, edges, spans[0]),
        [
            shape(chips, groups * reals, packed),
            shape(chips, groups * reals, packed + extra),
            pltpu.HBM((rows_dev, cols_dev, ch), F32),
            shape(rows_dev, ch),
            shape(rows_dev, ch),
        ],
        [in_smem()] * 3 + [in_hbm()] + [in_vmem()] * 4 + [in_hbm()] * 2 + [in_vmem()],
        [
            pltpu.VMEM((rows_dev, cols_dev, ch), BF16),
            pltpu.VMEM((rows_dev, cols_dev, ch), BF16),
            pltpu.VMEM((experts, 9 * ch, ch), BF16),
            pltpu.VMEM((rows_dev, cols_dev, ch), F32),
            pltpu.VMEM((3, rows_dev + 2, cols_dev, ch), BF16),
            pltpu.VMEM((TILE * TILE, 9 * ch), BF16),
            pltpu.VMEM((TILE * TILE, (SHARED + picked) * ch), BF16),
            pltpu.VMEM((TILE * TILE, (SHARED + picked) * ch), BF16),
            pltpu.VMEM((3, rows_dev + 2, cols_dev, ch), F32),
            planes(depth_in * virtual, ch),
            planes(round_up(max(width, reals * fold), 8), ch),
            pltpu.VMEM((rows_dev, ch), F32),
            pltpu.VMEM((rows_dev, ch), F32),
            pltpu.SemaphoreType.DMA((experts,)),
            pltpu.SemaphoreType.DMA((3,)),
        ],
        "conv",
        40,
        [in_vmem()] * 2 + [in_hbm()] + [in_vmem()] * 2,
    )(
        routes.reshape(-1),
        gates.reshape(-1),
        place,
        pltpu.with_memory_space_constraint(saved_mid, pltpu.HBM),
        left,
        right,
        top,
        bottom,
        pltpu.with_memory_space_constraint(out_grad, pltpu.HBM),
        pltpu.with_memory_space_constraint(expert_weight.reshape(experts, 9 * ch, ch), pltpu.HBM),
        tables,
    )

    gift = lax.ppermute(give, "gx", swap)
    messages = [(keep[d].astype(F32) + gift[d, :, :packed].astype(F32)).astype(BF16) for d in range(chips)]
    for d, which in ((1, 1), (chips - 1, 0)):
        edge = find_edge(gift, chips, per, ch, lines, which)
        messages[d] = jnp.concatenate([messages[d], edge], axis=1)
    parts = [messages[0]] + [ring(messages[d], "gx", 2 * d) for d in range(1, chips)]
    block_rows = here * 2 * virtual
    if split:
        ends = [rows_dev if d in (1, n_gy - 1) else 0 for d in range(n_gy)]
        regrouped = [shape(block_rows + end, ch) for end in ends]
    else:
        regrouped = [shape(block_rows, ch), shape(rows_dev, ch), shape(rows_dev, ch)]
    from_above, from_below, *regrouped = call(
        functools.partial(regroup_kernel, sizes, chips, here, edges, spans[2]),
        [shape(cols_dev, ch), shape(cols_dev, ch), *regrouped],
        [in_smem()] + [in_vmem()] * (4 + chips),
        [planes((reals + 1) * virtual, ch)],
        "regroup",
        8,
    )(place, gift, e_left, e_right, tables, *parts)

    if split:
        cells = [regrouped[0]] + [ring(regrouped[d], "gy", d) for d in range(1, n_gy)]
        from_left, from_right = cells[1], cells[n_gy - 1]
    else:
        gathered = lax.all_gather(regrouped[0], "gy", axis=0)
        cells = [gathered[z] for z in range(n_gy)]
        from_left, from_right = ring(regrouped[1], "gy", 1), ring(regrouped[2], "gy", -1)
    low_modes, *mixed = call(
        functools.partial(
            modes_kernel,
            sizes,
            split,
            1.0 / math.sqrt(full_rows * full_cols),
            1.0 / math.sqrt(2 * KH * KW),
            n_gy,
        ),
        [shape(4 * share, ch)] + [shape(here * 2 * cols_dev, ch) for _ in range(n_gy)],
        [in_smem()] + [in_vmem()] * (4 + n_gy),
        [],
        "modes",
        12,
    )(place, col_table, back_table, band_ids, band_matrix, *cells)
    if split:
        mixed = [mixed[0]] + [ring(mixed[d], "gy", -d) for d in range(1, n_gy)]
    else:
        mixed = [lax.dynamic_index_in_dim(jnp.stack(mixed), gy, 0, keepdims=False)]
    block = jnp.concatenate([*mixed, low_modes], axis=0)

    blocks = [block] + [ring(block, "gx", 2 * d) for d in range(1, chips)]
    blocks = blocks + [lax.ppermute(array, "gx", swap) for array in blocks]
    return call(
        functools.partial(final_kernel, n_gx, slots * 2 * cols_dev, edges, (spans[1], spans[3])),
        shape(rows_dev, cols_dev, ch),
        [in_smem(), in_vmem(), in_hbm()] + [in_vmem()] * (4 + n_gx),
        [
            pltpu.VMEM((rows_dev, cols_dev, ch), F32),
            planes(depth_out * cols_dev, ch),
            planes(rows_dev * cols_dev, ch),
            pltpu.VMEM((rows_dev, ch), F32),
            pltpu.VMEM((rows_dev, ch), F32),
            pltpu.SemaphoreType.DMA,
        ],
        "final",
        16,
    )(place, tables, grad, from_left, from_right, from_above, from_below, *blocks)


def solution(mesh):
    placed = (
        P("gx", "gy", None),
        P("gx", "gy", None),
        P(),
        P("gx", "gy", None),
        P("gx", "gy", None),
        P(),
        P(),
    )
    return jax.shard_map(
        body, mesh=mesh, in_specs=placed, out_specs=P("gx", "gy", None), check_vma=False
    )
```

time: 120 us -> 93.1 us (0.78)
  blocking collectives: 10.3 us -> 0 us
  starting transfers between devices: 25.9 us -> 19.8 us
  Pallas kernels: 44.4 us -> 39.6 us
  other arithmetic: 3.75 us -> 0.28 us
  local copies, waits for them, and re-layouts: 9.26 us -> 5.82 us
  waiting for transfers between devices: 23.7 us -> 26.8 us
  between operations: 1.57 us -> 0.28 us
    ppermute x8 -> x16, waiting for transfers between devices: 3.79 us -> 23.6 us  [ring(): lax.ppermute(array, axis, [(i, (i + step) % count) for i in range(count)])]
    all_to_all x3 -> x0, waiting for transfers between devices: 18 us -> none  [the longest x1 9.45 us: body(): lax.all_to_all(summed, 'gx', 0, 0, tiled=True, axis_index_groups=same_core)]
    all_to_all x3 -> x0, starting transfers between devices: 10.5 us -> none  [the longest x1 3.61 us: body(): lax.all_to_all(summed, 'gx', 0, 0, tiled=True, axis_index_groups=same_core)]
    all_gather x1 -> x0, blocking collectives: 10.3 us -> none  [body(): mine = lax.all_gather(block, 'gx', axis=0, axis_index_groups=same_core)]
    pallas_call x4, Pallas kernels: 44.4 us -> 39.6 us  [the longest x1 32.4 us: body(): call(functools.partial(conv_kernel, sizes, picked, edges, spans[0]), [sha...]
    ppermute x8 -> x16, starting transfers between devices: 15.4 us -> 19.2 us  [ring(): lax.ppermute(array, axis, [(i, (i + step) % count) for i in range(count)])]
    unnamed x14 -> x13, local copies, waits for them, and re-layouts: 3.61 us -> 0.12 us
    squeeze x2 -> x5, local copies, waits for them, and re-layouts: 0.74 us -> 3.05 us  [the longest x1 0.79 us: body(): tables = jnp.asarray(tables)[gx, gy]]
  transfers between devices with their start and end apart: 13 -> 21, of which waited for: 6 -> 14; matrix products, arithmetic and copies ran while one was open for 6% -> 5% of each run, Pallas kernels for 2% -> 0%
where the time goes in v2:
time: 93.1 us; the launch traced here: 92.6 us
  Pallas kernels  39.6 us (43%)
  waiting for transfers between devices  26.8 us (29%)
  starting transfers between devices  19.8 us (21%)
  local copies, waits for them, and re-layouts  5.82 us (6%)
    pallas_call x1, Pallas kernels, body(): call(functools.partial(conv_kernel, sizes, picked, edges, spans[0]), [sha...  32.4 us
    ppermute x16, waiting for transfers between devices, ring(): lax.ppermute(array, axis, [(i, (i + step) % count) for i in range(count)])  23.6 us
    ppermute x16, starting transfers between devices, ring(): lax.ppermute(array, axis, [(i, (i + step) % count) for i in range(count)])  19.2 us
    pallas_call x1, Pallas kernels, body(): call(functools.partial(final_kernel, n_gx, slots * 2 * cols_dev, edges, (...  4.68 us
    ppermute x1, waiting for transfers between devices, body(): gift = lax.ppermute(give, 'gx', swap)  2.18 us
  transfers between devices with their start and end apart: 21, of which 14 were waited for; matrix products, arithmetic and copies ran while one was open for 5% of the time, Pallas kernels for 0%

profile of v2, /device:TPU:0, one launch (start us, length us, event | category | flops | bytes accessed | tf_op | source)
XLA Modules:
  0.0 92.6 jit_solution(2049334799761382103)
XLA Ops:
  0.0 1.1 %fusion.4 = (bf16[48,1,256]{2,1,0:T(2,128)(2,1)S(1)}, bf16[48,1,256]{2,1,0:T(2,128)(2,1)S(1)}) fusion(bf16[48,32,256]{2,1,0:T(8,128)(2,1)} %x_far.1), kind=kLoop, calls=%fused_computation.31 | loop fusion | bytes 98304 | tf_op jit(solution)/shard_map/slice | solution.py:616
  1.1 3.1 %collective-permute-start = (bf16[48,256]{1,0:T(8,128)(2,1)S(1)}, bf16[48,256]{1,0:T(8,128)(2,1)S(1)}, u32[]{:S(2)}, u32[]{:S(2)}) collective-permute-start(bf16[48,256]{1,0:T(8,128)(2,1)S(1)} %bitcast.40), channel_id=1, source_target_pairs={{0,1},{1,2},{2,3},{3,0},{4,5},{5,6},{6,7},{7,4},{8,9},{9,10},{10,1... | collective-permute-start | bytes 73736 | tf_op jit(solution)/shard_map/ppermute | solution.py:599
  4.2 2.1 %collective-permute-start.1 = (bf16[48,256]{1,0:T(8,128)(2,1)S(1)}, bf16[48,256]{1,0:T(8,128)(2,1)S(1)}, u32[]{:S(2)}, u32[]{:S(2)}) collective-permute-start(bf16[48,256]{1,0:T(8,128)(2,1)S(1)} %bitcast.41), channel_id=1, source_target_pairs={{0,3},{1,0},{2,1},{3,2},{4,7},{5,4},{6,5},{7,6},{8,11},{9,8},{10,9... | collective-permute-start | bytes 73736 | tf_op jit(solution)/shard_map/ppermute | solution.py:599
  7.0 0.8 dynamic-slice_bitcast_fusion.tables
  8.3 1.2 %collective-permute-start.3 = (bf16[34,256]{1,0:T(8,128)(2,1)S(1)}, bf16[34,256]{1,0:T(8,128)(2,1)S(1)}, u32[]{:S(2)}, u32[]{:S(2)}) collective-permute-start(bf16[34,256]{1,0:T(8,128)(2,1)S(1)} %pad_maximum_fusion.3), channel_id=1, source_target_pairs={{0,28},{4,0},{8,4},{12,8},{16,12},{20,16},{24,20},{28,24},{1,29},{... | collective-permute-start | bytes 52232 | tf_op jit(solution)/shard_map/ppermute | solution.py:599
  10.5 0.8 reshape.26.gates
  11.2 2.5 %collective-permute-done.2.top = bf16[34,256]{1,0:T(8,128)(2,1)S(1)} collective-permute-done((bf16[34,256]{1,0:T(8,128)(2,1)S(1)}, bf16[34,256]{1,0:T(8,128)(2,1)S(1)}, u32[]{:S(2)}, u32[]{:S(2)}) %collective-permute-start.2) | collective-permute-done | bytes 17440 | tf_op jit(solution)/shard_map/ppermute | solution.py:599
  13.7 32.4 %conv.1 = (bf16[4,16,5120]{2,1,0:T(8,128)(2,1)S(1)}, bf16[4,16,5632]{2,1,0:T(8,128)(2,1)S(1)}, f32[48,32,256]{2,1,0:T(8,128)}, bf16[48,256]{1,0:T(8,128)(2,1)S(1)}, bf16[48,256]{1,0:T(8,128)(2,1)S(1)}) custom-call(s32[24]{0:T(128)S(1)} %reshape.25.routes, f32[36]{0:T(128)S(1)} %reshape.26.gates, s32[2]{0:T(128)S(1)} %pad_add_fusion.place_ref.place, ...), custom_call_target="tpu_custom_call" | custom-call | tf_op jit(solution)/shard_map/conv/pallas_call | solution.py:628
  46.2 2.2 %collective-permute-done.4.gift = bf16[4,16,5632]{2,1,0:T(8,128)(2,1)S(1)} collective-permute-done((bf16[4,16,5632]{2,1,0:T(8,128)(2,1)S(1)}, bf16[4,16,5632]{2,1,0:T(8,128)(2,1)S(1)}, u32[]{:S(2)}, u32[]{:S(2)}) %collective-permute-start.4) | collective-permute-done | bytes 720928 | tf_op jit(solution)/shard_map/ppermute | solution.py:672
  49.1 1.7 %collective-permute-start.5 = (bf16[16,5888]{1,0:T(8,128)(2,1)S(1)}, bf16[16,5888]{1,0:T(8,128)(2,1)S(1)}, u32[]{:S(2)}, u32[]{:S(2)}) collective-permute-start(bf16[16,5888]{1,0:T(8,128)(2,1)S(1)} %pad_maximum_fusion), channel_id=1, source_target_pairs={{0,8},{4,12},{8,16},{12,20},{16,24},{20,28},{24,0},{28,4},{1,9},{5... | collective-permute-start | bytes 565256 | tf_op jit(solution)/shard_map/ppermute | solution.py:599
  52.0 8.4 %collective-permute-done.6.refs_2_ = bf16[16,5120]{1,0:T(8,128)(2,1)S(1)} collective-permute-done((bf16[16,5120]{1,0:T(8,128)(2,1)S(1)}, bf16[16,5120]{1,0:T(8,128)(2,1)S(1)}, u32[]{:S(2)}, u32[]{:S(2)}) %collective-permute-start.6) | collective-permute-done | bytes 163872 | tf_op jit(solution)/shard_map/ppermute | solution.py:599
  60.5 0.8 regroup.1
  61.3 0.8 collective-permute-start.8
  62.0 3.1 %collective-permute-start.9 = (bf16[128,256]{1,0:T(8,128)(2,1)S(1)}, bf16[128,256]{1,0:T(8,128)(2,1)S(1)}, u32[]{:S(2)}, u32[]{:S(2)}) collective-permute-start(bf16[128,256]{1,0:T(8,128)(2,1)S(1)} %get-tuple-element.27), channel_id=1, source_target_pairs={{0,3},{1,0},{2,1},{3,2},{4,7},{5,4},{6,5},{7,6},{8,11},{9,8},{10,9... | collective-permute-start | bytes 196616 | tf_op jit(solution)/shard_map/ppermute | solution.py:599
  66.0 4.1 %collective-permute-done.10.refs_2_ = bf16[80,256]{1,0:T(8,128)(2,1)S(1)} collective-permute-done((bf16[80,256]{1,0:T(8,128)(2,1)S(1)}, bf16[80,256]{1,0:T(8,128)(2,1)S(1)}, u32[]{:S(2)}, u32[]{:S(2)}) %collective-permute-start.10) | collective-permute-done | bytes 40992 | tf_op jit(solution)/shard_map/ppermute | solution.py:599
  70.0 1.7 %modes.1 = (bf16[16,256]{1,0:T(8,128)(2,1)S(1)}, bf16[64,256]{1,0:T(8,128)(2,1)S(1)}, bf16[64,256]{1,0:T(8,128)(2,1)S(1)}, bf16[64,256]{1,0:T(8,128)(2,1)S(1)}, bf16[64,256]{1,0:T(8,128)(2,1)S(1)}) custom-call(s32[2]{0:T(128)S(1)} %pad_add_fusion.place_ref.place, bf16[64,160]{1,0:T(8,128)(2,1)S(1)} %dynamic-slice_bitcast_fusion.2.col_table, ...), custom_call_target="tpu_custom_call" | custom-call | tf_op jit(solution)/shard_map/modes/pallas_call | solution.py:700
  71.8 2.1 %collective-permute-start.11 = (bf16[64,256]{1,0:T(8,128)(2,1)S(1)}, bf16[64,256]{1,0:T(8,128)(2,1)S(1)}, u32[]{:S(2)}, u32[]{:S(2)}) collective-permute-start(bf16[64,256]{1,0:T(8,128)(2,1)S(1)} %get-tuple-element.33), channel_id=1, source_target_pairs={{0,3},{1,0},{2,1},{3,2},{4,7},{5,4},{6,5},{7,6},{8,11},{9,8},{10,9... | collective-permute-start | bytes 98312 | tf_op jit(solution)/shard_map/ppermute | solution.py:599
  74.7 1.6 %collective-permute-done.11 = bf16[64,256]{1,0:T(8,128)(2,1)S(1)} collective-permute-done((bf16[64,256]{1,0:T(8,128)(2,1)S(1)}, bf16[64,256]{1,0:T(8,128)(2,1)S(1)}, u32[]{:S(2)}, u32[]{:S(2)}) %collective-permute-start.11) | collective-permute-done | bytes 32800 | tf_op jit(solution)/shard_map/ppermute | solution.py:599
  76.2 2.5 %collective-permute-done.12 = bf16[64,256]{1,0:T(8,128)(2,1)S(1)} collective-permute-done((bf16[64,256]{1,0:T(8,128)(2,1)S(1)}, bf16[64,256]{1,0:T(8,128)(2,1)S(1)}, u32[]{:S(2)}, u32[]{:S(2)}) %collective-permute-start.12) | collective-permute-done | bytes 32800 | tf_op jit(solution)/shard_map/ppermute | solution.py:599
  78.7 0.9 collective-permute-done.13
  79.6 1.0 %collective-permute-start.15 = (bf16[272,256]{1,0:T(8,128)(2,1)S(1)}, bf16[272,256]{1,0:T(8,128)(2,1)S(1)}, u32[]{:S(2)}, u32[]{:S(2)}) collective-permute-start(bf16[272,256]{1,0:T(8,128)(2,1)S(1)} %constant_dynamic-update-slice_fusion.refs_0_), channel_id=1, source_target_pairs={{0,16},{4,20},{8,24},{12,28},{16,0},{20,4},{24,8},{28,12},{1,17},{... | collective-permute-start | bytes 417800 | tf_op jit(solution)/shard_map/ppermute | solution.py:599
  80.6 2.5 %collective-permute-start.16 = (bf16[272,256]{1,0:T(8,128)(2,1)S(1)}, bf16[272,256]{1,0:T(8,128)(2,1)S(1)}, u32[]{:S(2)}, u32[]{:S(2)}) collective-permute-start(bf16[272,256]{1,0:T(8,128)(2,1)S(1)} %constant_dynamic-update-slice_fusion.refs_0_), channel_id=1, source_target_pairs={{0,24},{4,28},{8,0},{12,4},{16,8},{20,12},{24,16},{28,20},{1,25},{... | collective-permute-start | bytes 417800 | tf_op jit(solution)/shard_map/ppermute | solution.py:599
  83.0 2.6 %collective-permute-done.14.refs_1_ = bf16[272,256]{1,0:T(8,128)(2,1)S(1)} collective-permute-done((bf16[272,256]{1,0:T(8,128)(2,1)S(1)}, bf16[272,256]{1,0:T(8,128)(2,1)S(1)}, u32[]{:S(2)}, u32[]{:S(2)}) %collective-permute-start.14) | collective-permute-done | bytes 139296 | tf_op jit(solution)/shard_map/ppermute | solution.py:599
  87.8 4.7 %final.1 = bf16[48,32,256]{2,1,0:T(8,128)(2,1)} custom-call(s32[2]{0:T(128)S(1)} %pad_add_fusion.place_ref.place, bf16[176,128]{1,0:T(8,128)(2,1)S(1)} %dynamic-slice_bitcast_fusion.tables, f32[48,32,256]{2,1,0:T(8,128)S(1)} %copy-done.1, bf16[128,256]{1,0:T(8,128)(2,1)S(1)} %collective-permute-done.8.refs_1_.left, ...), custom_call_target="tpu_custom_call" | custom-call | tf_op jit(solution)/shard_map/final/pallas_call | solution.py:723
  (52 shorter events, 7.9 us)
Async XLA Ops:
  1.1 6.9 %collective-permute-start = (bf16[48,256]{1,0:T(8,128)(2,1)S(1)}, bf16[48,256]{1,0:T(8,128)(2,1)S(1)}, u32[]{:S(2)}, u32[]{:S(2)}) collective-permute-start(bf16[48,256]{1,0:T(8,128)(2,1)S(1)} %bitcast.40), channel_id=1, source_target_pairs={{0,1},{1,2},{2,3},{3,0},{4,5},{5,6},{6,7},{7,4},{8,9},{9,10},{10,1... | collective-permute-start | bytes 73736 | tf_op jit(solution)/shard_map/ppermute | solution.py:599
  4.2 4.1 %collective-permute-start.1 = (bf16[48,256]{1,0:T(8,128)(2,1)S(1)}, bf16[48,256]{1,0:T(8,128)(2,1)S(1)}, u32[]{:S(2)}, u32[]{:S(2)}) collective-permute-start(bf16[48,256]{1,0:T(8,128)(2,1)S(1)} %bitcast.41), channel_id=1, source_target_pairs={{0,3},{1,0},{2,1},{3,2},{4,7},{5,4},{6,5},{7,6},{8,11},{9,8},{10,9... | collective-permute-start | bytes 73736 | tf_op jit(solution)/shard_map/ppermute | solution.py:599
  8.3 2.9 %collective-permute-start.3 = (bf16[34,256]{1,0:T(8,128)(2,1)S(1)}, bf16[34,256]{1,0:T(8,128)(2,1)S(1)}, u32[]{:S(2)}, u32[]{:S(2)}) collective-permute-start(bf16[34,256]{1,0:T(8,128)(2,1)S(1)} %pad_maximum_fusion.3), channel_id=1, source_target_pairs={{0,28},{4,0},{8,4},{12,8},{16,12},{20,16},{24,20},{28,24},{1,29},{... | collective-permute-start | bytes 52232 | tf_op jit(solution)/shard_map/ppermute | solution.py:599
  9.6 4.2 %collective-permute-start.2 = (bf16[34,256]{1,0:T(8,128)(2,1)S(1)}, bf16[34,256]{1,0:T(8,128)(2,1)S(1)}, u32[]{:S(2)}, u32[]{:S(2)}) collective-permute-start(bf16[34,256]{1,0:T(8,128)(2,1)S(1)} %pad_maximum_fusion.2), channel_id=1, source_target_pairs={{0,4},{4,8},{8,12},{12,16},{16,20},{20,24},{24,28},{28,0},{1,5},{5... | collective-permute-start | bytes 52232 | tf_op jit(solution)/shard_map/ppermute | solution.py:599
  46.1 2.3 %collective-permute-start.4 = (bf16[4,16,5632]{2,1,0:T(8,128)(2,1)S(1)}, bf16[4,16,5632]{2,1,0:T(8,128)(2,1)S(1)}, u32[]{:S(2)}, u32[]{:S(2)}) collective-permute-start(bf16[4,16,5632]{2,1,0:T(8,128)(2,1)S(1)} %get-tuple-element.22), channel_id=1, source_target_pairs={{0,4},{4,0},{8,12},{12,8},{16,20},{20,16},{24,28},{28,24},{1,5},{5... | collective-permute-start | bytes 2162696 | tf_op jit(solution)/shard_map/ppermute | solution.py:672
  48.6 17.3 %copy-start.2 = (s32[64,32]{0,1:T(8,128)S(1)}, s32[64,32]{0,1:T(8,128)}, u32[]{:S(2)}) copy-start(s32[64,32]{0,1:T(8,128)} %param.16) | copy-start | bytes 24580
  48.6 21.5 %copy-start = (bf16[16,256,256]{2,1,0:T(8,128)(2,1)S(1)}, bf16[16,256,256]{2,1,0:T(8,128)(2,1)}, u32[]{:S(2)}) copy-start(bf16[16,256,256]{2,1,0:T(8,128)(2,1)} %bands.1) | copy-start | bytes 6291460
  48.6 11.9 %collective-permute-start.7 = (bf16[16,5888]{1,0:T(8,128)(2,1)S(1)}, bf16[16,5888]{1,0:T(8,128)(2,1)S(1)}, u32[]{:S(2)}, u32[]{:S(2)}) collective-permute-start(bf16[16,5888]{1,0:T(8,128)(2,1)S(1)} %pad_maximum_fusion.1), channel_id=1, source_target_pairs={{0,24},{4,28},{8,0},{12,4},{16,8},{20,12},{24,16},{28,20},{1,25},{... | collective-permute-start | bytes 565256 | tf_op jit(solution)/shard_map/ppermute | solution.py:599
  49.1 11.4 %collective-permute-start.5 = (bf16[16,5888]{1,0:T(8,128)(2,1)S(1)}, bf16[16,5888]{1,0:T(8,128)(2,1)S(1)}, u32[]{:S(2)}, u32[]{:S(2)}) collective-permute-start(bf16[16,5888]{1,0:T(8,128)(2,1)S(1)} %pad_maximum_fusion), channel_id=1, source_target_pairs={{0,8},{4,12},{8,16},{12,20},{16,24},{20,28},{24,0},{28,4},{1,9},{5... | collective-permute-start | bytes 565256 | tf_op jit(solution)/shard_map/ppermute | solution.py:599
  50.8 9.7 %collective-permute-start.6 = (bf16[16,5120]{1,0:T(8,128)(2,1)S(1)}, bf16[16,5120]{1,0:T(8,128)(2,1)S(1)}, u32[]{:S(2)}, u32[]{:S(2)}) collective-permute-start(bf16[16,5120]{1,0:T(8,128)(2,1)S(1)} %get-tuple-element.38), channel_id=1, source_target_pairs={{0,16},{4,20},{8,24},{12,28},{16,0},{20,4},{24,8},{28,12},{1,17},{... | collective-permute-start | bytes 491528 | tf_op jit(solution)/shard_map/ppermute | solution.py:599
  61.3 8.8 %collective-permute-start.8 = (bf16[128,256]{1,0:T(8,128)(2,1)S(1)}, bf16[128,256]{1,0:T(8,128)(2,1)S(1)}, u32[]{:S(2)}, u32[]{:S(2)}) collective-permute-start(bf16[128,256]{1,0:T(8,128)(2,1)S(1)} %get-tuple-element.26), channel_id=1, source_target_pairs={{0,1},{1,2},{2,3},{3,0},{4,5},{5,6},{6,7},{7,4},{8,9},{9,10},{10,1... | collective-permute-start | bytes 196616 | tf_op jit(solution)/shard_map/ppermute | solution.py:599
  62.0 8.0 %collective-permute-start.9 = (bf16[128,256]{1,0:T(8,128)(2,1)S(1)}, bf16[128,256]{1,0:T(8,128)(2,1)S(1)}, u32[]{:S(2)}, u32[]{:S(2)}) collective-permute-start(bf16[128,256]{1,0:T(8,128)(2,1)S(1)} %get-tuple-element.27), channel_id=1, source_target_pairs={{0,3},{1,0},{2,1},{3,2},{4,7},{5,4},{6,5},{7,6},{8,11},{9,8},{10,9... | collective-permute-start | bytes 196616 | tf_op jit(solution)/shard_map/ppermute | solution.py:599
  65.1 4.9 %collective-permute-start.10 = (bf16[80,256]{1,0:T(8,128)(2,1)S(1)}, bf16[80,256]{1,0:T(8,128)(2,1)S(1)}, u32[]{:S(2)}, u32[]{:S(2)}) collective-permute-start(bf16[80,256]{1,0:T(8,128)(2,1)S(1)} %get-tuple-element.31), channel_id=1, source_target_pairs={{0,2},{1,3},{2,0},{3,1},{4,6},{5,7},{6,4},{7,5},{8,10},{9,11},{10,... | collective-permute-start | bytes 122888 | tf_op jit(solution)/shard_map/ppermute | solution.py:599
  66.0 21.8 %copy-start.1 = (f32[48,32,256]{2,1,0:T(8,128)S(1)}, f32[48,32,256]{2,1,0:T(8,128)}, u32[]{:S(2)}) copy-start(f32[48,32,256]{2,1,0:T(8,128)} %get-tuple-element.21.grad_far) | copy-start | bytes 4718596
  71.8 4.4 %collective-permute-start.11 = (bf16[64,256]{1,0:T(8,128)(2,1)S(1)}, bf16[64,256]{1,0:T(8,128)(2,1)S(1)}, u32[]{:S(2)}, u32[]{:S(2)}) collective-permute-start(bf16[64,256]{1,0:T(8,128)(2,1)S(1)} %get-tuple-element.33), channel_id=1, source_target_pairs={{0,3},{1,0},{2,1},{3,2},{4,7},{5,4},{6,5},{7,6},{8,11},{9,8},{10,9... | collective-permute-start | bytes 98312 | tf_op jit(solution)/shard_map/ppermute | solution.py:599
  73.9 4.8 %collective-permute-start.12 = (bf16[64,256]{1,0:T(8,128)(2,1)S(1)}, bf16[64,256]{1,0:T(8,128)(2,1)S(1)}, u32[]{:S(2)}, u32[]{:S(2)}) collective-permute-start(bf16[64,256]{1,0:T(8,128)(2,1)S(1)} %get-tuple-element.34), channel_id=1, source_target_pairs={{0,2},{1,3},{2,0},{3,1},{4,6},{5,7},{6,4},{7,5},{8,10},{9,11},{10,... | collective-permute-start | bytes 98312 | tf_op jit(solution)/shard_map/ppermute | solution.py:599
  73.9 5.7 %collective-permute-start.13 = (bf16[64,256]{1,0:T(8,128)(2,1)S(1)}, bf16[64,256]{1,0:T(8,128)(2,1)S(1)}, u32[]{:S(2)}, u32[]{:S(2)}) collective-permute-start(bf16[64,256]{1,0:T(8,128)(2,1)S(1)} %get-tuple-element.35), channel_id=1, source_target_pairs={{0,1},{1,2},{2,3},{3,0},{4,5},{5,6},{6,7},{7,4},{8,9},{9,10},{10,1... | collective-permute-start | bytes 98312 | tf_op jit(solution)/shard_map/ppermute | solution.py:599
  79.6 6.1 %collective-permute-start.14 = (bf16[272,256]{1,0:T(8,128)(2,1)S(1)}, bf16[272,256]{1,0:T(8,128)(2,1)S(1)}, u32[]{:S(2)}, u32[]{:S(2)}) collective-permute-start(bf16[272,256]{1,0:T(8,128)(2,1)S(1)} %constant_dynamic-update-slice_fusion.refs_0_), channel_id=1, source_target_pairs={{0,8},{4,12},{8,16},{12,20},{16,24},{20,28},{24,0},{28,4},{1,9},{5... | collective-permute-start | bytes 417800 | tf_op jit(solution)/shard_map/ppermute | solution.py:599
  79.6 6.6 %collective-permute-start.15 = (bf16[272,256]{1,0:T(8,128)(2,1)S(1)}, bf16[272,256]{1,0:T(8,128)(2,1)S(1)}, u32[]{:S(2)}, u32[]{:S(2)}) collective-permute-start(bf16[272,256]{1,0:T(8,128)(2,1)S(1)} %constant_dynamic-update-slice_fusion.refs_0_), channel_id=1, source_target_pairs={{0,16},{4,20},{8,24},{12,28},{16,0},{20,4},{24,8},{28,12},{1,17},{... | collective-permute-start | bytes 417800 | tf_op jit(solution)/shard_map/ppermute | solution.py:599
  80.6 5.7 %collective-permute-start.16 = (bf16[272,256]{1,0:T(8,128)(2,1)S(1)}, bf16[272,256]{1,0:T(8,128)(2,1)S(1)}, u32[]{:S(2)}, u32[]{:S(2)}) collective-permute-start(bf16[272,256]{1,0:T(8,128)(2,1)S(1)} %constant_dynamic-update-slice_fusion.refs_0_), channel_id=1, source_target_pairs={{0,24},{4,28},{8,0},{12,4},{16,8},{20,12},{24,16},{28,20},{1,25},{... | collective-permute-start | bytes 417800 | tf_op jit(solution)/shard_map/ppermute | solution.py:599
  83.0 3.7 %collective-permute-start.17 = (bf16[272,256]{1,0:T(8,128)(2,1)S(1)}, bf16[272,256]{1,0:T(8,128)(2,1)S(1)}, u32[]{:S(2)}, u32[]{:S(2)}) collective-permute-start(bf16[272,256]{1,0:T(8,128)(2,1)S(1)} %constant_dynamic-update-slice_fusion.refs_0_), channel_id=1, source_target_pairs={{0,4},{4,0},{8,12},{12,8},{16,20},{20,16},{24,28},{28,24},{1,5},{5... | collective-permute-start | bytes 417800 | tf_op jit(solution)/shard_map/ppermute | solution.py:722
  85.7 1.4 %collective-permute-start.18 = (bf16[272,256]{1,0:T(8,128)(2,1)S(1)}, bf16[272,256]{1,0:T(8,128)(2,1)S(1)}, u32[]{:S(2)}, u32[]{:S(2)}) collective-permute-start(bf16[272,256]{1,0:T(8,128)(2,1)S(1)} %collective-permute-done.14.refs_1_), channel_id=1, source_target_pairs={{0,4},{4,0},{8,12},{12,8},{16,20},{20,16},{24,28},{28,24},{1,5},{5... | collective-permute-start | bytes 417800 | tf_op jit(solution)/shard_map/ppermute | solution.py:722
  86.2 1.4 %collective-permute-start.19 = (bf16[272,256]{1,0:T(8,128)(2,1)S(1)}, bf16[272,256]{1,0:T(8,128)(2,1)S(1)}, u32[]{:S(2)}, u32[]{:S(2)}) collective-permute-start(bf16[272,256]{1,0:T(8,128)(2,1)S(1)} %collective-permute-done.15.refs_2_), channel_id=1, source_target_pairs={{0,4},{4,0},{8,12},{12,8},{16,20},{20,16},{24,28},{28,24},{1,5},{5... | collective-permute-start | bytes 417800 | tf_op jit(solution)/shard_map/ppermute | solution.py:722
  86.2 1.6 %collective-permute-start.20 = (bf16[272,256]{1,0:T(8,128)(2,1)S(1)}, bf16[272,256]{1,0:T(8,128)(2,1)S(1)}, u32[]{:S(2)}, u32[]{:S(2)}) collective-permute-start(bf16[272,256]{1,0:T(8,128)(2,1)S(1)} %collective-permute-done.16.refs_3_), channel_id=1, source_target_pairs={{0,4},{4,0},{8,12},{12,8},{16,20},{20,16},{24,28},{28,24},{1,5},{5... | collective-permute-start | bytes 417800 | tf_op jit(solution)/shard_map/ppermute | solution.py:722

commit v3 on v2

--- a/solution.py
+++ b/solution.py
@@ -55,6 +55,10 @@
         ref[h, pl.ds(start, values.shape[0], stride), :] = values[:, h * LANES : (h + 1) * LANES]
 
 
+def pitch(cols):
+    return cols + 8 if cols % 16 == 0 else cols
+
+
 def planes(rows, ch):
     return pltpu.VMEM((ch // LANES, rows, LANES), F32)
 
@@ -68,8 +72,13 @@
     field_copies = [
         pltpu.make_async_copy(x_far, x, field_sems.at[0]),
         pltpu.make_async_copy(grad_out_far, grad_out, field_sems.at[1]),
-        pltpu.make_async_copy(grad, grad_far, field_sems.at[2]),
     ]
+    pieces = rows_dev // TILE
+
+    def grad_copy(i):
+        span = pl.ds(i * TILE, TILE)
+        return pltpu.make_async_copy(grad.at[span], grad_far.at[span], field_sems.at[2 + i])
+
 
     def fetch(e):
         return pltpu.make_async_copy(weight_far.at[e], weight.at[e], weight_sems.at[e])
@@ -185,7 +194,7 @@
             fetch(e).wait()
         for e in early[first + 4 : first + 6]:
             fetch(e).start()
-        if first == firsts[-1]:
+        if first == min(2, firsts[-1]):
             for e in range(SHARED, experts):
 
                 @pl.when(jnp.logical_not(in_first(e)))
@@ -233,8 +242,9 @@
             grad[at] = put_ext(at + 1, grad_out[at].astype(F32))
         return carry
 
-    lax.fori_loop(0, rows_dev // 4, join, 0)
-    field_copies[2].start()
+    for i in range(pieces):
+        lax.fori_loop(i * TILE // 4, (i + 1) * TILE // 4, join, 0)
+        grad_copy(i).start()
     blocks = []
     for at in (0, rows_dev + 1):
         line = put_ext(at, None)
@@ -283,7 +293,8 @@
             later[v] = found
     for v, found in later.items():
         emit(v, found)
-    field_copies[2].wait()
+    for i in range(pieces):
+        grad_copy(i).wait()
 
 
 def neighbours(place, edges):
@@ -427,30 +438,33 @@
 def final_kernel(count, main, edges, spans, place, tables, grad_far, left, right, above, below, *refs):
     blocks, (out, grad, rows, cells, lcol, rcol, sem) = refs[:count], refs[count:]
     rows_dev, cols_dev, ch = out.shape
+    apart = pitch(cols_dev)
     table, low_table = tables[spans[0]], tables[spans[1]]
     depth = table.shape[1]
     valid = neighbours(place, edges)
     grad_copy = pltpu.make_async_copy(grad_far, grad, sem)
     grad_copy.start()
     for place, block in enumerate(blocks):
-        set_rows(rows, place * main, block[:main].astype(F32))
-    used = count * main
+        for i in range(main // cols_dev):
+            line = block[i * cols_dev : (i + 1) * cols_dev].astype(F32)
+            set_rows(rows, (place * (main // cols_dev) + i) * apart, line)
+    used = count * (main // cols_dev)
     low = jnp.concatenate([block[main:] for block in blocks], axis=0)
-    set_rows(rows, used, jnp.dot(low_table, low, preferred_element_type=F32))
-    set_rows(rows, used + cols_dev, jnp.zeros((rows.shape[1] - used - cols_dev, ch), F32))
+    set_rows(rows, used * apart, jnp.dot(low_table, low, preferred_element_type=F32))
+    set_rows(rows, (used + 1) * apart, jnp.zeros((rows.shape[1] - (used + 1) * apart, ch), F32))
     lcol[...] = left[left.shape[0] - rows_dev :].astype(F32) * valid[0]
     rcol[...] = right[right.shape[0] - rows_dev :].astype(F32) * valid[1]
     for w in range(0, cols_dev, 2):
         modes = jnp.concatenate(
-            [get_rows(rows, w + i, depth, cols_dev).astype(BF16) for i in range(2)], axis=1
+            [get_rows(rows, w + i, depth, apart).astype(BF16) for i in range(2)], axis=1
         )
         lines = jnp.dot(table, modes, preferred_element_type=F32)
         for i in range(2):
-            set_rows(cells, w + i, lines[:, i * ch : (i + 1) * ch], cols_dev)
+            set_rows(cells, w + i, lines[:, i * ch : (i + 1) * ch], apart)
     column = lax.broadcasted_iota(jnp.int32, (cols_dev, ch), 0)
 
     def total(at):
-        line = get_rows(cells, pl.multiple_of(at * cols_dev, 8), cols_dev) + grad[at]
+        line = get_rows(cells, pl.multiple_of(at * apart, 8), cols_dev) + grad[at]
         line = line + jnp.where(column == 0, lcol[pl.ds(at, 1), :], 0.0)
         return line + jnp.where(column == cols_dev - 1, rcol[pl.ds(at, 1), :], 0.0)
 
@@ -650,7 +664,7 @@
             pltpu.VMEM((rows_dev, ch), F32),
             pltpu.VMEM((rows_dev, ch), F32),
             pltpu.SemaphoreType.DMA((experts,)),
-            pltpu.SemaphoreType.DMA((3,)),
+            pltpu.SemaphoreType.DMA((2 + rows_dev // TILE,)),
         ],
         "conv",
         40,
@@ -726,8 +740,8 @@
         [in_smem(), in_vmem(), in_hbm()] + [in_vmem()] * (4 + n_gx),
         [
             pltpu.VMEM((rows_dev, cols_dev, ch), F32),
-            planes(depth_out * cols_dev, ch),
-            planes(rows_dev * cols_dev, ch),
+            planes(depth_out * pitch(cols_dev), ch),
+            planes(rows_dev * pitch(cols_dev), ch),
             pltpu.VMEM((rows_dev, ch), F32),
             pltpu.VMEM((rows_dev, ch), F32),
             pltpu.SemaphoreType.DMA,

time: 93.1 us -> 89.8 us (0.965)
  Pallas kernels: 39.6 us -> 36.3 us
    pallas_call x1, Pallas kernels: 4.68 us -> 2.71 us  [body(): call(functools.partial(final_kernel, n_gx, slots * 2 * cols_dev, edges, (...]
    pallas_call x1, Pallas kernels: 32.4 us -> 31.1 us  [body(): call(functools.partial(conv_kernel, sizes, picked, edges, spans[0]), [sha...]
where the time goes in v3:
time: 89.8 us; the launch traced here: 89.4 us
  Pallas kernels  36.3 us (40%)
  waiting for transfers between devices  26.8 us (30%)
  starting transfers between devices  19.8 us (22%)
  local copies, waits for them, and re-layouts  5.82 us (6%)
    pallas_call x1, Pallas kernels, body(): call(functools.partial(conv_kernel, sizes, picked, edges, spans[0]), [sha...  31.1 us
    ppermute x16, waiting for transfers between devices, ring(): lax.ppermute(array, axis, [(i, (i + step) % count) for i in range(count)])  23.6 us
    ppermute x16, starting transfers between devices, ring(): lax.ppermute(array, axis, [(i, (i + step) % count) for i in range(count)])  19.2 us
    pallas_call x1, Pallas kernels, body(): call(functools.partial(final_kernel, n_gx, slots * 2 * cols_dev, edges, (...  2.71 us
    ppermute x1, waiting for transfers between devices, body(): gift = lax.ppermute(give, 'gx', swap)  2.18 us
  transfers between devices with their start and end apart: 21, of which 14 were waited for; matrix products, arithmetic and copies ran while one was open for 5% of the time, Pallas kernels for 0%

profile of v3, /device:TPU:0, one launch (start us, length us, event | category | flops | bytes accessed | tf_op | source)
XLA Modules:
  0.0 89.4 jit_solution(889616702150197335)
XLA Ops:
  0.0 1.1 %fusion.4 = (bf16[48,1,256]{2,1,0:T(2,128)(2,1)S(1)}, bf16[48,1,256]{2,1,0:T(2,128)(2,1)S(1)}) fusion(bf16[48,32,256]{2,1,0:T(8,128)(2,1)} %x_far.1), kind=kLoop, calls=%fused_computation.31 | loop fusion | bytes 98304 | tf_op jit(solution)/shard_map/slice | solution.py:630
  1.1 3.1 %collective-permute-start = (bf16[48,256]{1,0:T(8,128)(2,1)S(1)}, bf16[48,256]{1,0:T(8,128)(2,1)S(1)}, u32[]{:S(2)}, u32[]{:S(2)}) collective-permute-start(bf16[48,256]{1,0:T(8,128)(2,1)S(1)} %bitcast.40), channel_id=1, source_target_pairs={{0,1},{1,2},{2,3},{3,0},{4,5},{5,6},{6,7},{7,4},{8,9},{9,10},{10,1... | collective-permute-start | bytes 73736 | tf_op jit(solution)/shard_map/ppermute | solution.py:613
  4.2 2.1 %collective-permute-start.1 = (bf16[48,256]{1,0:T(8,128)(2,1)S(1)}, bf16[48,256]{1,0:T(8,128)(2,1)S(1)}, u32[]{:S(2)}, u32[]{:S(2)}) collective-permute-start(bf16[48,256]{1,0:T(8,128)(2,1)S(1)} %bitcast.41), channel_id=1, source_target_pairs={{0,3},{1,0},{2,1},{3,2},{4,7},{5,4},{6,5},{7,6},{8,11},{9,8},{10,9... | collective-permute-start | bytes 73736 | tf_op jit(solution)/shard_map/ppermute | solution.py:613
  7.0 0.8 dynamic-slice_bitcast_fusion.tables
  8.3 1.2 %collective-permute-start.3 = (bf16[34,256]{1,0:T(8,128)(2,1)S(1)}, bf16[34,256]{1,0:T(8,128)(2,1)S(1)}, u32[]{:S(2)}, u32[]{:S(2)}) collective-permute-start(bf16[34,256]{1,0:T(8,128)(2,1)S(1)} %pad_maximum_fusion.3), channel_id=1, source_target_pairs={{0,28},{4,0},{8,4},{12,8},{16,12},{20,16},{24,20},{28,24},{1,29},{... | collective-permute-start | bytes 52232 | tf_op jit(solution)/shard_map/ppermute | solution.py:613
  10.5 0.8 reshape.26.gates
  11.2 2.5 %collective-permute-done.2.top = bf16[34,256]{1,0:T(8,128)(2,1)S(1)} collective-permute-done((bf16[34,256]{1,0:T(8,128)(2,1)S(1)}, bf16[34,256]{1,0:T(8,128)(2,1)S(1)}, u32[]{:S(2)}, u32[]{:S(2)}) %collective-permute-start.2) | collective-permute-done | bytes 17440 | tf_op jit(solution)/shard_map/ppermute | solution.py:613
  13.7 31.1 %conv.1 = (bf16[4,16,5120]{2,1,0:T(8,128)(2,1)S(1)}, bf16[4,16,5632]{2,1,0:T(8,128)(2,1)S(1)}, f32[48,32,256]{2,1,0:T(8,128)}, bf16[48,256]{1,0:T(8,128)(2,1)S(1)}, bf16[48,256]{1,0:T(8,128)(2,1)S(1)}) custom-call(s32[24]{0:T(128)S(1)} %reshape.25.routes, f32[36]{0:T(128)S(1)} %reshape.26.gates, s32[2]{0:T(128)S(1)} %pad_add_fusion.place_ref.place, ...), custom_call_target="tpu_custom_call" | custom-call | tf_op jit(solution)/shard_map/conv/pallas_call | solution.py:642
  44.9 2.2 %collective-permute-done.4.gift = bf16[4,16,5632]{2,1,0:T(8,128)(2,1)S(1)} collective-permute-done((bf16[4,16,5632]{2,1,0:T(8,128)(2,1)S(1)}, bf16[4,16,5632]{2,1,0:T(8,128)(2,1)S(1)}, u32[]{:S(2)}, u32[]{:S(2)}) %collective-permute-start.4) | collective-permute-done | bytes 720928 | tf_op jit(solution)/shard_map/ppermute | solution.py:686
  47.8 1.7 %collective-permute-start.5 = (bf16[16,5888]{1,0:T(8,128)(2,1)S(1)}, bf16[16,5888]{1,0:T(8,128)(2,1)S(1)}, u32[]{:S(2)}, u32[]{:S(2)}) collective-permute-start(bf16[16,5888]{1,0:T(8,128)(2,1)S(1)} %pad_maximum_fusion), channel_id=1, source_target_pairs={{0,8},{4,12},{8,16},{12,20},{16,24},{20,28},{24,0},{28,4},{1,9},{5... | collective-permute-start | bytes 565256 | tf_op jit(solution)/shard_map/ppermute | solution.py:613
  50.7 8.4 %collective-permute-done.6.refs_2_ = bf16[16,5120]{1,0:T(8,128)(2,1)S(1)} collective-permute-done((bf16[16,5120]{1,0:T(8,128)(2,1)S(1)}, bf16[16,5120]{1,0:T(8,128)(2,1)S(1)}, u32[]{:S(2)}, u32[]{:S(2)}) %collective-permute-start.6) | collective-permute-done | bytes 163872 | tf_op jit(solution)/shard_map/ppermute | solution.py:613
  59.2 0.8 regroup.1
  60.0 0.8 collective-permute-start.8
  60.7 3.1 %collective-permute-start.9 = (bf16[128,256]{1,0:T(8,128)(2,1)S(1)}, bf16[128,256]{1,0:T(8,128)(2,1)S(1)}, u32[]{:S(2)}, u32[]{:S(2)}) collective-permute-start(bf16[128,256]{1,0:T(8,128)(2,1)S(1)} %get-tuple-element.27), channel_id=1, source_target_pairs={{0,3},{1,0},{2,1},{3,2},{4,7},{5,4},{6,5},{7,6},{8,11},{9,8},{10,9... | collective-permute-start | bytes 196616 | tf_op jit(solution)/shard_map/ppermute | solution.py:613
  64.7 4.1 %collective-permute-done.10.refs_2_ = bf16[80,256]{1,0:T(8,128)(2,1)S(1)} collective-permute-done((bf16[80,256]{1,0:T(8,128)(2,1)S(1)}, bf16[80,256]{1,0:T(8,128)(2,1)S(1)}, u32[]{:S(2)}, u32[]{:S(2)}) %collective-permute-start.10) | collective-permute-done | bytes 40992 | tf_op jit(solution)/shard_map/ppermute | solution.py:613
  68.7 1.7 %modes.1 = (bf16[16,256]{1,0:T(8,128)(2,1)S(1)}, bf16[64,256]{1,0:T(8,128)(2,1)S(1)}, bf16[64,256]{1,0:T(8,128)(2,1)S(1)}, bf16[64,256]{1,0:T(8,128)(2,1)S(1)}, bf16[64,256]{1,0:T(8,128)(2,1)S(1)}) custom-call(s32[2]{0:T(128)S(1)} %pad_add_fusion.place_ref.place, bf16[64,160]{1,0:T(8,128)(2,1)S(1)} %dynamic-slice_bitcast_fusion.2.col_table, ...), custom_call_target="tpu_custom_call" | custom-call | tf_op jit(solution)/shard_map/modes/pallas_call | solution.py:714
  70.5 2.1 %collective-permute-start.11 = (bf16[64,256]{1,0:T(8,128)(2,1)S(1)}, bf16[64,256]{1,0:T(8,128)(2,1)S(1)}, u32[]{:S(2)}, u32[]{:S(2)}) collective-permute-start(bf16[64,256]{1,0:T(8,128)(2,1)S(1)} %get-tuple-element.33), channel_id=1, source_target_pairs={{0,3},{1,0},{2,1},{3,2},{4,7},{5,4},{6,5},{7,6},{8,11},{9,8},{10,9... | collective-permute-start | bytes 98312 | tf_op jit(solution)/shard_map/ppermute | solution.py:613
  73.3 1.6 %collective-permute-done.11 = bf16[64,256]{1,0:T(8,128)(2,1)S(1)} collective-permute-done((bf16[64,256]{1,0:T(8,128)(2,1)S(1)}, bf16[64,256]{1,0:T(8,128)(2,1)S(1)}, u32[]{:S(2)}, u32[]{:S(2)}) %collective-permute-start.11) | collective-permute-done | bytes 32800 | tf_op jit(solution)/shard_map/ppermute | solution.py:613
  74.9 2.5 %collective-permute-done.12 = bf16[64,256]{1,0:T(8,128)(2,1)S(1)} collective-permute-done((bf16[64,256]{1,0:T(8,128)(2,1)S(1)}, bf16[64,256]{1,0:T(8,128)(2,1)S(1)}, u32[]{:S(2)}, u32[]{:S(2)}) %collective-permute-start.12) | collective-permute-done | bytes 32800 | tf_op jit(solution)/shard_map/ppermute | solution.py:613
  77.4 0.9 %collective-permute-done.13 = bf16[64,256]{1,0:T(8,128)(2,1)S(1)} collective-permute-done((bf16[64,256]{1,0:T(8,128)(2,1)S(1)}, bf16[64,256]{1,0:T(8,128)(2,1)S(1)}, u32[]{:S(2)}, u32[]{:S(2)}) %collective-permute-start.13) | collective-permute-done | bytes 32800 | tf_op jit(solution)/shard_map/ppermute | solution.py:613
  78.3 1.0 %collective-permute-start.15 = (bf16[272,256]{1,0:T(8,128)(2,1)S(1)}, bf16[272,256]{1,0:T(8,128)(2,1)S(1)}, u32[]{:S(2)}, u32[]{:S(2)}) collective-permute-start(bf16[272,256]{1,0:T(8,128)(2,1)S(1)} %constant_dynamic-update-slice_fusion.refs_0_), channel_id=1, source_target_pairs={{0,16},{4,20},{8,24},{12,28},{16,0},{20,4},{24,8},{28,12},{1,17},{... | collective-permute-start | bytes 417800 | tf_op jit(solution)/shard_map/ppermute | solution.py:613
  79.3 2.5 %collective-permute-start.16 = (bf16[272,256]{1,0:T(8,128)(2,1)S(1)}, bf16[272,256]{1,0:T(8,128)(2,1)S(1)}, u32[]{:S(2)}, u32[]{:S(2)}) collective-permute-start(bf16[272,256]{1,0:T(8,128)(2,1)S(1)} %constant_dynamic-update-slice_fusion.refs_0_), channel_id=1, source_target_pairs={{0,24},{4,28},{8,0},{12,4},{16,8},{20,12},{24,16},{28,20},{1,25},{... | collective-permute-start | bytes 417800 | tf_op jit(solution)/shard_map/ppermute | solution.py:613
  81.7 2.6 %collective-permute-done.14.refs_1_ = bf16[272,256]{1,0:T(8,128)(2,1)S(1)} collective-permute-done((bf16[272,256]{1,0:T(8,128)(2,1)S(1)}, bf16[272,256]{1,0:T(8,128)(2,1)S(1)}, u32[]{:S(2)}, u32[]{:S(2)}) %collective-permute-start.14) | collective-permute-done | bytes 139296 | tf_op jit(solution)/shard_map/ppermute | solution.py:613
  86.5 2.7 %final.1 = bf16[48,32,256]{2,1,0:T(8,128)(2,1)} custom-call(s32[2]{0:T(128)S(1)} %pad_add_fusion.place_ref.place, bf16[176,128]{1,0:T(8,128)(2,1)S(1)} %dynamic-slice_bitcast_fusion.tables, f32[48,32,256]{2,1,0:T(8,128)S(1)} %copy-done.1, bf16[128,256]{1,0:T(8,128)(2,1)S(1)} %collective-permute-done.8.refs_1_.left, ...), custom_call_target="tpu_custom_call" | custom-call | tf_op jit(solution)/shard_map/final/pallas_call | solution.py:737
  (52 shorter events, 7.9 us)
Async XLA Ops:
  1.1 6.9 %collective-permute-start = (bf16[48,256]{1,0:T(8,128)(2,1)S(1)}, bf16[48,256]{1,0:T(8,128)(2,1)S(1)}, u32[]{:S(2)}, u32[]{:S(2)}) collective-permute-start(bf16[48,256]{1,0:T(8,128)(2,1)S(1)} %bitcast.40), channel_id=1, source_target_pairs={{0,1},{1,2},{2,3},{3,0},{4,5},{5,6},{6,7},{7,4},{8,9},{9,10},{10,1... | collective-permute-start | bytes 73736 | tf_op jit(solution)/shard_map/ppermute | solution.py:613
  4.2 4.1 %collective-permute-start.1 = (bf16[48,256]{1,0:T(8,128)(2,1)S(1)}, bf16[48,256]{1,0:T(8,128)(2,1)S(1)}, u32[]{:S(2)}, u32[]{:S(2)}) collective-permute-start(bf16[48,256]{1,0:T(8,128)(2,1)S(1)} %bitcast.41), channel_id=1, source_target_pairs={{0,3},{1,0},{2,1},{3,2},{4,7},{5,4},{6,5},{7,6},{8,11},{9,8},{10,9... | collective-permute-start | bytes 73736 | tf_op jit(solution)/shard_map/ppermute | solution.py:613
  8.3 2.9 %collective-permute-start.3 = (bf16[34,256]{1,0:T(8,128)(2,1)S(1)}, bf16[34,256]{1,0:T(8,128)(2,1)S(1)}, u32[]{:S(2)}, u32[]{:S(2)}) collective-permute-start(bf16[34,256]{1,0:T(8,128)(2,1)S(1)} %pad_maximum_fusion.3), channel_id=1, source_target_pairs={{0,28},{4,0},{8,4},{12,8},{16,12},{20,16},{24,20},{28,24},{1,29},{... | collective-permute-start | bytes 52232 | tf_op jit(solution)/shard_map/ppermute | solution.py:613
  9.6 4.2 %collective-permute-start.2 = (bf16[34,256]{1,0:T(8,128)(2,1)S(1)}, bf16[34,256]{1,0:T(8,128)(2,1)S(1)}, u32[]{:S(2)}, u32[]{:S(2)}) collective-permute-start(bf16[34,256]{1,0:T(8,128)(2,1)S(1)} %pad_maximum_fusion.2), channel_id=1, source_target_pairs={{0,4},{4,8},{8,12},{12,16},{16,20},{20,24},{24,28},{28,0},{1,5},{5... | collective-permute-start | bytes 52232 | tf_op jit(solution)/shard_map/ppermute | solution.py:613
  44.8 2.3 %collective-permute-start.4 = (bf16[4,16,5632]{2,1,0:T(8,128)(2,1)S(1)}, bf16[4,16,5632]{2,1,0:T(8,128)(2,1)S(1)}, u32[]{:S(2)}, u32[]{:S(2)}) collective-permute-start(bf16[4,16,5632]{2,1,0:T(8,128)(2,1)S(1)} %get-tuple-element.22), channel_id=1, source_target_pairs={{0,4},{4,0},{8,12},{12,8},{16,20},{20,16},{24,28},{28,24},{1,5},{5... | collective-permute-start | bytes 2162696 | tf_op jit(solution)/shard_map/ppermute | solution.py:686
  47.3 17.3 %copy-start.2 = (s32[64,32]{0,1:T(8,128)S(1)}, s32[64,32]{0,1:T(8,128)}, u32[]{:S(2)}) copy-start(s32[64,32]{0,1:T(8,128)} %param.16) | copy-start | bytes 24580
  47.3 21.5 %copy-start = (bf16[16,256,256]{2,1,0:T(8,128)(2,1)S(1)}, bf16[16,256,256]{2,1,0:T(8,128)(2,1)}, u32[]{:S(2)}) copy-start(bf16[16,256,256]{2,1,0:T(8,128)(2,1)} %bands.1) | copy-start | bytes 6291460
  47.3 11.9 %collective-permute-start.7 = (bf16[16,5888]{1,0:T(8,128)(2,1)S(1)}, bf16[16,5888]{1,0:T(8,128)(2,1)S(1)}, u32[]{:S(2)}, u32[]{:S(2)}) collective-permute-start(bf16[16,5888]{1,0:T(8,128)(2,1)S(1)} %pad_maximum_fusion.1), channel_id=1, source_target_pairs={{0,24},{4,28},{8,0},{12,4},{16,8},{20,12},{24,16},{28,20},{1,25},{... | collective-permute-start | bytes 565256 | tf_op jit(solution)/shard_map/ppermute | solution.py:613
  47.8 11.4 %collective-permute-start.5 = (bf16[16,5888]{1,0:T(8,128)(2,1)S(1)}, bf16[16,5888]{1,0:T(8,128)(2,1)S(1)}, u32[]{:S(2)}, u32[]{:S(2)}) collective-permute-start(bf16[16,5888]{1,0:T(8,128)(2,1)S(1)} %pad_maximum_fusion), channel_id=1, source_target_pairs={{0,8},{4,12},{8,16},{12,20},{16,24},{20,28},{24,0},{28,4},{1,9},{5... | collective-permute-start | bytes 565256 | tf_op jit(solution)/shard_map/ppermute | solution.py:613
  49.5 9.7 %collective-permute-start.6 = (bf16[16,5120]{1,0:T(8,128)(2,1)S(1)}, bf16[16,5120]{1,0:T(8,128)(2,1)S(1)}, u32[]{:S(2)}, u32[]{:S(2)}) collective-permute-start(bf16[16,5120]{1,0:T(8,128)(2,1)S(1)} %get-tuple-element.38), channel_id=1, source_target_pairs={{0,16},{4,20},{8,24},{12,28},{16,0},{20,4},{24,8},{28,12},{1,17},{... | collective-permute-start | bytes 491528 | tf_op jit(solution)/shard_map/ppermute | solution.py:613
  60.0 8.8 %collective-permute-start.8 = (bf16[128,256]{1,0:T(8,128)(2,1)S(1)}, bf16[128,256]{1,0:T(8,128)(2,1)S(1)}, u32[]{:S(2)}, u32[]{:S(2)}) collective-permute-start(bf16[128,256]{1,0:T(8,128)(2,1)S(1)} %get-tuple-element.26), channel_id=1, source_target_pairs={{0,1},{1,2},{2,3},{3,0},{4,5},{5,6},{6,7},{7,4},{8,9},{9,10},{10,1... | collective-permute-start | bytes 196616 | tf_op jit(solution)/shard_map/ppermute | solution.py:613
  60.7 8.0 %collective-permute-start.9 = (bf16[128,256]{1,0:T(8,128)(2,1)S(1)}, bf16[128,256]{1,0:T(8,128)(2,1)S(1)}, u32[]{:S(2)}, u32[]{:S(2)}) collective-permute-start(bf16[128,256]{1,0:T(8,128)(2,1)S(1)} %get-tuple-element.27), channel_id=1, source_target_pairs={{0,3},{1,0},{2,1},{3,2},{4,7},{5,4},{6,5},{7,6},{8,11},{9,8},{10,9... | collective-permute-start | bytes 196616 | tf_op jit(solution)/shard_map/ppermute | solution.py:613
  63.8 4.9 %collective-permute-start.10 = (bf16[80,256]{1,0:T(8,128)(2,1)S(1)}, bf16[80,256]{1,0:T(8,128)(2,1)S(1)}, u32[]{:S(2)}, u32[]{:S(2)}) collective-permute-start(bf16[80,256]{1,0:T(8,128)(2,1)S(1)} %get-tuple-element.31), channel_id=1, source_target_pairs={{0,2},{1,3},{2,0},{3,1},{4,6},{5,7},{6,4},{7,5},{8,10},{9,11},{10,... | collective-permute-start | bytes 122888 | tf_op jit(solution)/shard_map/ppermute | solution.py:613
  64.7 21.8 %copy-start.1 = (f32[48,32,256]{2,1,0:T(8,128)S(1)}, f32[48,32,256]{2,1,0:T(8,128)}, u32[]{:S(2)}) copy-start(f32[48,32,256]{2,1,0:T(8,128)} %get-tuple-element.21.grad_far) | copy-start | bytes 4718596
  70.5 4.4 %collective-permute-start.11 = (bf16[64,256]{1,0:T(8,128)(2,1)S(1)}, bf16[64,256]{1,0:T(8,128)(2,1)S(1)}, u32[]{:S(2)}, u32[]{:S(2)}) collective-permute-start(bf16[64,256]{1,0:T(8,128)(2,1)S(1)} %get-tuple-element.33), channel_id=1, source_target_pairs={{0,3},{1,0},{2,1},{3,2},{4,7},{5,4},{6,5},{7,6},{8,11},{9,8},{10,9... | collective-permute-start | bytes 98312 | tf_op jit(solution)/shard_map/ppermute | solution.py:613
  72.6 4.8 %collective-permute-start.12 = (bf16[64,256]{1,0:T(8,128)(2,1)S(1)}, bf16[64,256]{1,0:T(8,128)(2,1)S(1)}, u32[]{:S(2)}, u32[]{:S(2)}) collective-permute-start(bf16[64,256]{1,0:T(8,128)(2,1)S(1)} %get-tuple-element.34), channel_id=1, source_target_pairs={{0,2},{1,3},{2,0},{3,1},{4,6},{5,7},{6,4},{7,5},{8,10},{9,11},{10,... | collective-permute-start | bytes 98312 | tf_op jit(solution)/shard_map/ppermute | solution.py:613
  72.6 5.7 %collective-permute-start.13 = (bf16[64,256]{1,0:T(8,128)(2,1)S(1)}, bf16[64,256]{1,0:T(8,128)(2,1)S(1)}, u32[]{:S(2)}, u32[]{:S(2)}) collective-permute-start(bf16[64,256]{1,0:T(8,128)(2,1)S(1)} %get-tuple-element.35), channel_id=1, source_target_pairs={{0,1},{1,2},{2,3},{3,0},{4,5},{5,6},{6,7},{7,4},{8,9},{9,10},{10,1... | collective-permute-start | bytes 98312 | tf_op jit(solution)/shard_map/ppermute | solution.py:613
  78.3 6.1 %collective-permute-start.14 = (bf16[272,256]{1,0:T(8,128)(2,1)S(1)}, bf16[272,256]{1,0:T(8,128)(2,1)S(1)}, u32[]{:S(2)}, u32[]{:S(2)}) collective-permute-start(bf16[272,256]{1,0:T(8,128)(2,1)S(1)} %constant_dynamic-update-slice_fusion.refs_0_), channel_id=1, source_target_pairs={{0,8},{4,12},{8,16},{12,20},{16,24},{20,28},{24,0},{28,4},{1,9},{5... | collective-permute-start | bytes 417800 | tf_op jit(solution)/shard_map/ppermute | solution.py:613
  78.3 6.6 %collective-permute-start.15 = (bf16[272,256]{1,0:T(8,128)(2,1)S(1)}, bf16[272,256]{1,0:T(8,128)(2,1)S(1)}, u32[]{:S(2)}, u32[]{:S(2)}) collective-permute-start(bf16[272,256]{1,0:T(8,128)(2,1)S(1)} %constant_dynamic-update-slice_fusion.refs_0_), channel_id=1, source_target_pairs={{0,16},{4,20},{8,24},{12,28},{16,0},{20,4},{24,8},{28,12},{1,17},{... | collective-permute-start | bytes 417800 | tf_op jit(solution)/shard_map/ppermute | solution.py:613
  79.3 5.7 %collective-permute-start.16 = (bf16[272,256]{1,0:T(8,128)(2,1)S(1)}, bf16[272,256]{1,0:T(8,128)(2,1)S(1)}, u32[]{:S(2)}, u32[]{:S(2)}) collective-permute-start(bf16[272,256]{1,0:T(8,128)(2,1)S(1)} %constant_dynamic-update-slice_fusion.refs_0_), channel_id=1, source_target_pairs={{0,24},{4,28},{8,0},{12,4},{16,8},{20,12},{24,16},{28,20},{1,25},{... | collective-permute-start | bytes 417800 | tf_op jit(solution)/shard_map/ppermute | solution.py:613
  81.7 3.7 %collective-permute-start.17 = (bf16[272,256]{1,0:T(8,128)(2,1)S(1)}, bf16[272,256]{1,0:T(8,128)(2,1)S(1)}, u32[]{:S(2)}, u32[]{:S(2)}) collective-permute-start(bf16[272,256]{1,0:T(8,128)(2,1)S(1)} %constant_dynamic-update-slice_fusion.refs_0_), channel_id=1, source_target_pairs={{0,4},{4,0},{8,12},{12,8},{16,20},{20,16},{24,28},{28,24},{1,5},{5... | collective-permute-start | bytes 417800 | tf_op jit(solution)/shard_map/ppermute | solution.py:736
  84.4 1.4 %collective-permute-start.18 = (bf16[272,256]{1,0:T(8,128)(2,1)S(1)}, bf16[272,256]{1,0:T(8,128)(2,1)S(1)}, u32[]{:S(2)}, u32[]{:S(2)}) collective-permute-start(bf16[272,256]{1,0:T(8,128)(2,1)S(1)} %collective-permute-done.14.refs_1_), channel_id=1, source_target_pairs={{0,4},{4,0},{8,12},{12,8},{16,20},{20,16},{24,28},{28,24},{1,5},{5... | collective-permute-start | bytes 417800 | tf_op jit(solution)/shard_map/ppermute | solution.py:736
  84.9 1.4 %collective-permute-start.19 = (bf16[272,256]{1,0:T(8,128)(2,1)S(1)}, bf16[272,256]{1,0:T(8,128)(2,1)S(1)}, u32[]{:S(2)}, u32[]{:S(2)}) collective-permute-start(bf16[272,256]{1,0:T(8,128)(2,1)S(1)} %collective-permute-done.15.refs_2_), channel_id=1, source_target_pairs={{0,4},{4,0},{8,12},{12,8},{16,20},{20,16},{24,28},{28,24},{1,5},{5... | collective-permute-start | bytes 417800 | tf_op jit(solution)/shard_map/ppermute | solution.py:736
  84.9 1.6 %collective-permute-start.20 = (bf16[272,256]{1,0:T(8,128)(2,1)S(1)}, bf16[272,256]{1,0:T(8,128)(2,1)S(1)}, u32[]{:S(2)}, u32[]{:S(2)}) collective-permute-start(bf16[272,256]{1,0:T(8,128)(2,1)S(1)} %collective-permute-done.16.refs_3_), channel_id=1, source_target_pairs={{0,4},{4,0},{8,12},{12,8},{16,20},{20,16},{24,28},{28,24},{1,5},{5... | collective-permute-start | bytes 417800 | tf_op jit(solution)/shard_map/ppermute | solution.py:736

commit v4 on v3

--- a/solution.py
+++ b/solution.py
@@ -37,7 +37,7 @@
 def gelu_slope(values):
     size = jnp.abs(values)
     t = 1.0 / (1.0 + 0.23164189 * size)
-    bell = jnp.exp(-0.5 * values * values)
+    bell = jnp.exp2(values * (values * -0.7213475204444817))
     poly = 0.5307027145 * t - 0.7265760135
     poly = poly * t + 0.7107068705
     poly = poly * t - 0.1422483680
@@ -184,9 +184,9 @@
         gather(tile + 1)
         for i, first in enumerate(firsts):
             preact = forward(tile + 1, first)
+            slopes(tile + 1, first, preact, target)
             for a in range(i, 3 if first == firsts[-1] else i + 1):
                 backward(tile, a, source)
-            slopes(tile + 1, first, preact, target)
 
     gather(0)
     for first in firsts:
@@ -407,12 +407,13 @@
             ],
             axis=0,
         ).astype(BF16)
+        wide = coefs.astype(F32)
         plus_line = bands_of(slot, KW, 0)
         minus_line = bands_of(jnp.where(slot == 0, KH // 2, KH - slot), KW, 0)
         band = jnp.concatenate([plus_line, minus_line, plus_line, minus_line] + [low_line] * 4, axis=0)
         mixed = None
         for b in range(bands.shape[0]):
-            chosen = jnp.where(band == float(b), coefs, jnp.zeros_like(coefs))
+            chosen = jnp.where(band == float(b), wide, 0.0).astype(BF16)
             part = lax.dot_general(chosen, bands[b], NT, preferred_element_type=F32)
             mixed = part if mixed is None else mixed + part
         mixed = (mixed * back_scale).astype(BF16)
@@ -436,7 +437,7 @@
 
 
 def final_kernel(count, main, edges, spans, place, tables, grad_far, left, right, above, below, *refs):
-    blocks, (out, grad, rows, cells, lcol, rcol, sem) = refs[:count], refs[count:]
+    blocks, (out_far, out, grad, rows, cells, lcol, rcol, sem, out_sems) = refs[:count], refs[count:]
     rows_dev, cols_dev, ch = out.shape
     apart = pitch(cols_dev)
     table, low_table = tables[spans[0]], tables[spans[1]]
@@ -476,10 +477,19 @@
             out[at] = total(at).astype(BF16)
         return carry
 
-    lax.fori_loop(0, rows_dev // 4, store, 0)
-    out[0] = (total(0) + above[...].astype(F32)).astype(BF16)
     last = rows_dev - 1
-    out[last] = (total(last) + below[...].astype(F32)).astype(BF16)
+    copies = []
+    for i in range(rows_dev // TILE):
+        lax.fori_loop(i * TILE // 4, (i + 1) * TILE // 4, store, 0)
+        if i == 0:
+            out[0] = (total(0) + above[...].astype(F32)).astype(BF16)
+        if (i + 1) * TILE == rows_dev:
+            out[last] = (total(last) + below[...].astype(F32)).astype(BF16)
+        span = pl.ds(i * TILE, TILE)
+        copies.append(pltpu.make_async_copy(out.at[span], out_far.at[span], out_sems.at[i]))
+        copies[-1].start()
+    for copy in copies:
+        copy.wait()
 
 
 def in_vmem():
@@ -739,15 +749,18 @@
         shape(rows_dev, cols_dev, ch),
         [in_smem(), in_vmem(), in_hbm()] + [in_vmem()] * (4 + n_gx),
         [
+            pltpu.VMEM((rows_dev, cols_dev, ch), BF16),
             pltpu.VMEM((rows_dev, cols_dev, ch), F32),
             planes(depth_out * pitch(cols_dev), ch),
             planes(rows_dev * pitch(cols_dev), ch),
             pltpu.VMEM((rows_dev, ch), F32),
             pltpu.VMEM((rows_dev, ch), F32),
             pltpu.SemaphoreType.DMA,
+            pltpu.SemaphoreType.DMA((rows_dev // TILE,)),
         ],
         "final",
         16,
+        in_hbm(),
     )(place, tables, grad, from_left, from_right, from_above, from_below, *blocks)
 
 

time: 89.8 us -> 89.4 us (level)
  no operation moved by 1% of the time
where the time goes in v4:
time: 89.4 us; the launch traced here: 89 us
  Pallas kernels  36 us (40%)
  waiting for transfers between devices  26.8 us (30%)
  starting transfers between devices  19.9 us (22%)
  local copies, waits for them, and re-layouts  5.82 us (7%)
    pallas_call x1, Pallas kernels, body(): call(functools.partial(conv_kernel, sizes, picked, edges, spans[0]), [sha...  30.9 us
    ppermute x16, waiting for transfers between devices, ring(): lax.ppermute(array, axis, [(i, (i + step) % count) for i in range(count)])  23.6 us
    ppermute x16, starting transfers between devices, ring(): lax.ppermute(array, axis, [(i, (i + step) % count) for i in range(count)])  19.3 us
    pallas_call x1, Pallas kernels, body(): call(functools.partial(final_kernel, n_gx, slots * 2 * cols_dev, edges, (...  2.56 us
    ppermute x1, waiting for transfers between devices, body(): gift = lax.ppermute(give, 'gx', swap)  2.18 us
  transfers between devices with their start and end apart: 21, of which 14 were waited for; matrix products, arithmetic and copies ran while one was open for 5% of the time, Pallas kernels for 0%

profile of v4, /device:TPU:0, one launch (start us, length us, event | category | flops | bytes accessed | tf_op | source)
XLA Modules:
  0.0 89.0 jit_solution(17138610546036814218)
XLA Ops:
  0.0 1.1 %fusion.4 = (bf16[48,1,256]{2,1,0:T(2,128)(2,1)S(1)}, bf16[48,1,256]{2,1,0:T(2,128)(2,1)S(1)}) fusion(bf16[48,32,256]{2,1,0:T(8,128)(2,1)} %x_far.1), kind=kLoop, calls=%fused_computation.31 | loop fusion | bytes 98304 | tf_op jit(solution)/shard_map/slice | solution.py:640
  1.1 3.1 %collective-permute-start = (bf16[48,256]{1,0:T(8,128)(2,1)S(1)}, bf16[48,256]{1,0:T(8,128)(2,1)S(1)}, u32[]{:S(2)}, u32[]{:S(2)}) collective-permute-start(bf16[48,256]{1,0:T(8,128)(2,1)S(1)} %bitcast.40), channel_id=1, source_target_pairs={{0,1},{1,2},{2,3},{3,0},{4,5},{5,6},{6,7},{7,4},{8,9},{9,10},{10,1... | collective-permute-start | bytes 73736 | tf_op jit(solution)/shard_map/ppermute | solution.py:623
  4.2 2.1 %collective-permute-start.1 = (bf16[48,256]{1,0:T(8,128)(2,1)S(1)}, bf16[48,256]{1,0:T(8,128)(2,1)S(1)}, u32[]{:S(2)}, u32[]{:S(2)}) collective-permute-start(bf16[48,256]{1,0:T(8,128)(2,1)S(1)} %bitcast.41), channel_id=1, source_target_pairs={{0,3},{1,0},{2,1},{3,2},{4,7},{5,4},{6,5},{7,6},{8,11},{9,8},{10,9... | collective-permute-start | bytes 73736 | tf_op jit(solution)/shard_map/ppermute | solution.py:623
  7.0 0.8 dynamic-slice_bitcast_fusion.tables
  8.3 1.2 %collective-permute-start.3 = (bf16[34,256]{1,0:T(8,128)(2,1)S(1)}, bf16[34,256]{1,0:T(8,128)(2,1)S(1)}, u32[]{:S(2)}, u32[]{:S(2)}) collective-permute-start(bf16[34,256]{1,0:T(8,128)(2,1)S(1)} %pad_maximum_fusion.3), channel_id=1, source_target_pairs={{0,28},{4,0},{8,4},{12,8},{16,12},{20,16},{24,20},{28,24},{1,29},{... | collective-permute-start | bytes 52232 | tf_op jit(solution)/shard_map/ppermute | solution.py:623
  9.7 0.8 reshape.25.routes
  10.5 0.8 reshape.26.gates
  11.2 2.5 %collective-permute-done.2.top = bf16[34,256]{1,0:T(8,128)(2,1)S(1)} collective-permute-done((bf16[34,256]{1,0:T(8,128)(2,1)S(1)}, bf16[34,256]{1,0:T(8,128)(2,1)S(1)}, u32[]{:S(2)}, u32[]{:S(2)}) %collective-permute-start.2) | collective-permute-done | bytes 17440 | tf_op jit(solution)/shard_map/ppermute | solution.py:623
  13.7 30.9 %conv.1 = (bf16[4,16,5120]{2,1,0:T(8,128)(2,1)S(1)}, bf16[4,16,5632]{2,1,0:T(8,128)(2,1)S(1)}, f32[48,32,256]{2,1,0:T(8,128)}, bf16[48,256]{1,0:T(8,128)(2,1)S(1)}, bf16[48,256]{1,0:T(8,128)(2,1)S(1)}) custom-call(s32[24]{0:T(128)S(1)} %reshape.25.routes, f32[36]{0:T(128)S(1)} %reshape.26.gates, s32[2]{0:T(128)S(1)} %pad_add_fusion.place_ref.place, ...), custom_call_target="tpu_custom_call" | custom-call | tf_op jit(solution)/shard_map/conv/pallas_call | solution.py:652
  44.7 2.2 %collective-permute-done.4.gift = bf16[4,16,5632]{2,1,0:T(8,128)(2,1)S(1)} collective-permute-done((bf16[4,16,5632]{2,1,0:T(8,128)(2,1)S(1)}, bf16[4,16,5632]{2,1,0:T(8,128)(2,1)S(1)}, u32[]{:S(2)}, u32[]{:S(2)}) %collective-permute-start.4) | collective-permute-done | bytes 720928 | tf_op jit(solution)/shard_map/ppermute | solution.py:696
  47.6 1.7 %collective-permute-start.5 = (bf16[16,5888]{1,0:T(8,128)(2,1)S(1)}, bf16[16,5888]{1,0:T(8,128)(2,1)S(1)}, u32[]{:S(2)}, u32[]{:S(2)}) collective-permute-start(bf16[16,5888]{1,0:T(8,128)(2,1)S(1)} %pad_maximum_fusion), channel_id=1, source_target_pairs={{0,8},{4,12},{8,16},{12,20},{16,24},{20,28},{24,0},{28,4},{1,9},{5... | collective-permute-start | bytes 565256 | tf_op jit(solution)/shard_map/ppermute | solution.py:623
  50.5 8.4 %collective-permute-done.6.refs_2_ = bf16[16,5120]{1,0:T(8,128)(2,1)S(1)} collective-permute-done((bf16[16,5120]{1,0:T(8,128)(2,1)S(1)}, bf16[16,5120]{1,0:T(8,128)(2,1)S(1)}, u32[]{:S(2)}, u32[]{:S(2)}) %collective-permute-start.6) | collective-permute-done | bytes 163872 | tf_op jit(solution)/shard_map/ppermute | solution.py:623
  59.0 0.8 regroup.1
  60.5 3.1 %collective-permute-start.9 = (bf16[128,256]{1,0:T(8,128)(2,1)S(1)}, bf16[128,256]{1,0:T(8,128)(2,1)S(1)}, u32[]{:S(2)}, u32[]{:S(2)}) collective-permute-start(bf16[128,256]{1,0:T(8,128)(2,1)S(1)} %get-tuple-element.27), channel_id=1, source_target_pairs={{0,3},{1,0},{2,1},{3,2},{4,7},{5,4},{6,5},{7,6},{8,11},{9,8},{10,9... | collective-permute-start | bytes 196616 | tf_op jit(solution)/shard_map/ppermute | solution.py:623
  64.5 4.1 %collective-permute-done.10.refs_2_ = bf16[80,256]{1,0:T(8,128)(2,1)S(1)} collective-permute-done((bf16[80,256]{1,0:T(8,128)(2,1)S(1)}, bf16[80,256]{1,0:T(8,128)(2,1)S(1)}, u32[]{:S(2)}, u32[]{:S(2)}) %collective-permute-start.10) | collective-permute-done | bytes 40992 | tf_op jit(solution)/shard_map/ppermute | solution.py:623
  68.5 1.7 %modes.1 = (bf16[16,256]{1,0:T(8,128)(2,1)S(1)}, bf16[64,256]{1,0:T(8,128)(2,1)S(1)}, bf16[64,256]{1,0:T(8,128)(2,1)S(1)}, bf16[64,256]{1,0:T(8,128)(2,1)S(1)}, bf16[64,256]{1,0:T(8,128)(2,1)S(1)}) custom-call(s32[2]{0:T(128)S(1)} %pad_add_fusion.place_ref.place, bf16[64,160]{1,0:T(8,128)(2,1)S(1)} %dynamic-slice_bitcast_fusion.2.col_table, ...), custom_call_target="tpu_custom_call" | custom-call | tf_op jit(solution)/shard_map/modes/pallas_call | solution.py:724
  70.3 2.1 %collective-permute-start.11 = (bf16[64,256]{1,0:T(8,128)(2,1)S(1)}, bf16[64,256]{1,0:T(8,128)(2,1)S(1)}, u32[]{:S(2)}, u32[]{:S(2)}) collective-permute-start(bf16[64,256]{1,0:T(8,128)(2,1)S(1)} %get-tuple-element.33), channel_id=1, source_target_pairs={{0,3},{1,0},{2,1},{3,2},{4,7},{5,4},{6,5},{7,6},{8,11},{9,8},{10,9... | collective-permute-start | bytes 98312 | tf_op jit(solution)/shard_map/ppermute | solution.py:623
  73.1 1.6 %collective-permute-done.11 = bf16[64,256]{1,0:T(8,128)(2,1)S(1)} collective-permute-done((bf16[64,256]{1,0:T(8,128)(2,1)S(1)}, bf16[64,256]{1,0:T(8,128)(2,1)S(1)}, u32[]{:S(2)}, u32[]{:S(2)}) %collective-permute-start.11) | collective-permute-done | bytes 32800 | tf_op jit(solution)/shard_map/ppermute | solution.py:623
  74.7 2.5 %collective-permute-done.12 = bf16[64,256]{1,0:T(8,128)(2,1)S(1)} collective-permute-done((bf16[64,256]{1,0:T(8,128)(2,1)S(1)}, bf16[64,256]{1,0:T(8,128)(2,1)S(1)}, u32[]{:S(2)}, u32[]{:S(2)}) %collective-permute-start.12) | collective-permute-done | bytes 32800 | tf_op jit(solution)/shard_map/ppermute | solution.py:623
  77.2 0.9 %collective-permute-done.13 = bf16[64,256]{1,0:T(8,128)(2,1)S(1)} collective-permute-done((bf16[64,256]{1,0:T(8,128)(2,1)S(1)}, bf16[64,256]{1,0:T(8,128)(2,1)S(1)}, u32[]{:S(2)}, u32[]{:S(2)}) %collective-permute-start.13) | collective-permute-done | bytes 32800 | tf_op jit(solution)/shard_map/ppermute | solution.py:623
  78.1 1.0 %collective-permute-start.15 = (bf16[272,256]{1,0:T(8,128)(2,1)S(1)}, bf16[272,256]{1,0:T(8,128)(2,1)S(1)}, u32[]{:S(2)}, u32[]{:S(2)}) collective-permute-start(bf16[272,256]{1,0:T(8,128)(2,1)S(1)} %constant_dynamic-update-slice_fusion.refs_0_), channel_id=1, source_target_pairs={{0,16},{4,20},{8,24},{12,28},{16,0},{20,4},{24,8},{28,12},{1,17},{... | collective-permute-start | bytes 417800 | tf_op jit(solution)/shard_map/ppermute | solution.py:623
  79.1 2.4 %collective-permute-start.16 = (bf16[272,256]{1,0:T(8,128)(2,1)S(1)}, bf16[272,256]{1,0:T(8,128)(2,1)S(1)}, u32[]{:S(2)}, u32[]{:S(2)}) collective-permute-start(bf16[272,256]{1,0:T(8,128)(2,1)S(1)} %constant_dynamic-update-slice_fusion.refs_0_), channel_id=1, source_target_pairs={{0,24},{4,28},{8,0},{12,4},{16,8},{20,12},{24,16},{28,20},{1,25},{... | collective-permute-start | bytes 417800 | tf_op jit(solution)/shard_map/ppermute | solution.py:623
  81.5 2.6 %collective-permute-done.14.refs_1_ = bf16[272,256]{1,0:T(8,128)(2,1)S(1)} collective-permute-done((bf16[272,256]{1,0:T(8,128)(2,1)S(1)}, bf16[272,256]{1,0:T(8,128)(2,1)S(1)}, u32[]{:S(2)}, u32[]{:S(2)}) %collective-permute-start.14) | collective-permute-done | bytes 139296 | tf_op jit(solution)/shard_map/ppermute | solution.py:623
  86.3 2.6 %final.1 = bf16[48,32,256]{2,1,0:T(8,128)(2,1)} custom-call(s32[2]{0:T(128)S(1)} %pad_add_fusion.place_ref.place, bf16[176,128]{1,0:T(8,128)(2,1)S(1)} %dynamic-slice_bitcast_fusion.tables, f32[48,32,256]{2,1,0:T(8,128)S(1)} %copy-done.1, bf16[128,256]{1,0:T(8,128)(2,1)S(1)} %collective-permute-done.8.refs_1_.left, ...), custom_call_target="tpu_custom_call" | custom-call | tf_op jit(solution)/shard_map/final/pallas_call | solution.py:747
  (52 shorter events, 7.9 us)
Async XLA Ops:
  1.1 6.9 %collective-permute-start = (bf16[48,256]{1,0:T(8,128)(2,1)S(1)}, bf16[48,256]{1,0:T(8,128)(2,1)S(1)}, u32[]{:S(2)}, u32[]{:S(2)}) collective-permute-start(bf16[48,256]{1,0:T(8,128)(2,1)S(1)} %bitcast.40), channel_id=1, source_target_pairs={{0,1},{1,2},{2,3},{3,0},{4,5},{5,6},{6,7},{7,4},{8,9},{9,10},{10,1... | collective-permute-start | bytes 73736 | tf_op jit(solution)/shard_map/ppermute | solution.py:623
  4.2 4.1 %collective-permute-start.1 = (bf16[48,256]{1,0:T(8,128)(2,1)S(1)}, bf16[48,256]{1,0:T(8,128)(2,1)S(1)}, u32[]{:S(2)}, u32[]{:S(2)}) collective-permute-start(bf16[48,256]{1,0:T(8,128)(2,1)S(1)} %bitcast.41), channel_id=1, source_target_pairs={{0,3},{1,0},{2,1},{3,2},{4,7},{5,4},{6,5},{7,6},{8,11},{9,8},{10,9... | collective-permute-start | bytes 73736 | tf_op jit(solution)/shard_map/ppermute | solution.py:623
  8.3 2.9 %collective-permute-start.3 = (bf16[34,256]{1,0:T(8,128)(2,1)S(1)}, bf16[34,256]{1,0:T(8,128)(2,1)S(1)}, u32[]{:S(2)}, u32[]{:S(2)}) collective-permute-start(bf16[34,256]{1,0:T(8,128)(2,1)S(1)} %pad_maximum_fusion.3), channel_id=1, source_target_pairs={{0,28},{4,0},{8,4},{12,8},{16,12},{20,16},{24,20},{28,24},{1,29},{... | collective-permute-start | bytes 52232 | tf_op jit(solution)/shard_map/ppermute | solution.py:623
  9.6 4.2 %collective-permute-start.2 = (bf16[34,256]{1,0:T(8,128)(2,1)S(1)}, bf16[34,256]{1,0:T(8,128)(2,1)S(1)}, u32[]{:S(2)}, u32[]{:S(2)}) collective-permute-start(bf16[34,256]{1,0:T(8,128)(2,1)S(1)} %pad_maximum_fusion.2), channel_id=1, source_target_pairs={{0,4},{4,8},{8,12},{12,16},{16,20},{20,24},{24,28},{28,0},{1,5},{5... | collective-permute-start | bytes 52232 | tf_op jit(solution)/shard_map/ppermute | solution.py:623
  44.6 2.3 %collective-permute-start.4 = (bf16[4,16,5632]{2,1,0:T(8,128)(2,1)S(1)}, bf16[4,16,5632]{2,1,0:T(8,128)(2,1)S(1)}, u32[]{:S(2)}, u32[]{:S(2)}) collective-permute-start(bf16[4,16,5632]{2,1,0:T(8,128)(2,1)S(1)} %get-tuple-element.22), channel_id=1, source_target_pairs={{0,4},{4,0},{8,12},{12,8},{16,20},{20,16},{24,28},{28,24},{1,5},{5... | collective-permute-start | bytes 2162696 | tf_op jit(solution)/shard_map/ppermute | solution.py:696
  47.1 17.3 %copy-start.2 = (s32[64,32]{0,1:T(8,128)S(1)}, s32[64,32]{0,1:T(8,128)}, u32[]{:S(2)}) copy-start(s32[64,32]{0,1:T(8,128)} %param.16) | copy-start | bytes 24580
  47.1 21.5 %copy-start = (bf16[16,256,256]{2,1,0:T(8,128)(2,1)S(1)}, bf16[16,256,256]{2,1,0:T(8,128)(2,1)}, u32[]{:S(2)}) copy-start(bf16[16,256,256]{2,1,0:T(8,128)(2,1)} %bands.1) | copy-start | bytes 6291460
  47.1 11.9 %collective-permute-start.7 = (bf16[16,5888]{1,0:T(8,128)(2,1)S(1)}, bf16[16,5888]{1,0:T(8,128)(2,1)S(1)}, u32[]{:S(2)}, u32[]{:S(2)}) collective-permute-start(bf16[16,5888]{1,0:T(8,128)(2,1)S(1)} %pad_maximum_fusion.1), channel_id=1, source_target_pairs={{0,24},{4,28},{8,0},{12,4},{16,8},{20,12},{24,16},{28,20},{1,25},{... | collective-permute-start | bytes 565256 | tf_op jit(solution)/shard_map/ppermute | solution.py:623
  47.6 11.4 %collective-permute-start.5 = (bf16[16,5888]{1,0:T(8,128)(2,1)S(1)}, bf16[16,5888]{1,0:T(8,128)(2,1)S(1)}, u32[]{:S(2)}, u32[]{:S(2)}) collective-permute-start(bf16[16,5888]{1,0:T(8,128)(2,1)S(1)} %pad_maximum_fusion), channel_id=1, source_target_pairs={{0,8},{4,12},{8,16},{12,20},{16,24},{20,28},{24,0},{28,4},{1,9},{5... | collective-permute-start | bytes 565256 | tf_op jit(solution)/shard_map/ppermute | solution.py:623
  49.3 9.7 %collective-permute-start.6 = (bf16[16,5120]{1,0:T(8,128)(2,1)S(1)}, bf16[16,5120]{1,0:T(8,128)(2,1)S(1)}, u32[]{:S(2)}, u32[]{:S(2)}) collective-permute-start(bf16[16,5120]{1,0:T(8,128)(2,1)S(1)} %get-tuple-element.38), channel_id=1, source_target_pairs={{0,16},{4,20},{8,24},{12,28},{16,0},{20,4},{24,8},{28,12},{1,17},{... | collective-permute-start | bytes 491528 | tf_op jit(solution)/shard_map/ppermute | solution.py:623
  59.8 8.8 %collective-permute-start.8 = (bf16[128,256]{1,0:T(8,128)(2,1)S(1)}, bf16[128,256]{1,0:T(8,128)(2,1)S(1)}, u32[]{:S(2)}, u32[]{:S(2)}) collective-permute-start(bf16[128,256]{1,0:T(8,128)(2,1)S(1)} %get-tuple-element.26), channel_id=1, source_target_pairs={{0,1},{1,2},{2,3},{3,0},{4,5},{5,6},{6,7},{7,4},{8,9},{9,10},{10,1... | collective-permute-start | bytes 196616 | tf_op jit(solution)/shard_map/ppermute | solution.py:623
  60.5 8.0 %collective-permute-start.9 = (bf16[128,256]{1,0:T(8,128)(2,1)S(1)}, bf16[128,256]{1,0:T(8,128)(2,1)S(1)}, u32[]{:S(2)}, u32[]{:S(2)}) collective-permute-start(bf16[128,256]{1,0:T(8,128)(2,1)S(1)} %get-tuple-element.27), channel_id=1, source_target_pairs={{0,3},{1,0},{2,1},{3,2},{4,7},{5,4},{6,5},{7,6},{8,11},{9,8},{10,9... | collective-permute-start | bytes 196616 | tf_op jit(solution)/shard_map/ppermute | solution.py:623
  63.6 4.9 %collective-permute-start.10 = (bf16[80,256]{1,0:T(8,128)(2,1)S(1)}, bf16[80,256]{1,0:T(8,128)(2,1)S(1)}, u32[]{:S(2)}, u32[]{:S(2)}) collective-permute-start(bf16[80,256]{1,0:T(8,128)(2,1)S(1)} %get-tuple-element.31), channel_id=1, source_target_pairs={{0,2},{1,3},{2,0},{3,1},{4,6},{5,7},{6,4},{7,5},{8,10},{9,11},{10,... | collective-permute-start | bytes 122888 | tf_op jit(solution)/shard_map/ppermute | solution.py:623
  64.5 21.8 %copy-start.1 = (f32[48,32,256]{2,1,0:T(8,128)S(1)}, f32[48,32,256]{2,1,0:T(8,128)}, u32[]{:S(2)}) copy-start(f32[48,32,256]{2,1,0:T(8,128)} %get-tuple-element.21.grad_far) | copy-start | bytes 4718596
  70.3 4.4 %collective-permute-start.11 = (bf16[64,256]{1,0:T(8,128)(2,1)S(1)}, bf16[64,256]{1,0:T(8,128)(2,1)S(1)}, u32[]{:S(2)}, u32[]{:S(2)}) collective-permute-start(bf16[64,256]{1,0:T(8,128)(2,1)S(1)} %get-tuple-element.33), channel_id=1, source_target_pairs={{0,3},{1,0},{2,1},{3,2},{4,7},{5,4},{6,5},{7,6},{8,11},{9,8},{10,9... | collective-permute-start | bytes 98312 | tf_op jit(solution)/shard_map/ppermute | solution.py:623
  72.4 4.8 %collective-permute-start.12 = (bf16[64,256]{1,0:T(8,128)(2,1)S(1)}, bf16[64,256]{1,0:T(8,128)(2,1)S(1)}, u32[]{:S(2)}, u32[]{:S(2)}) collective-permute-start(bf16[64,256]{1,0:T(8,128)(2,1)S(1)} %get-tuple-element.34), channel_id=1, source_target_pairs={{0,2},{1,3},{2,0},{3,1},{4,6},{5,7},{6,4},{7,5},{8,10},{9,11},{10,... | collective-permute-start | bytes 98312 | tf_op jit(solution)/shard_map/ppermute | solution.py:623
  72.4 5.7 %collective-permute-start.13 = (bf16[64,256]{1,0:T(8,128)(2,1)S(1)}, bf16[64,256]{1,0:T(8,128)(2,1)S(1)}, u32[]{:S(2)}, u32[]{:S(2)}) collective-permute-start(bf16[64,256]{1,0:T(8,128)(2,1)S(1)} %get-tuple-element.35), channel_id=1, source_target_pairs={{0,1},{1,2},{2,3},{3,0},{4,5},{5,6},{6,7},{7,4},{8,9},{9,10},{10,1... | collective-permute-start | bytes 98312 | tf_op jit(solution)/shard_map/ppermute | solution.py:623
  78.1 6.1 %collective-permute-start.14 = (bf16[272,256]{1,0:T(8,128)(2,1)S(1)}, bf16[272,256]{1,0:T(8,128)(2,1)S(1)}, u32[]{:S(2)}, u32[]{:S(2)}) collective-permute-start(bf16[272,256]{1,0:T(8,128)(2,1)S(1)} %constant_dynamic-update-slice_fusion.refs_0_), channel_id=1, source_target_pairs={{0,8},{4,12},{8,16},{12,20},{16,24},{20,28},{24,0},{28,4},{1,9},{5... | collective-permute-start | bytes 417800 | tf_op jit(solution)/shard_map/ppermute | solution.py:623
  78.1 6.6 %collective-permute-start.15 = (bf16[272,256]{1,0:T(8,128)(2,1)S(1)}, bf16[272,256]{1,0:T(8,128)(2,1)S(1)}, u32[]{:S(2)}, u32[]{:S(2)}) collective-permute-start(bf16[272,256]{1,0:T(8,128)(2,1)S(1)} %constant_dynamic-update-slice_fusion.refs_0_), channel_id=1, source_target_pairs={{0,16},{4,20},{8,24},{12,28},{16,0},{20,4},{24,8},{28,12},{1,17},{... | collective-permute-start | bytes 417800 | tf_op jit(solution)/shard_map/ppermute | solution.py:623
  79.1 5.6 %collective-permute-start.16 = (bf16[272,256]{1,0:T(8,128)(2,1)S(1)}, bf16[272,256]{1,0:T(8,128)(2,1)S(1)}, u32[]{:S(2)}, u32[]{:S(2)}) collective-permute-start(bf16[272,256]{1,0:T(8,128)(2,1)S(1)} %constant_dynamic-update-slice_fusion.refs_0_), channel_id=1, source_target_pairs={{0,24},{4,28},{8,0},{12,4},{16,8},{20,12},{24,16},{28,20},{1,25},{... | collective-permute-start | bytes 417800 | tf_op jit(solution)/shard_map/ppermute | solution.py:623
  81.5 3.7 %collective-permute-start.17 = (bf16[272,256]{1,0:T(8,128)(2,1)S(1)}, bf16[272,256]{1,0:T(8,128)(2,1)S(1)}, u32[]{:S(2)}, u32[]{:S(2)}) collective-permute-start(bf16[272,256]{1,0:T(8,128)(2,1)S(1)} %constant_dynamic-update-slice_fusion.refs_0_), channel_id=1, source_target_pairs={{0,4},{4,0},{8,12},{12,8},{16,20},{20,16},{24,28},{28,24},{1,5},{5... | collective-permute-start | bytes 417800 | tf_op jit(solution)/shard_map/ppermute | solution.py:746
  84.2 1.4 %collective-permute-start.18 = (bf16[272,256]{1,0:T(8,128)(2,1)S(1)}, bf16[272,256]{1,0:T(8,128)(2,1)S(1)}, u32[]{:S(2)}, u32[]{:S(2)}) collective-permute-start(bf16[272,256]{1,0:T(8,128)(2,1)S(1)} %collective-permute-done.14.refs_1_), channel_id=1, source_target_pairs={{0,4},{4,0},{8,12},{12,8},{16,20},{20,16},{24,28},{28,24},{1,5},{5... | collective-permute-start | bytes 417800 | tf_op jit(solution)/shard_map/ppermute | solution.py:746
  84.7 1.4 %collective-permute-start.19 = (bf16[272,256]{1,0:T(8,128)(2,1)S(1)}, bf16[272,256]{1,0:T(8,128)(2,1)S(1)}, u32[]{:S(2)}, u32[]{:S(2)}) collective-permute-start(bf16[272,256]{1,0:T(8,128)(2,1)S(1)} %collective-permute-done.15.refs_2_), channel_id=1, source_target_pairs={{0,4},{4,0},{8,12},{12,8},{16,20},{20,16},{24,28},{28,24},{1,5},{5... | collective-permute-start | bytes 417800 | tf_op jit(solution)/shard_map/ppermute | solution.py:746
  84.7 1.6 %collective-permute-start.20 = (bf16[272,256]{1,0:T(8,128)(2,1)S(1)}, bf16[272,256]{1,0:T(8,128)(2,1)S(1)}, u32[]{:S(2)}, u32[]{:S(2)}) collective-permute-start(bf16[272,256]{1,0:T(8,128)(2,1)S(1)} %collective-permute-done.16.refs_3_), channel_id=1, source_target_pairs={{0,4},{4,0},{8,12},{12,8},{16,20},{20,16},{24,28},{28,24},{1,5},{5... | collective-permute-start | bytes 417800 | tf_op jit(solution)/shard_map/ppermute | solution.py:746
